TPU v7x, 32 devices: a whole 2x2x4 slice. The times are simulated.
32 devices in a mesh: group: 4 (over x, core), expert: 8 (over z, y).
Axes of the slice: x: 2, y: 2, z: 4, core: 2. Of those that a mesh axis runs over, the one named last changes fastest.
Arguments:
- tokens: bfloat16 [128, 197, 768], P(('group', 'expert')), may hold values from -6 to 6
- cotangent: bfloat16 [128, 197, 768], P(('group', 'expert')), may hold values from -6 to 6
- routes: int32 [128, 197, 2], P(('group', 'expert')), may hold values from 0 to 15, all different within a row
- order: int32 [32, 788], P(('group', 'expert')), may hold values from 0 to 787, each once within a row
- ln1_gain: float32 [768], P(('group', 'expert')), may hold values from 0.5 to 1.5
- ln1_bias: float32 [768], P(('group', 'expert')), may hold values from -0.625 to 0.625
- w_qkv: float32 [768, 2304], P(('group', 'expert')), may hold values from -0.21875 to 0.21875
- w_out: float32 [768, 768], P(('group', 'expert')), may hold values from -0.875 to 0.875
- b_out: float32 [768], P(('group', 'expert')), may hold values from -1.25 to 1.25
- ln2_gain: float32 [768], P(('group', 'expert')), may hold values from 0.5 to 1.5
- ln2_bias: float32 [768], P(('group', 'expert')), may hold values from -0.625 to 0.625
- w_router: float32 [768, 16], P(('group', 'expert')), may hold values from -0.15625 to 0.15625
- w_in: float32 [16, 768, 3072], P('expert', 'group'), may hold values from -0.21875 to 0.21875
- b_in: float32 [16, 3072], P('expert', 'group'), may hold values from -1.25 to 1.25
- w_back: float32 [16, 3072, 768], P('expert', 'group'), may hold values from -1.75 to 1.75
- b_back: float32 [16, 768], P('expert', 'group'), may hold values from -1.25 to 1.25
Outputs:
- output: bfloat16 [128, 197, 768], P(('group', 'expert'))
- grad_tokens: float32 [128, 197, 768], P(('group', 'expert'))
- grad_ln1_gain: float32 [768], P(('group', 'expert'))
- grad_ln1_bias: float32 [768], P(('group', 'expert'))
- grad_w_qkv: float32 [768, 2304], P(('group', 'expert'))
- grad_w_out: float32 [768, 768], P(('group', 'expert'))
- grad_b_out: float32 [768], P(('group', 'expert'))
- grad_ln2_gain: float32 [768], P(('group', 'expert'))
- grad_ln2_bias: float32 [768], P(('group', 'expert'))
- grad_w_router: float32 [768, 16], P(('group', 'expert'))
- grad_w_in: float32 [16, 768, 3072], P('expert', 'group')
- grad_b_in: float32 [16, 3072], P('expert', 'group')
- grad_w_back: float32 [16, 3072, 768], P('expert', 'group')
- grad_b_back: float32 [16, 768], P('expert', 'group')
Inputs may be any that keep to these rules, and one draw needn't show every extreme that they name: `routes`: each row names two different experts. Each row of order holds every token number of its block once.
All inputs are finite; a program needn't handle non-finite values.
Results may differ from a plain program's by a relative error of at most 0.015.
The roundings to bfloat16 on the way count: a program that leaves them out, or rounds other values in their place, can miss the bound.
Values may be sent and summed in bfloat16 or wider, within the bound.
No kernel may reach another device: no remote copies, remote signals or barrier semaphores. Data moves between devices by JAX's collectives and lax.ppermute only.
A program may use at most 256 MiB of HBM per device.

v0:
```python
import jax
import jax.numpy as jnp
from jax import lax
from jax.sharding import PartitionSpec as P

HEAD_DIM = 64


def layer_norm(features, gain_vec, shift_vec):
    centre = features - jnp.mean(features, axis=-1, keepdims=True)
    spread = jnp.mean(centre * centre, axis=-1, keepdims=True)
    return centre * lax.rsqrt(spread + 1e-06) * gain_vec + shift_vec


def place_pairs(choices, ranked, experts, capacity):
    tok_count = choices.shape[0]
    ordered = jnp.concatenate([choices[ranked, 0], choices[ranked, 1]])
    labels = jnp.arange(experts, dtype=jnp.int32)
    onehot = (ordered[:, None] == labels[None, :]).astype(jnp.int32)
    before = jnp.cumsum(onehot, axis=0, dtype=jnp.int32) - onehot
    placed = jnp.sum(before * onehot, axis=1, dtype=jnp.int32)
    first = jnp.zeros((tok_count,), jnp.int32).at[ranked].set(placed[:tok_count])
    second = jnp.zeros((tok_count,), jnp.int32).at[ranked].set(placed[tok_count:])
    slot_pos = jnp.stack([first, second], axis=1)
    target = jnp.where(slot_pos < capacity, choices * capacity + slot_pos, experts * capacity)
    owners = jnp.repeat(jnp.arange(tok_count, dtype=jnp.int32), 2)
    source = (
        jnp.full((experts * capacity + 1,), tok_count, jnp.int32).at[target.reshape(-1)].set(owners)
    )
    return (target, source[: experts * capacity])


def pick_rows(table_rows, slot_index):
    padded = jnp.concatenate(
        [table_rows, jnp.zeros((1, table_rows.shape[1]), table_rows.dtype)], axis=0
    )
    return padded[slot_index]


def per_device(
    tokens,
    cotangent,
    routes,
    order,
    ln1_gain,
    ln1_bias,
    w_qkv,
    w_out,
    b_out,
    ln2_gain,
    ln2_bias,
    w_router,
    w_in,
    b_in,
    w_back,
    b_back,
):
    images, length, model_width = tokens.shape
    tok_count = images * length
    head_count = model_width // HEAD_DIM
    score_scale = HEAD_DIM ** (-0.5)
    gain_one, shift_one, wide_qkv, wide_out, bias_out, gain_two, shift_two, wide_router = (
        lax.all_gather(ln1_gain.astype(jnp.bfloat16), ("group", "expert"), axis=0, tiled=True),
        lax.all_gather(ln1_bias.astype(jnp.bfloat16), ("group", "expert"), axis=0, tiled=True),
        lax.all_gather(w_qkv.astype(jnp.bfloat16), ("group", "expert"), axis=0, tiled=True),
        lax.all_gather(w_out.astype(jnp.bfloat16), ("group", "expert"), axis=0, tiled=True),
        lax.all_gather(b_out.astype(jnp.bfloat16), ("group", "expert"), axis=0, tiled=True),
        lax.all_gather(ln2_gain.astype(jnp.bfloat16), ("group", "expert"), axis=0, tiled=True),
        lax.all_gather(ln2_bias.astype(jnp.bfloat16), ("group", "expert"), axis=0, tiled=True),
        lax.all_gather(w_router.astype(jnp.bfloat16), ("group", "expert"), axis=0, tiled=True),
    )
    experts = wide_router.shape[1]
    capacity = max(2, 5 * tok_count // (2 * experts))
    first_w, first_b, second_w, second_b = (
        lax.all_gather(w_in.astype(jnp.bfloat16), "group", axis=1, tiled=True),
        lax.all_gather(b_in.astype(jnp.bfloat16), "group", axis=1, tiled=True),
        lax.all_gather(w_back.astype(jnp.bfloat16), "group", axis=1, tiled=True),
        lax.all_gather(b_back.astype(jnp.bfloat16), "group", axis=1, tiled=True),
    )
    token_rows = tokens.astype(jnp.float32).reshape(tok_count, model_width)
    normed, norm_one_back = jax.vjp(
        layer_norm, token_rows, gain_one.astype(jnp.float32), shift_one.astype(jnp.float32)
    )
    normed_low = normed.astype(jnp.bfloat16)
    projected = jnp.dot(normed_low, wide_qkv, preferred_element_type=jnp.float32).astype(
        jnp.bfloat16
    )
    projected = projected.reshape(images, length, 3, head_count, HEAD_DIM)
    queries, all_keys, values = (projected[:, :, 0], projected[:, :, 1], projected[:, :, 2])
    scores = (
        jnp.einsum("bqhd,bkhd->bhqk", queries, all_keys, preferred_element_type=jnp.float32)
        * score_scale
    )
    row_max = jnp.max(scores, axis=-1, keepdims=True)
    shifted = jnp.exp(scores - row_max)
    row_total = jnp.sum(shifted, axis=-1, keepdims=True)
    log_total = row_max + jnp.log(row_total)
    weights_low = (shifted / row_total).astype(jnp.bfloat16)
    mixed_rows = jnp.einsum(
        "bhqk,bkhd->bqhd", weights_low, values, preferred_element_type=jnp.float32
    )
    mixed_rows = mixed_rows.astype(jnp.bfloat16).reshape(tok_count, model_width)
    first_sum = (
        token_rows
        + jnp.dot(mixed_rows, wide_out, preferred_element_type=jnp.float32)
        + bias_out.astype(jnp.float32)
    )
    routed, norm_two_back = jax.vjp(
        layer_norm, first_sum, gain_two.astype(jnp.float32), shift_two.astype(jnp.float32)
    )
    routed_low = routed.astype(jnp.bfloat16)
    logits = jnp.dot(routed_low, wide_router, preferred_element_type=jnp.float32)
    gate_probs, gate_back = jax.vjp(lambda entries: jax.nn.softmax(entries, axis=-1), logits)
    choices = routes.reshape(tok_count, 2)
    target, source = place_pairs(choices, order.reshape(tok_count), experts, capacity)
    sent_rows = pick_rows(routed_low, source).reshape(experts, capacity, model_width)
    arrived = lax.all_to_all(sent_rows, "expert", split_axis=0, concat_axis=1, tiled=True)
    inner_pre = jnp.einsum("lrd,ldh->lrh", arrived, first_w, preferred_element_type=jnp.float32)
    inner_pre = inner_pre + first_b.astype(jnp.float32)[:, None, :]
    active, gelu_back = jax.vjp(jax.nn.gelu, inner_pre)
    active_low = active.astype(jnp.bfloat16)
    outcome = jnp.einsum("lrh,lhd->lrd", active_low, second_w, preferred_element_type=jnp.float32)
    outcome = (outcome + second_b.astype(jnp.float32)[:, None, :]).astype(jnp.bfloat16)
    returned = lax.all_to_all(outcome, "expert", split_axis=1, concat_axis=0, tiled=True).reshape(
        experts * capacity, model_width
    )
    picked = pick_rows(returned, target).astype(jnp.float32)
    chosen = jnp.take_along_axis(gate_probs, choices, axis=1)
    mixture = jnp.sum(chosen[:, :, None] * picked, axis=1)
    output = (first_sum + mixture).astype(jnp.bfloat16).reshape(images, length, model_width)
    grad_out = cotangent.astype(jnp.float32).reshape(tok_count, model_width)
    grad_chosen = jnp.sum(grad_out[:, None, :] * picked, axis=2)
    labels = jnp.arange(experts, dtype=jnp.int32)
    onehot = (choices[:, :, None] == labels[None, None, :]).astype(jnp.float32)
    grad_gates = jnp.sum(onehot * grad_chosen[:, :, None], axis=1)
    grad_logits = gate_back(grad_gates)[0].astype(jnp.bfloat16)
    grad_router = jnp.einsum(
        "td,te->de", routed_low, grad_logits, preferred_element_type=jnp.float32
    )
    grad_routed = jnp.einsum(
        "te,de->td", grad_logits, wide_router, preferred_element_type=jnp.float32
    )
    slot_gate = (
        jnp.zeros((experts * capacity + 1,), jnp.float32)
        .at[target.reshape(-1)]
        .set(chosen.reshape(-1))
    )
    slot_gate = slot_gate[: experts * capacity]
    grad_sent = (pick_rows(grad_out, source) * slot_gate[:, None]).astype(jnp.bfloat16)
    grad_arrived = lax.all_to_all(
        grad_sent.reshape(experts, capacity, model_width),
        "expert",
        split_axis=0,
        concat_axis=1,
        tiled=True,
    )
    grad_second_b = jnp.sum(grad_arrived, axis=1, dtype=jnp.float32)
    grad_second_w = jnp.einsum(
        "lrh,lrd->lhd", active_low, grad_arrived, preferred_element_type=jnp.float32
    )
    grad_active = jnp.einsum(
        "lrd,lhd->lrh", grad_arrived, second_w, preferred_element_type=jnp.float32
    )
    grad_inner = gelu_back(grad_active)[0]
    grad_first_b = jnp.sum(grad_inner, axis=1)
    grad_inner_low = grad_inner.astype(jnp.bfloat16)
    grad_first_w = jnp.einsum(
        "lrd,lrh->ldh", arrived, grad_inner_low, preferred_element_type=jnp.float32
    )
    grad_slots = jnp.einsum(
        "lrh,ldh->lrd", grad_inner_low, first_w, preferred_element_type=jnp.float32
    ).astype(jnp.bfloat16)
    share_w_in, share_b_in, share_w_back, share_b_back = (
        lax.psum_scatter(
            grad_first_w.astype(jnp.bfloat16), "group", scatter_dimension=1, tiled=True
        ).astype(jnp.float32),
        lax.psum_scatter(
            grad_first_b.astype(jnp.bfloat16), "group", scatter_dimension=1, tiled=True
        ).astype(jnp.float32),
        lax.psum_scatter(
            grad_second_w.astype(jnp.bfloat16), "group", scatter_dimension=1, tiled=True
        ).astype(jnp.float32),
        lax.psum_scatter(
            grad_second_b.astype(jnp.bfloat16), "group", scatter_dimension=1, tiled=True
        ).astype(jnp.float32),
    )
    grad_returned = lax.all_to_all(
        grad_slots, "expert", split_axis=1, concat_axis=0, tiled=True
    ).reshape(experts * capacity, model_width)
    grad_routed = grad_routed + jnp.sum(pick_rows(grad_returned, target), axis=1, dtype=jnp.float32)
    grad_norm_two, grad_gain_two, grad_shift_two = norm_two_back(grad_routed)
    grad_first = grad_out + grad_norm_two
    grad_bias_out = jnp.sum(grad_first, axis=0)
    grad_first_low = grad_first.astype(jnp.bfloat16)
    grad_wide_out = jnp.einsum(
        "td,te->de", mixed_rows, grad_first_low, preferred_element_type=jnp.float32
    )
    grad_mixed = jnp.einsum(
        "te,de->td", grad_first_low, wide_out, preferred_element_type=jnp.float32
    )
    grad_mixed = grad_mixed.astype(jnp.bfloat16).reshape(images, length, head_count, HEAD_DIM)
    grad_weights = jnp.einsum(
        "bqhd,bkhd->bhqk", grad_mixed, values, preferred_element_type=jnp.float32
    )
    weights_again = jnp.exp(
        jnp.einsum("bqhd,bkhd->bhqk", queries, all_keys, preferred_element_type=jnp.float32)
        * score_scale
        - log_total
    )
    inner_sum = jnp.sum(grad_weights * weights_again, axis=-1, keepdims=True)
    grad_scores = (weights_again * (grad_weights - inner_sum)).astype(jnp.bfloat16)
    grad_queries = (
        jnp.einsum("bhqk,bkhd->bqhd", grad_scores, all_keys, preferred_element_type=jnp.float32)
        * score_scale
    )
    grad_keys = (
        jnp.einsum("bhqk,bqhd->bkhd", grad_scores, queries, preferred_element_type=jnp.float32)
        * score_scale
    )
    grad_values = jnp.einsum(
        "bhqk,bqhd->bkhd", weights_low, grad_mixed, preferred_element_type=jnp.float32
    )
    grad_projected = jnp.stack([grad_queries, grad_keys, grad_values], axis=2).astype(jnp.bfloat16)
    grad_projected = grad_projected.reshape(tok_count, 3 * model_width)
    grad_wide_qkv = jnp.einsum(
        "td,te->de", normed_low, grad_projected, preferred_element_type=jnp.float32
    )
    grad_normed = jnp.einsum(
        "te,de->td", grad_projected, wide_qkv, preferred_element_type=jnp.float32
    )
    grad_rows, grad_gain_one, grad_shift_one = norm_one_back(grad_normed)
    grad_tokens = (grad_first + grad_rows).reshape(images, length, model_width)
    (
        share_gain_one,
        share_shift_one,
        share_qkv,
        share_out,
        share_bias_out,
        share_gain_two,
        share_shift_two,
        share_router,
    ) = (
        lax.psum_scatter(grad_gain_one, ("group", "expert"), scatter_dimension=0, tiled=True),
        lax.psum_scatter(grad_shift_one, ("group", "expert"), scatter_dimension=0, tiled=True),
        lax.psum_scatter(grad_wide_qkv, ("group", "expert"), scatter_dimension=0, tiled=True),
        lax.psum_scatter(grad_wide_out, ("group", "expert"), scatter_dimension=0, tiled=True),
        lax.psum_scatter(grad_bias_out, ("group", "expert"), scatter_dimension=0, tiled=True),
        lax.psum_scatter(grad_gain_two, ("group", "expert"), scatter_dimension=0, tiled=True),
        lax.psum_scatter(grad_shift_two, ("group", "expert"), scatter_dimension=0, tiled=True),
        lax.psum_scatter(grad_router, ("group", "expert"), scatter_dimension=0, tiled=True),
    )
    return (
        output,
        grad_tokens,
        share_gain_one,
        share_shift_one,
        share_qkv,
        share_out,
        share_bias_out,
        share_gain_two,
        share_shift_two,
        share_router,
        share_w_in,
        share_b_in,
        share_w_back,
        share_b_back,
    )


def solution(mesh):
    placed = (
        P(("group", "expert"), None, None),
        P(("group", "expert"), None, None),
        P(("group", "expert"), None, None),
        P(("group", "expert"), None),
        P(("group", "expert")),
        P(("group", "expert")),
        P(("group", "expert"), None),
        P(("group", "expert"), None),
        P(("group", "expert")),
        P(("group", "expert")),
        P(("group", "expert")),
        P(("group", "expert"), None),
        P("expert", "group", None),
        P("expert", "group"),
        P("expert", "group", None),
        P("expert", "group"),
    )
    return jax.shard_map(
        per_device,
        mesh=mesh,
        in_specs=placed,
        out_specs=(
            P(("group", "expert"), None, None),
            P(("group", "expert"), None, None),
            P(("group", "expert")),
            P(("group", "expert")),
            P(("group", "expert"), None),
            P(("group", "expert"), None),
            P(("group", "expert")),
            P(("group", "expert")),
            P(("group", "expert")),
            P(("group", "expert"), None),
            P("expert", "group", None),
            P("expert", "group"),
            P("expert", "group", None),
            P("expert", "group"),
        ),
        check_vma=False,
    )
```

profile of v0, /device:TPU:0, one launch (start us, length us, event | category | flops | bytes accessed | tf_op | source)
XLA Modules:
  0.0 1026.9 jit_solution(15350705115636417793)
XLA Ops:
  18.9 10.5 %gather_fusion = s32[788]{0:T(1024)S(1)} fusion(s32[788,2]{0,1:T(2,128)S(1)} %reshape.447, s32[788]{0:T(1024)S(1)} %get-tuple-element.120), kind=kCustom, calls=%fused_computation | custom fusion | bytes 12608 | tf_op jit(solution)/shard_map/gather | solution.py:17
  29.5 10.5 %gather_fusion.1 = s32[788]{0:T(1024)S(1)} fusion(s32[788,2]{0,1:T(2,128)S(1)} %reshape.447, s32[788]{0:T(1024)S(1)} %get-tuple-element.122), kind=kCustom, calls=%fused_computation.1 | custom fusion | bytes 12608 | tf_op jit(solution)/shard_map/gather | solution.py:17
  61.6 42.2 %all-reduce.19 = (bf16[768]{0:T(1024)(128)(2,1)S(1)}, bf16[768]{0:T(1024)(128)(2,1)S(1)}, bf16[768]{0:T(1024)(128)(2,1)S(1)}, bf16[768]{0:T(1024)(128)(2,1)S(1)}, bf16[768]{0:T(1024)(128)(2,1)S(1)}) all-reduce(bf16[768]{0:T(1024)(128)(2,1)S(1)} %dynamic-update-slice.1, ...), channel_id=1, replica_groups=mesh['group'=4,'expert'=8] {'group','expert'}, use_global_device_ids=true, to_apply=%add.8 | all-reduce | flops 3840 | bytes 15360
  104.8 78.7 %all-gather = bf16[32,24,16]{1,2,0:T(8,128)(2,1)S(1)} all-gather(bf16[1,24,16]{1,2,0:T(8,128)(2,1)S(1)} %convert_bitcast_fusion), channel_id=1, replica_groups=mesh['group'=4,'expert'=8] {'group','expert'}, dimensions={0}, use_global_device_ids=true | all-gather | bytes 25344 | tf_op jit(solution)/shard_map/all_gather | solution.py:70
  204.8 9.4 gather_fusion.4
  226.2 11.9 %reshape.575 = bf16[4,197,3,12,64]{4,3,2,1,0:T(8,128)(2,1)} reshape(bf16[788,2304]{1,0:T(8,128)(2,1)} %convolution_convert_fusion.2) | data formatting | bytes 7262208 | tf_op jit(solution)/shard_map/reshape | solution.py:88
  280.6 20.0 %gather_fusion.6 = f32[1576]{0:T(1024)S(1)} fusion(f32[788,16]{0,1:T(8,128)S(1)} %fusion.33, s32[1576]{0:T(1024)S(1)} %reshape.509), kind=kCustom, calls=%fused_computation.6 | custom fusion | bytes 25216 | tf_op jit(solution)/shard_map/jit(take_along_axis)/gather | solution.py:128
  319.3 9.4 gather_fusion.2
  332.2 55.1 %all-to-all-done.2 = bf16[16,123,768]{2,1,0:T(8,128)(2,1)} async-done(((bf16[16,123,768]{2,1,0:T(8,128)(2,1)}), bf16[16,123,768]{2,1,0:T(8,128)(2,1)}, u32[]{:S(2)}, u32[]{:S(2)}) %all-to-all-start.2) | async-done | bytes 3022880 | tf_op jit(solution)/shard_map/all_to_all | solution.py:150
  406.8 55.0 %all-to-all-done = bf16[16,123,768]{2,1,0:T(8,128)(2,1)S(1)} async-done(((bf16[16,123,768]{2,1,0:T(8,128)(2,1)}), bf16[16,123,768]{2,1,0:T(8,128)(2,1)S(1)}, u32[]{:S(2)}, u32[]{:S(2)}) %all-to-all-start) | async-done | bytes 3022880 | tf_op jit(solution)/shard_map/all_to_all | solution.py:117
  467.3 17.8 %fusion.60 = f32[2,984,3072]{2,1,0:T(8,128)} fusion(bf16[2,984,768]{2,1,0:T(8,128)(2,1)} %all_to_all.51, bf16[2,768,3072]{2,1,0:T(8,128)(2,1)} %all-gather.11.cloned.1.call-done), kind=kOutput, calls=%fused_computation.154 | convolution fusion | flops 9286189056 | bytes 36642816 | tf_op jit(solution)/shard_map/lrd,ldh->lrh/dot_general | solution.py:118
  485.1 30.8 %fusion.51 = (bf16[2,3072]{1,0:T(2,128)(2,1)S(1)}, bf16[2,984,3072]{2,1,0:T(8,128)(2,1)}, bf16[2,984,3072]{2,1,0:T(8,128)(2,1)}) fusion(f32[2,984,3072]{2,1,0:T(8,128)} %fusion.60, f32[2,3072]{1,0:T(2,128)S(1)} %convert_element_type.186, bf16[2,984,768]{2,1,0:T(8,128)(2,1)S(1)} %copy-done.27, bf16[2,3072,768]{2,1,0:T(8,128)(2,1)} %all-gather.13.cloned.1.call-done), kind=kOutput, calls=%fused_computation.146 | convolution fusion | flops 9431279616 | bytes 60862464 | tf_op jit(solution)/shard_map/lrd,lhd->lrh/dot_general | solution.py:161
  517.2 17.6 %convolution_convert_fusion.1 = bf16[2,768,3072]{2,1,0:T(8,128)(2,1)} fusion(bf16[2,984,768]{2,1,0:T(8,128)(2,1)} %all_to_all.51, bf16[2,984,3072]{2,1,0:T(8,128)(2,1)} %get-tuple-element.135), kind=kOutput, calls=%fused_computation.29 | convolution fusion | flops 9290907648 | bytes 24551424 | tf_op jit(solution)/shard_map/lrd,lrh->ldh/dot_general | solution.py:167
  534.9 15.5 %convolution_convert_fusion = bf16[2,3072,768]{2,1,0:T(8,128)(2,1)} fusion(bf16[2,984,3072]{2,1,0:T(8,128)(2,1)} %get-tuple-element.142, bf16[2,984,768]{2,1,0:T(8,128)(2,1)S(1)} %copy-done.27), kind=kOutput, calls=%fused_computation.28 | convolution fusion | flops 9290907648 | bytes 24551424 | tf_op jit(solution)/shard_map/lrh,lrd->lhd/dot_general | solution.py:158
  550.4 18.9 %fusion.10 = bf16[2,984,768]{2,1,0:T(8,128)(2,1)S(1)} fusion(bf16[2,768,3072]{2,1,0:T(8,128)(2,1)} %all-gather.11.cloned.1.call-done, bf16[2,984,3072]{2,1,0:T(8,128)(2,1)} %get-tuple-element.135), kind=kOutput, calls=%fused_computation.57 | convolution fusion | flops 9287700480 | bytes 24551424 | tf_op jit(solution)/shard_map/lrh,ldh->lrd/dot_general | solution.py:170
  583.0 15.3 %add_convert_fusion = bf16[2,984,768]{2,1,0:T(8,128)(2,1)S(1)} fusion(f32[2,768]{1,0:T(2,128)S(1)} %bitcast.151, bf16[2,984,3072]{2,1,0:T(8,128)(2,1)} %get-tuple-element.142, bf16[2,3072,768]{2,1,0:T(8,128)(2,1)} %all-gather.13.cloned.1.call-done), kind=kOutput, calls=%fused_computation.34 | convolution fusion | flops 9289211904 | bytes 24557568 | tf_op jit(solution)/shard_map/lrh,lhd->lrd/dot_general | solution.py:122
  602.3 43.5 %all-to-all-done.3 = bf16[2,984,768]{2,0,1:T(2,128)(2,1)} async-done(((bf16[2,984,768]{2,0,1:T(2,128)(2,1)}), bf16[2,984,768]{2,0,1:T(2,128)(2,1)}, u32[]{:S(2)}, u32[]{:S(2)}) %all-to-all-start.3) | async-done | bytes 3022880 | tf_op jit(solution)/shard_map/all_to_all | solution.py:187
  660.1 57.8 %all-to-all-done.1 = bf16[2,984,768]{2,0,1:T(2,128)(2,1)} async-done(((bf16[2,984,768]{2,0,1:T(2,128)(2,1)}), bf16[2,984,768]{2,0,1:T(2,128)(2,1)}, u32[]{:S(2)}, u32[]{:S(2)}) %all-to-all-start.1) | async-done | bytes 3022880 | tf_op jit(solution)/shard_map/all_to_all | solution.py:124
  745.5 13.7 %multiply_reduce_fusion.2 = (f32[788,2]{1,0:T(8,128)S(1)}, f32[788,768]{1,0:T(8,128)}) fusion(f32[788,2,768]{2,1,0:T(2,128)} %reshape.552, f32[788,768]{1,0:T(8,128)S(1)} %copy-done.4, f32[788,2]{1,0:T(8,128)S(1)} %copy-done.30), kind=kLoop, calls=%fused_computation.36 | loop fusion | flops 4234712 | bytes 9695552 | tf_op jit(solution)/shard_map/reduce_sum | solution.py:132
  766.0 9.6 reduce_sum.266
  811.5 11.9 %multiply_convert_fusion.1 = bf16[4,12,197,197]{2,3,1,0:T(8,128)(2,1)} fusion(f32[4,12,197,197]{2,3,1,0:T(8,128)} %get-tuple-element.161, f32[4,12,197,197]{2,3,1,0:T(8,128)} %copy-done.2, f32[4,12,197]{2,1,0:T(8,128)S(1)} %get-tuple-element.160, f32[4,12,197]{2,1,0:T(8,128)S(1)} %log_add_fusion), kind=kLoop, calls=%fused_computation.20 | loop fusion | flops 9314160 | bytes 18703968 | tf_op jit(solution)/shard_map/convert_element_type | solution.py:211
  837.1 9.8 convert_element_type.203
  871.0 39.2 %all-reduce.18 = (f32[768]{0:T(1024)S(1)}, f32[768]{0:T(1024)S(1)}, f32[768]{0:T(1024)S(1)}, f32[768]{0:T(1024)S(1)}, f32[768]{0:T(1024)S(1)}, /*index=5*/f32[768,16]{0,1:T(8,128)S(1)}) all-reduce(f32[768]{0:T(1024)S(1)} %get-tuple-element.114, ...), channel_id=2, replica_groups=mesh['group'=4,'expert'=8] {'group','expert'}, use_global_device_ids=true, to_apply=%region_26.27.clone | all-reduce | flops 16128 | bytes 129024
  931.7 88.1 %reduce-scatter.12.cloned.1.call-done = f32[24,2304]{1,0:T(8,128)} async-done(((f32[768,2304]{1,0:T(8,128)}), f32[24,2304]{1,0:T(8,128)}) %reduce-scatter.12.cloned.1.call-update) | async-done | bytes 221200 | tf_op jit(solution)/shard_map/reduce_scatter | solution.py:245
  (383 shorter events, 318.7 us)
Async XLA Ops:
  7.2 212.1 %all-gather.7.cloned.1.call-start = ((), (), s32[]{:S(2)}) async-start(), calls=%async_computation.10 | async-start | bytes 3649536 | tf_op jit(solution)/shard_map/all_gather | solution.py:65
  8.8 265.3 %all-gather.9.cloned.1.call-start = ((), (), s32[]{:S(2)}) async-start(), calls=%async_computation.11 | async-start | bytes 1216512 | tf_op jit(solution)/shard_map/all_gather | solution.py:66
  10.4 456.9 %all-gather.11.cloned.1.call-start = ((), (), s32[]{:S(2)}) async-start(), calls=%async_computation.12 | async-start | bytes 11796480 | tf_op jit(solution)/shard_map/all_gather | solution.py:75
  14.6 470.5 %all-gather.13.cloned.1.call-start = ((), (), s32[]{:S(2)}) async-start(), calls=%async_computation.13 | async-start | bytes 11796480 | tf_op jit(solution)/shard_map/all_gather | solution.py:77
  60.5 135.2 %copy-start.36 = (bf16[4,197,768]{2,0,1:T(4,128)(2,1)S(1)}, bf16[4,197,768]{2,0,1:T(4,128)(2,1)}, u32[]{:S(2)}) copy-start(bf16[4,197,768]{2,0,1:T(4,128)(2,1)} %param.17) | copy-start | bytes 3631108
  103.8 115.5 %copy-start.68 = (f32[768]{0:T(1024)}, f32[768]{0:T(1024)S(1)}, u32[]{:S(2)}) copy-start(f32[768]{0:T(1024)S(1)} %convert_element_type.167) | copy-start | bytes 9220
  103.8 115.5 %copy-start.56 = (f32[768]{0:T(1024)}, f32[768]{0:T(1024)S(1)}, u32[]{:S(2)}) copy-start(f32[768]{0:T(1024)S(1)} %convert_element_type.165) | copy-start | bytes 9220
  103.9 174.7 %copy-start.52 = (f32[768]{0:T(1024)}, f32[768]{0:T(1024)S(1)}, u32[]{:S(2)}) copy-start(f32[768]{0:T(1024)S(1)} %convert_element_type.178) | copy-start | bytes 9220
  104.0 115.3 %copy-start.64 = (f32[788]{0:T(1024)}, f32[788]{0:T(1024)S(1)}, u32[]{:S(2)}) copy-start(f32[788]{0:T(1024)S(1)} %div.69) | copy-start | bytes 9460
  104.8 90.0 %copy-start.60 = (f32[788]{0:T(1024)}, f32[788]{0:T(1024)S(1)}, u32[]{:S(2)}) copy-start(f32[788]{0:T(1024)S(1)} %add.224) | copy-start | bytes 9460
  104.8 114.6 %copy-start.66 = (f32[788]{0:T(1024)}, f32[788]{0:T(1024)S(1)}, u32[]{:S(2)}) copy-start(f32[788]{0:T(1024)S(1)} %rsqrt.23) | copy-start | bytes 9460
  183.7 95.7 %copy-start.41 = (bf16[768,16]{0,1:T(8,128)(2,1)}, bf16[768,16]{0,1:T(8,128)(2,1)S(1)}, u32[]{:S(2)}) copy-start(bf16[768,16]{0,1:T(8,128)(2,1)S(1)} %reshape.565) | copy-start | bytes 73732
  314.6 72.7 %all-to-all-start.2 = ((bf16[16,123,768]{2,1,0:T(8,128)(2,1)}), bf16[16,123,768]{2,1,0:T(8,128)(2,1)}, u32[]{:S(2)}, u32[]{:S(2)}) async-start(bf16[16,123,768]{2,1,0:T(8,128)(2,1)} %multiply_convert_fusion.2), calls=%async_computation.2 | async-start | bytes 6291456 | tf_op jit(solution)/shard_map/all_to_all | solution.py:150
  332.2 58.8 %copy-start.73 = (f32[2,768]{1,0:T(2,128)S(1)}, f32[2,768]{1,0:T(2,128)}, u32[]{:S(2)}) copy-start(f32[2,768]{1,0:T(2,128)} %param.29) | copy-start | bytes 18436
  387.3 74.5 %all-to-all-start = ((bf16[16,123,768]{2,1,0:T(8,128)(2,1)}), bf16[16,123,768]{2,1,0:T(8,128)(2,1)S(1)}, u32[]{:S(2)}, u32[]{:S(2)}) async-start(bf16[16,123,768]{2,1,0:T(8,128)(2,1)} %reshape.453), calls=%async_computation | async-start | bytes 6291456 | tf_op jit(solution)/shard_map/all_to_all | solution.py:117
  391.0 464.2 %reduce-scatter.22.cloned.1.call-start = ((), (), s32[]{:S(2)}) async-start(), calls=%async_computation.19 | async-start | bytes 245760
  467.2 389.5 %reduce-scatter.20.cloned.1.call-start = ((), (), s32[]{:S(2)}) async-start(), calls=%async_computation.18 | async-start | bytes 983040
  517.2 405.7 %reduce-scatter.16.cloned.1.call-start = ((), (), s32[]{:S(2)}) async-start(), calls=%async_computation.16 | async-start | bytes 11796480 | tf_op jit(solution)/shard_map/reduce_scatter | solution.py:174
  534.9 392.5 %reduce-scatter.18.cloned.1.call-start = ((), (), s32[]{:S(2)}) async-start(), calls=%async_computation.17 | async-start | bytes 11796480 | tf_op jit(solution)/shard_map/reduce_scatter | solution.py:180
  573.3 72.6 %all-to-all-start.3 = ((bf16[2,984,768]{2,0,1:T(2,128)(2,1)}), bf16[2,984,768]{2,0,1:T(2,128)(2,1)}, u32[]{:S(2)}, u32[]{:S(2)}) async-start(bf16[2,984,768]{2,0,1:T(2,128)(2,1)} %copy.278), calls=%async_computation.3 | async-start | bytes 6045696 | tf_op jit(solution)/shard_map/all_to_all | solution.py:187
  645.9 72.0 %all-to-all-start.1 = ((bf16[2,984,768]{2,0,1:T(2,128)(2,1)}), bf16[2,984,768]{2,0,1:T(2,128)(2,1)}, u32[]{:S(2)}, u32[]{:S(2)}) async-start(bf16[2,984,768]{2,0,1:T(2,128)(2,1)} %copy.268), calls=%async_computation.1 | async-start | bytes 6045696 | tf_op jit(solution)/shard_map/all_to_all | solution.py:124
  650.4 281.3 %reduce-scatter.14.cloned.1.call-start = ((), (), s32[]{:S(2)}) async-start(), calls=%async_computation.15 | async-start | bytes 2433024 | tf_op jit(solution)/shard_map/reduce_scatter | solution.py:246
  797.3 222.5 %reduce-scatter.12.cloned.1.call-start = ((), (), s32[]{:S(2)}) async-start(), calls=%async_computation.14 | async-start | bytes 7299072 | tf_op jit(solution)/shard_map/reduce_scatter | solution.py:245
  862.1 51.0 %copy-start.25 = (f32[788,768]{1,0:T(8,128)S(1)}, f32[788,768]{1,0:T(8,128)}, u32[]{:S(2)}) copy-start(f32[788,768]{1,0:T(8,128)} %reshape.444) | copy-start | bytes 7262212
  (72 other events, 877.8 us)
Sparse Core Ops, SparseCore 0:
  11.5 62.9 all-gather.6
  78.0 53.0 all-gather.8
  133.2 63.0 all-gather.10
  197.8 64.2 all-gather.12
  467.3 18.7 reduce-scatter.21
  517.3 22.2 reduce-scatter.19
  542.3 78.4 reduce-scatter.15
  623.6 78.4 reduce-scatter.17
  797.4 98.2 reduce-scatter.13
  901.8 117.9 reduce-scatter.11
where the time goes:
time: 1030 us
  waiting for transfers between devices  300 us (29%)
  local copies, waits for them, and re-layouts  256 us (25%)
  matrix products  177 us (17%)
  blocking collectives  170 us (17%)
  other arithmetic  89.3 us (9%)
  starting transfers between devices  17.7 us (2%)
  between operations  16 us (2%)
    reduce_scatter x1, waiting for transfers between devices, per_device(): lax.psum_scatter(grad_wide_qkv, ('group', 'expert'), scatter_dimension=0,...  88.1 us
    unnamed x2, blocking collectives  81.4 us
    all_gather x1, blocking collectives, per_device(): lax.all_gather(w_router.astype(jnp.bfloat16), ('group', 'expert'), axis=0...  78.7 us
    all_to_all x1, waiting for transfers between devices, per_device(): lax.all_to_all(outcome, 'expert', split_axis=1, concat_axis=0, tiled=True)  57.8 us
    all_to_all x1, waiting for transfers between devices, per_device(): lax.all_to_all(grad_sent.reshape(experts, capacity, model_width), 'expert...  55.1 us
    all_to_all x1, waiting for transfers between devices, per_device(): lax.all_to_all(sent_rows, 'expert', split_axis=0, concat_axis=1, tiled=True)  55 us
    all_to_all x1, waiting for transfers between devices, per_device(): lax.all_to_all(grad_slots, 'expert', split_axis=1, concat_axis=0, tiled=T...  43.5 us
    gather x5, local copies, waits for them, and re-layouts, pick_rows(): return padded[slot_index]  36.3 us
  transfers between devices with their start and end apart: 14, of which 5 were waited for; matrix products, arithmetic and copies ran while one was open for 49% of the time, Pallas kernels for 0%

commit v1 on v0

v1 whole, which is shorter than its diff:
```python
import functools

import jax
import jax.numpy as jnp
from jax import lax
from jax.experimental import pallas as pl
from jax.experimental.pallas import tpu as pltpu
from jax.sharding import PartitionSpec as P

HEAD_DIM = 64
LANES = 128
VECTORS = 5
f32 = jnp.float32
bf16 = jnp.bfloat16
BOTH = ("group", "expert")


def dot(a, b):
    return lax.dot_general(a, b, (((1,), (0,)), ((), ())), preferred_element_type=f32)


def dot_nt(a, b):
    return lax.dot_general(a, b, (((1,), (1,)), ((), ())), preferred_element_type=f32)


def dot_tn(a, b):
    return lax.dot_general(a, b, (((0,), (0,)), ((), ())), preferred_element_type=f32)


def iota(shape, dim):
    return lax.broadcasted_iota(jnp.int32, shape, dim)


def params(mib, grid=1):
    return pltpu.CompilerParams(
        vmem_limit_bytes=mib * 1024 * 1024, dimension_semantics=("arbitrary",) * grid
    )


def three_parts(value):
    high = value.astype(bf16).astype(f32)
    rest = value - high
    mid = rest.astype(bf16).astype(f32)
    return high, mid, rest - mid


def norm_parts(rows):
    centre = rows - jnp.mean(rows, axis=-1, keepdims=True)
    spread = jnp.mean(centre * centre, axis=-1, keepdims=True)
    scale = lax.rsqrt(spread + 1e-06)
    return centre * scale, scale


def norm_backward(grad, unit, scale, gain):
    lead = grad * gain
    first = jnp.mean(lead, axis=-1, keepdims=True)
    second = jnp.mean(lead * unit, axis=-1, keepdims=True)
    return scale * (lead - first - unit * second)


def load_weights(step, core, parts, scratch, sems):
    copies = []
    for k, (own, other) in enumerate(parts):
        copies.append(pltpu.make_async_copy(own, scratch[k].at[:, core], sems.at[2 * k]))
        copies.append(pltpu.make_async_copy(other, scratch[k].at[:, 1 - core], sems.at[2 * k + 1]))

    @pl.when(step == 0)
    def _():
        for copy in copies:
            copy.start()
        for copy in copies:
            copy.wait()


def route_kernel(labels, cap, capp, routes_ref, order_ref, rows_ref, cols_ref):
    images, _, length = routes_ref.shape
    tok_count = order_ref.shape[1]
    order = order_ref[...]
    label = iota((labels, length), 0)
    perms, hots = [], []
    counts = jnp.zeros((2 * labels, tok_count), f32)
    for i in range(images):
        perm = jnp.where(iota((length, tok_count), 0) + i * length == order, 1.0, 0.0).astype(bf16)
        hot = jnp.concatenate(
            [
                jnp.where(label == routes_ref[i, 0:1, :], 1.0, 0.0),
                jnp.where(label == routes_ref[i, 1:2, :], 1.0, 0.0),
            ],
            axis=0,
        )
        perms.append(perm)
        hots.append(hot)
        counts = counts + dot(hot.astype(bf16), perm)
    earlier = jnp.where(
        iota((tok_count, tok_count), 0) < iota((tok_count, tok_count), 1), 1.0, 0.0
    ).astype(bf16)
    before = dot(counts.astype(bf16), earlier)
    total = jnp.sum(counts[:labels], axis=1, keepdims=True)
    before = jnp.concatenate([before[:labels], before[labels:] + total], axis=0)
    before = jnp.minimum(before, float(cap)).astype(bf16)
    same = jnp.where(iota((length, length), 0) == iota((length, length), 1), 1.0, 0.0).astype(bf16)
    for i in range(images):
        back = dot_nt(before, perms[i]) * hots[i]
        slot_one = jnp.sum(back[:labels], axis=0, keepdims=True)
        slot_two = jnp.sum(back[labels:], axis=0, keepdims=True)
        one = routes_ref[i, 0:1, :].astype(f32)
        two = routes_ref[i, 1:2, :].astype(f32)
        kept_one = jnp.where(slot_one < cap, one, -1.0)
        kept_two = jnp.where(slot_two < cap, two, -1.0)
        slot_one = jnp.where(slot_one < cap, slot_one, 0.0)
        slot_two = jnp.where(slot_two < cap, slot_two, 0.0)
        aim_one = (kept_one * capp + slot_one).astype(jnp.int32)
        aim_two = (kept_two * capp + slot_two).astype(jnp.int32)
        rows_ref[i] = jnp.concatenate(
            [aim_one, aim_two, jnp.zeros((6, length), jnp.int32)], axis=0
        )
        stacked = jnp.concatenate(
            [kept_one, slot_one, kept_two, slot_two, one, two, one, two], axis=0
        ).astype(bf16)
        turned = dot_nt(same, stacked)
        cols_ref[i] = jnp.concatenate(
            [
                turned[:, 0:1] * capp + turned[:, 1:2],
                turned[:, 2:3] * capp + turned[:, 3:4],
                turned[:, 4:5],
                turned[:, 5:6],
                turned[:, 4:8],
            ],
            axis=1,
        ).astype(jnp.int32)


def route(routes, order, labels, cap, capp):
    images, _, length = routes.shape
    return pl.pallas_call(
        functools.partial(route_kernel, labels, cap, capp),
        out_shape=(
            jax.ShapeDtypeStruct((images, 8, length), jnp.int32),
            jax.ShapeDtypeStruct((images, length, 8), jnp.int32),
        ),
        compiler_params=pltpu.CompilerParams(vmem_limit_bytes=40 * 1024 * 1024),
        name="route_tokens",
    )(routes, order)


def dispatch_kernel(cap, capp, owners, local, gated, joint, rows_ref, value_ref, *refs):
    images, length, width = value_ref.shape
    outs = refs[1:] if gated else refs
    span = owners * capp
    for l in range(local):
        slots = iota((span, length), 0) + l * span
        total = None
        gate_rows = None
        for i in range(images):
            one = slots == rows_ref[i, 0:1, :]
            two = slots == rows_ref[i, 1:2, :]
            both = jnp.where(one | two, 1.0, 0.0).astype(bf16)
            part = dot(both, value_ref[i])
            total = part if total is None else total + part
            if gated:
                gates = refs[0][i]
                first = dot_nt(gates[0:8], jnp.where(one, 1.0, 0.0).astype(bf16))
                second = dot_nt(gates[8:16], jnp.where(two, 1.0, 0.0).astype(bf16))
                part = first + second
                gate_rows = part if gate_rows is None else gate_rows + part
        for o in range(owners):
            block = total[o * capp : (o + 1) * capp]
            if joint:
                outs[0][o, l * capp : (l + 1) * capp, :] = block.astype(bf16)
            else:
                outs[l][o] = block.astype(bf16)
            if gated:
                tail = block[capp - 16 :, 0:capp]
                spare = gate_rows[:, o * capp : (o + 1) * capp]
                line = iota((16, capp), 0) - (cap - (capp - 16))
                for k in range(3):
                    tail = jnp.where(line == k, spare[k : k + 1], tail)
                outs[l][o, capp - 16 :, 0:capp] = tail.astype(bf16)


def dispatch(rows, values, gates, cap, capp, owners, local):
    width = values.shape[2]
    joint = gates is None
    operands = (rows, values) if joint else (rows, values, gates)
    out_shape = [jax.ShapeDtypeStruct((owners, capp, width), bf16)] * local
    if joint:
        out_shape = [jax.ShapeDtypeStruct((owners, local * capp, width), bf16)]
    return pl.pallas_call(
        functools.partial(dispatch_kernel, cap, capp, owners, local, not joint, joint),
        out_shape=out_shape,
        compiler_params=pltpu.CompilerParams(vmem_limit_bytes=40 * 1024 * 1024),
        name="fill_slots",
    )(*operands)


def forward_kernel(
    labels,
    core_ref,
    tokens_ref,
    routes_ref,
    one_own,
    one_other,
    two_own,
    two_other,
    qkv_ref,
    mixed_ref,
    lse_ref,
    first_ref,
    routed_ref,
    gates_ref,
    gate_rows_ref,
    total_ref,
    one_ref,
    two_ref,
    misc_ref,
    sems,
):
    _, length, width = tokens_ref.shape
    step = pl.program_id(0)
    parts = ((one_own, one_other), (two_own, two_other))
    load_weights(step, core_ref[0], parts, (one_ref, two_ref), sems)

    @pl.when(step == 0)
    def _():
        misc_ref[...] = jnp.transpose(two_ref[..., 2 * width :].reshape(width, LANES))

    vec = [misc_ref[labels + k : labels + k + 1, :].astype(f32) for k in range(VECTORS)]
    rows = tokens_ref[0].astype(f32)
    unit, _ = norm_parts(rows)
    normed = (unit * vec[0] + vec[1]).astype(bf16)
    projected = jnp.concatenate(
        [
            dot(normed, one_ref[...].reshape(width, 2 * width)).astype(bf16),
            dot(normed, two_ref[..., 0:width].reshape(width, width)).astype(bf16),
        ],
        axis=1,
    )
    qkv_ref[0] = projected
    lane = iota((length, LANES), 1)
    low_half = lane < HEAD_DIM
    pieces = []
    for pair in range(width // LANES):
        at = pair * LANES
        query = projected[:, at : at + LANES] * jnp.asarray(HEAD_DIM**-0.5, bf16)
        keys = projected[:, width + at : width + at + LANES]
        values = projected[:, 2 * width + at : 2 * width + at + LANES]
        mixed = None
        for half in range(2):
            own = low_half if half == 0 else jnp.logical_not(low_half)
            scores = dot_nt(jnp.where(own, query, jnp.zeros_like(query)), keys)
            top = jnp.max(scores, axis=-1, keepdims=True)
            shifted = jnp.exp(scores - top)
            total = jnp.sum(shifted, axis=-1, keepdims=True)
            head = 2 * pair + half
            total_ref[0:length, :] = jnp.where(
                lane == head, top + jnp.log(total), total_ref[0:length, :]
            )
            low = (shifted * (1.0 / total)).astype(bf16)
            part = dot(low, jnp.where(own, values, jnp.zeros_like(values)))
            mixed = part if mixed is None else mixed + part
        pieces.append(mixed.astype(bf16))
    mixed = jnp.concatenate(pieces, axis=1)
    mixed_ref[0] = mixed
    lse_ref[0] = jnp.transpose(total_ref[...])[0:16]
    w_out = two_ref[..., width : 2 * width].reshape(width, width)
    first = rows + dot(mixed, w_out) + vec[2]
    first_ref[0] = first
    unit, _ = norm_parts(first)
    routed = (unit * vec[3] + vec[4]).astype(bf16)
    routed_ref[0] = routed
    router = misc_ref[0:labels, :]
    logits = dot_nt(routed, router)
    shifted = jnp.exp(logits - jnp.max(logits, axis=1, keepdims=True))
    gates_ref[0] = shifted / jnp.sum(shifted, axis=1, keepdims=True)
    logits = dot_nt(router, routed)
    shifted = jnp.exp(logits - jnp.max(logits, axis=0, keepdims=True))
    gates = shifted / jnp.sum(shifted, axis=0, keepdims=True)
    label = iota((labels, length), 0)
    blank = jnp.zeros((5, length), f32)
    stack = []
    for k in range(2):
        chosen = jnp.where(label == routes_ref[0, k : k + 1, :], gates, 0.0)
        stack += [*three_parts(jnp.sum(chosen, axis=0, keepdims=True)), blank]
    gate_rows_ref[0] = jnp.concatenate(stack, axis=0).astype(bf16)


def weight_scratch(packed):
    return [
        pltpu.VMEM((part[0].shape[0], 2, *part[0].shape[1:]), part[0].dtype) for part in packed
    ]


def forward(core, tokens, routes, packed, labels):
    images, length, width = tokens.shape
    whole = lambda *tail: pl.BlockSpec((1, *tail), lambda i: (i, 0, 0))
    lanes = -(-length // LANES) * LANES
    return pl.pallas_call(
        functools.partial(forward_kernel, labels),
        grid=(images,),
        in_specs=[
            pl.BlockSpec(memory_space=pltpu.SMEM),
            whole(length, width),
            whole(2, length),
            *[pl.BlockSpec(memory_space=pl.ANY)] * 4,
        ],
        out_specs=[
            whole(length, 3 * width),
            whole(length, width),
            whole(16, lanes),
            whole(length, width),
            whole(length, width),
            whole(length, labels),
            whole(16, length),
        ],
        out_shape=[
            jax.ShapeDtypeStruct((images, length, 3 * width), bf16),
            jax.ShapeDtypeStruct((images, length, width), bf16),
            jax.ShapeDtypeStruct((images, 16, lanes), f32),
            jax.ShapeDtypeStruct((images, length, width), f32),
            jax.ShapeDtypeStruct((images, length, width), bf16),
            jax.ShapeDtypeStruct((images, length, labels), f32),
            jax.ShapeDtypeStruct((images, 16, length), bf16),
        ],
        scratch_shapes=[
            pltpu.VMEM((lanes, LANES), f32),
            *weight_scratch(packed),
            pltpu.VMEM((LANES, width), bf16),
            pltpu.SemaphoreType.DMA((4,)),
        ],
        compiler_params=params(40),
        cost_estimate=pl.CostEstimate(
            flops=16_000_000_000, bytes_accessed=20_000_000, transcendentals=2_000_000
        ),
        name="attention_forward",
    )(core, tokens, routes, *packed[0], *packed[1])


def expert_kernel(
    cap,
    rows_ref,
    cot_ref,
    win_ref,
    wback_ref,
    bback_ref,
    out_ref,
    grad_ref,
    gwin_ref,
    gwback_ref,
    turned_ref,
    grad_out_ref,
    out_acc_ref,
    grad_acc_ref,
    active_ref,
    inner_ref,
    bias_ref,
):
    owners, capp, width = rows_ref.shape
    hidden = win_ref.shape[-1]
    total = owners * capp
    spare = cap - (capp - 16)
    step = pl.program_id(0)
    last = pl.num_programs(0) - 1

    @pl.when(step == 0)
    def _():
        summed = jnp.zeros((1, width), f32)
        for b in range(owners):
            tail = rows_ref[b, capp - 16 :, 0:capp].astype(f32)
            gate = (
                tail[spare : spare + 1] + tail[spare + 1 : spare + 2] + tail[spare + 2 : spare + 3]
            )
            gate = jnp.transpose(jnp.broadcast_to(gate, (LANES, capp)))[:, 0:1]
            part = (cot_ref[b].astype(f32) * gate).astype(bf16)
            grad_out_ref[b * capp : (b + 1) * capp, :] = part
            summed = summed + jnp.sum(part.astype(f32), axis=0, keepdims=True)
            turned_ref[:, b * capp : (b + 1) * capp] = jnp.transpose(rows_ref[b])
        bias_ref[...] = jnp.broadcast_to(summed, bias_ref.shape)
        out_acc_ref[...] = jnp.zeros_like(out_acc_ref)
        grad_acc_ref[...] = jnp.zeros_like(grad_acc_ref)

    first = win_ref[...].reshape(width, hidden)
    second = wback_ref[0, 0, 0:hidden, :]
    bias = wback_ref[0, 0, hidden : hidden + 16, :].astype(f32)[0:1, 0:hidden]
    bias_sum = jnp.zeros((1, hidden), f32)
    per = max(1, 256 // capp)
    k0 = 0.7978845608028654
    k1 = 0.044715
    for c in range(owners // per):
        at = slice(c * per * capp, (c + 1) * per * capp)
        block = rows_ref[c * per : (c + 1) * per].reshape(per * capp, width)
        inner = dot(block, first) + bias
        square = inner * inner
        curve = jnp.tanh(inner * (k0 + (k0 * k1) * square))
        half = 0.5 * (1.0 + curve)
        low = (inner * half).astype(bf16)
        active_ref[at, :] = low
        slope = half + (0.5 * inner) * (1.0 - curve * curve) * (k0 + (3.0 * k0 * k1) * square)
        grad_inner = dot_nt(grad_out_ref[at, :], second) * slope
        bias_sum = bias_sum + jnp.sum(grad_inner, axis=0, keepdims=True)
        grad_low = grad_inner.astype(bf16)
        inner_ref[at, :] = grad_low
        out_acc_ref[at, :] += dot(low, second)
        grad_acc_ref[at, :] += dot_nt(grad_low, first)
    gwin_ref[...] = dot(turned_ref[...], inner_ref[...]).astype(bf16).reshape(gwin_ref.shape)
    gwback_ref[0, 0:hidden, :] = dot_tn(active_ref[...], grad_out_ref[...]).astype(bf16)
    row = iota((16, width), 0)
    if hidden < width:
        bias_sum = jnp.concatenate([bias_sum, jnp.zeros((1, width - hidden), f32)], axis=1)
    pad = jnp.where(row == 0, bias_sum, jnp.where(row == 1, bias_ref[0:1, :], 0.0))
    gwback_ref[0, hidden : hidden + 16, :] = pad.astype(bf16)

    @pl.when(step == last)
    def _():
        for b in range(owners):
            at = slice(b * capp, (b + 1) * capp)
            result = (out_acc_ref[at, :] + bback_ref[...].astype(f32)).astype(bf16)
            out_ref[b] = result
            score = jnp.sum(result.astype(f32) * cot_ref[b].astype(f32), axis=1, keepdims=True)
            score = jnp.transpose(jnp.broadcast_to(score, (capp, LANES)))[0:1, :]
            back = grad_acc_ref[at, :]
            grad_ref[b] = back.astype(bf16)
            tail = back[capp - 16 :, 0:capp]
            line = iota((16, capp), 0) - spare
            for k, part in enumerate(three_parts(score)):
                tail = jnp.where(line == k, part, tail)
            grad_ref[b, capp - 16 :, 0:capp] = tail.astype(bf16)


def expert(rows, cots, win, wback, bback, which, cap):
    owners, capp, width = rows.shape
    groups, _, depth, wide = win.shape
    hidden = wide // groups
    total = owners * capp
    full = lambda shape: pl.BlockSpec(shape, lambda j: (0,) * len(shape))
    flops = 2 * 6 * total * width * wide
    return pl.pallas_call(
        functools.partial(expert_kernel, cap),
        grid=(groups,),
        in_specs=[
            full((owners, capp, width)),
            pl.BlockSpec((owners, capp, width), lambda j: (0, which, 0)),
            pl.BlockSpec((groups, 1, depth, hidden), lambda j: (0, which, 0, j)),
            pl.BlockSpec((1, 1, hidden + 16, width), lambda j: (j, which, 0, 0)),
            full((1, width)),
        ],
        out_specs=[
            full((owners, capp, width)),
            full((owners, capp, width)),
            pl.BlockSpec((groups, depth, hidden), lambda j: (0, 0, j)),
            pl.BlockSpec((1, hidden + 16, width), lambda j: (j, 0, 0)),
        ],
        out_shape=[
            jax.ShapeDtypeStruct((owners, capp, width), bf16),
            jax.ShapeDtypeStruct((owners, capp, width), bf16),
            jax.ShapeDtypeStruct((groups, depth, wide), bf16),
            jax.ShapeDtypeStruct((groups, hidden + 16, width), bf16),
        ],
        scratch_shapes=[
            pltpu.VMEM((width, total), bf16),
            pltpu.VMEM((total, width), bf16),
            pltpu.VMEM((total, width), f32),
            pltpu.VMEM((total, width), f32),
            pltpu.VMEM((total, hidden), bf16),
            pltpu.VMEM((total, hidden), bf16),
            pltpu.VMEM((8, width), f32),
        ],
        compiler_params=params(56),
        cost_estimate=pl.CostEstimate(
            flops=flops, bytes_accessed=30_000_000, transcendentals=total * wide
        ),
        name="expert_rows",
    )(rows, cots, win, wback, bback)


def add_to(ref, columns, value):
    shape = (*ref.shape[:-1], value.shape[-1])
    ref[..., columns] += value.reshape(shape)


def backward_kernel(
    labels,
    local,
    cap,
    core_ref,
    tokens_ref,
    cot_ref,
    cols_ref,
    qkv_ref,
    mixed_ref,
    lse_ref,
    first_ref,
    routed_ref,
    gates_ref,
    one_own,
    one_other,
    two_own,
    two_other,
    *refs,
):
    slots = refs[:local]
    (
        grad_tokens_ref,
        keep_one_ref,
        send_one_ref,
        keep_two_ref,
        send_two_ref,
        grad_one_ref,
        grad_two_ref,
        stack_ref,
        vec_ref,
        score_ref,
        one_ref,
        two_ref,
        misc_ref,
        sems,
    ) = refs[local:]
    _, length, width = tokens_ref.shape
    owners, capp, _ = slots[0].shape
    spare = cap - (capp - 16)
    span = owners * capp
    step = pl.program_id(0)
    parts = ((one_own, one_other), (two_own, two_other))
    load_weights(step, core_ref[0], parts, (one_ref, two_ref), sems)

    @pl.when(step == 0)
    def _():
        misc_ref[...] = jnp.transpose(two_ref[..., 2 * width :].reshape(width, LANES))

    vec = [misc_ref[labels + k : labels + k + 1, :].astype(f32) for k in range(VECTORS)]

    @pl.when(step == 0)
    def _():
        grad_one_ref[...] = jnp.zeros_like(grad_one_ref)
        grad_two_ref[...] = jnp.zeros_like(grad_two_ref)
        vec_ref[...] = jnp.zeros_like(vec_ref)
        stack_ref[...] = jnp.zeros_like(stack_ref)
        for l in range(local):
            for o in range(owners):
                score_ref[:, l * span + o * capp : l * span + (o + 1) * capp] = slots[l][
                    o, capp - 16 :, 0:capp
                ]

    cot = cot_ref[0].astype(f32)
    aim_one, aim_two = cols_ref[0, :, 0:1], cols_ref[0, :, 1:2]
    route_one, route_two = cols_ref[0, :, 2:3], cols_ref[0, :, 3:4]
    picked = None
    gate_one = None
    gate_two = None
    for l in range(local):
        lane = iota((length, span), 1) + l * span
        one = jnp.where(lane == aim_one, 1.0, 0.0)
        two = jnp.where(lane == aim_two, 1.0, 0.0)
        part = dot((one + two).astype(bf16), slots[l][...].reshape(span, width))
        picked = part if picked is None else picked + part
        score = score_ref[:, l * span : (l + 1) * span]
        part_one = dot_nt(one.astype(bf16), score)
        part_two = dot_nt(two.astype(bf16), score)
        gate_one = part_one if gate_one is None else gate_one + part_one
        gate_two = part_two if gate_two is None else gate_two + part_two
    line = iota((length, 16), 1)
    mine = (line >= spare) & (line < spare + 3)
    gate_one = jnp.sum(jnp.where(mine, gate_one, 0.0), axis=1, keepdims=True)
    gate_two = jnp.sum(jnp.where(mine, gate_two, 0.0), axis=1, keepdims=True)
    label = iota((length, labels), 1)
    grad_gates = jnp.where(label == route_one, gate_one, 0.0) + jnp.where(
        label == route_two, gate_two, 0.0
    )
    gates = gates_ref[0]
    inner = jnp.sum(grad_gates * gates, axis=1, keepdims=True)
    grad_logits = (gates * (grad_gates - inner)).astype(bf16)
    router = misc_ref[0:labels, :]
    routed = routed_ref[0]
    stack_ref[0:labels, :] += dot_tn(grad_logits, routed)
    grad_routed = dot(grad_logits, router) + picked
    unit, scale = norm_parts(first_ref[0])
    vec_ref[3:4, :] += jnp.sum(grad_routed * unit, axis=0, keepdims=True)
    vec_ref[4:5, :] += jnp.sum(grad_routed, axis=0, keepdims=True)
    grad_first = cot + norm_backward(grad_routed, unit, scale, vec[3])
    vec_ref[2:3, :] += jnp.sum(grad_first, axis=0, keepdims=True)
    first_low = grad_first.astype(bf16)
    add_to(grad_two_ref, slice(width, 2 * width), dot_tn(mixed_ref[0], first_low))
    w_out = two_ref[..., width : 2 * width].reshape(width, width)
    grad_mixed = dot_nt(first_low, w_out).astype(bf16)
    low_half = iota((length, LANES), 1) < HEAD_DIM
    rate = jnp.asarray(HEAD_DIM**-0.5, bf16)
    grads = [[], [], []]
    for pair in range(width // LANES):
        at = pair * LANES
        query = qkv_ref[0, :, at : at + LANES] * rate
        keys = qkv_ref[0, :, width + at : width + at + LANES]
        values = qkv_ref[0, :, 2 * width + at : 2 * width + at + LANES]
        mix = grad_mixed[:, at : at + LANES]
        grad_q = grad_k = grad_v = None
        for half in range(2):
            own = low_half if half == 0 else jnp.logical_not(low_half)
            none = jnp.zeros_like(query)
            query_own = jnp.where(own, query, none)
            mix_own = jnp.where(own, mix, none)
            head = 2 * pair + half
            probs = jnp.exp(dot_nt(keys, query_own) - lse_ref[0, head : head + 1, 0:length])
            grad_probs = dot_nt(values, mix_own)
            inner = jnp.sum(grad_probs * probs, axis=0, keepdims=True)
            scores = (probs * (grad_probs - inner)).astype(bf16)
            part = dot(probs.astype(bf16), mix_own)
            grad_v = part if grad_v is None else grad_v + part
            part = dot(scores, query_own)
            grad_k = part if grad_k is None else grad_k + part
            part = dot_tn(scores, jnp.where(own, keys, none))
            grad_q = part if grad_q is None else grad_q + part
        grads[0].append((grad_q * HEAD_DIM**-0.5).astype(bf16))
        grads[1].append(grad_k.astype(bf16))
        grads[2].append(grad_v.astype(bf16))
    grad_one = jnp.concatenate(grads[0] + grads[1], axis=1)
    grad_two = jnp.concatenate(grads[2], axis=1)
    rows = tokens_ref[0].astype(f32)
    unit, scale = norm_parts(rows)
    normed = (unit * vec[0] + vec[1]).astype(bf16)
    add_to(grad_one_ref, slice(None), dot_tn(normed, grad_one))
    add_to(grad_two_ref, slice(0, width), dot_tn(normed, grad_two))
    grad_normed = dot_nt(grad_one, one_ref[...].reshape(width, 2 * width))
    grad_normed += dot_nt(grad_two, two_ref[..., 0:width].reshape(width, width))
    vec_ref[0:1, :] += jnp.sum(grad_normed * unit, axis=0, keepdims=True)
    vec_ref[1:2, :] += jnp.sum(grad_normed, axis=0, keepdims=True)
    grad_tokens_ref[0] = grad_first + norm_backward(grad_normed, unit, scale, vec[0])

    @pl.when(step == pl.num_programs(0) - 1)
    def _():
        stack_ref[labels : labels + 8, :] = vec_ref[...]
        add_to(grad_two_ref, slice(2 * width, None), jnp.transpose(stack_ref[...]))
        mine, other = core_ref[0], 1 - core_ref[0]
        keep_one_ref[...] = grad_one_ref[:, mine]
        keep_two_ref[...] = grad_two_ref[:, mine]
        send_one_ref[...] = grad_one_ref[:, other].astype(bf16)
        send_two_ref[...] = grad_two_ref[:, other].astype(bf16)


def backward(
    core, tokens, cot, cols, qkv, mixed, lse, first, routed, gates, cap, packed, slots, labels
):
    images, length, width = tokens.shape
    local = len(slots)
    owners, capp, _ = slots[0].shape
    whole = lambda *tail: pl.BlockSpec((1, *tail), lambda i: (i, 0, 0))
    shapes = [part[0].shape for part in packed]
    still = lambda shape: pl.BlockSpec(shape, lambda i: (0, 0, 0))
    return pl.pallas_call(
        functools.partial(backward_kernel, labels, local, cap),
        grid=(images,),
        in_specs=[
            pl.BlockSpec(memory_space=pltpu.SMEM),
            whole(length, width),
            whole(length, width),
            whole(length, 8),
            whole(length, 3 * width),
            whole(length, width),
            whole(*lse.shape[1:]),
            whole(length, width),
            whole(length, width),
            whole(length, labels),
            *[pl.BlockSpec(memory_space=pl.ANY)] * 4,
            *[pl.BlockSpec((owners, capp, width), lambda i: (0, 0, 0))] * local,
        ],
        out_specs=[
            whole(length, width),
            *[still(shape) for shape in shapes for _ in range(2)],
        ],
        out_shape=[
            jax.ShapeDtypeStruct((images, length, width), f32),
            *[jax.ShapeDtypeStruct(shape, kind) for shape in shapes for kind in (f32, bf16)],
        ],
        scratch_shapes=[
            *[pltpu.VMEM((shape[0], 2, *shape[1:]), f32) for shape in shapes],
            pltpu.VMEM((LANES, width), f32),
            pltpu.VMEM((8, width), f32),
            pltpu.VMEM((16, local * owners * capp), bf16),
            *weight_scratch(packed),
            pltpu.VMEM((LANES, width), bf16),
            pltpu.SemaphoreType.DMA((4,)),
        ],
        compiler_params=params(58),
        cost_estimate=pl.CostEstimate(
            flops=40_000_000_000, bytes_accessed=40_000_000, transcendentals=2_000_000
        ),
        name="attention_backward",
    )(
        core,
        tokens,
        cot,
        cols,
        qkv,
        mixed,
        lse,
        first,
        routed,
        gates,
        *packed[0],
        *packed[1],
        *slots,
    )


def output_kernel(labels, local, first_ref, cols_ref, gates_ref, slots_ref, out_ref):
    _, length, width = first_ref.shape
    owners, capp, _ = slots_ref.shape
    capp = capp // local
    span = owners * capp
    label = iota((length, labels), 1)
    total = first_ref[0]
    for k in range(2):
        picked = None
        for l in range(local):
            lane = iota((length, span), 1) + l * span
            hot = jnp.where(lane == cols_ref[0, :, k : k + 1], 1.0, 0.0).astype(bf16)
            part = dot(hot, slots_ref[:, l * capp : (l + 1) * capp, :].reshape(span, width))
            picked = part if picked is None else picked + part
        chosen = jnp.where(label == cols_ref[0, :, k + 2 : k + 3], gates_ref[0], 0.0)
        total = total + jnp.sum(chosen, axis=1, keepdims=True) * picked
    out_ref[0] = total.astype(bf16)


def combine(first, cols, gates, slots, local):
    images, length, width = first.shape
    labels = gates.shape[2]
    whole = lambda *tail: pl.BlockSpec((1, *tail), lambda i: (i, 0, 0))
    return pl.pallas_call(
        functools.partial(output_kernel, labels, local),
        grid=(images,),
        in_specs=[
            whole(length, width),
            whole(length, 8),
            whole(length, labels),
            pl.BlockSpec(slots.shape, lambda i: (0, 0, 0)),
        ],
        out_specs=whole(length, width),
        out_shape=jax.ShapeDtypeStruct((images, length, width), bf16),
        compiler_params=params(40),
        name="combine_outputs",
    )(first, cols, gates, slots)


def bits_of(groups, owners):
    outer = [("group", k) for k in reversed(range(1, groups.bit_length() - 1))]
    inner = [("expert", k) for k in reversed(range(owners.bit_length() - 1))]
    return outer, inner


def swap(block, hop, sizes):
    axis, bit = hop
    return lax.ppermute(block, axis, [(d, d ^ (1 << bit)) for d in range(sizes[axis])])


def own_bit(hop):
    return lax.rem(lax.axis_index(hop[0]) >> hop[1], 2)


def spread(block, have, hops, order, sizes):
    for hop in hops:
        other = swap(block, hop, sizes)
        have = sorted([*have, hop], key=order.index)
        at = have.index(hop)
        mine = own_bit(hop) == 0
        block = jnp.stack(
            [jnp.where(mine, block, other), jnp.where(mine, other, block)], axis=at
        )
    return block, have


def gather_back(total, hops, order, sizes):
    have = list(order)
    for hop in hops:
        at = have.index(hop)
        have.remove(hop)
        bit = own_bit(hop)
        away = lax.dynamic_index_in_dim(total, 1 - bit, at, keepdims=False)
        stay = lax.dynamic_index_in_dim(total, bit, at, keepdims=False)
        total = stay + swap(away.astype(bf16), hop, sizes).astype(f32)
    return total


def per_device(
    groups,
    owners,
    tokens,
    cotangent,
    routes,
    order,
    ln1_gain,
    ln1_bias,
    w_qkv,
    w_out,
    b_out,
    ln2_gain,
    ln2_bias,
    w_router,
    w_in,
    b_in,
    w_back,
    b_back,
):
    images, length, width = tokens.shape
    tok_count = images * length
    labels = w_router.shape[1]
    local = labels // owners
    depth = w_in.shape[1]
    hidden = w_back.shape[1]
    cap = max(2, 5 * tok_count // (2 * labels))
    capp = -(-(cap + 3) // 16) * 16

    own = width // (groups * owners)
    sizes = {"group": groups, "expert": owners}
    outer, inner = bits_of(groups, owners)
    order_of_hops = [*outer, *inner]
    sibling = ("group", 0)
    core = own_bit(sibling).astype(jnp.int32).reshape(1)
    routes_one = [*inner, *outer]
    routes_two = [*inner[:-1], *outer, *inner[-1:]]
    router = w_router.reshape(own, owners, local).swapaxes(1, 2).reshape(own, labels)
    vectors = jnp.stack([ln1_gain, ln1_bias, b_out, ln2_gain, ln2_bias], axis=1)
    blank = jnp.zeros((own, LANES - labels - VECTORS), f32)
    slices = [
        w_qkv[:, : 2 * width].astype(bf16),
        jnp.concatenate([w_qkv[:, 2 * width :], w_out, router, vectors, blank], axis=1).astype(bf16),
    ]
    near = inner[:-1]
    slices = [spread(block, [], near, order_of_hops, sizes) for block in slices]

    marks = (routes % local) * owners + routes // local
    marks = marks.swapaxes(1, 2)
    rows, cols = route(marks, order, labels, cap, capp)
    cots = dispatch(rows, cotangent, None, cap, capp, owners, local)[0]
    exchange = lambda block: lax.all_to_all(block, "expert", 0, 0, tiled=True)
    cots, one, two = lax.optimization_barrier((cots, slices[0][0], slices[1][0]))
    cots = exchange(cots)
    packed = []
    for block, (_, have), path in ((one, slices[0], routes_one), (two, slices[1], routes_two)):
        half, _ = spread(block, have, path[len(near) :], order_of_hops, sizes)
        half = half.reshape(groups // 2, owners * own, block.shape[-1])
        packed.append((half, swap(half, sibling, sizes)))

    biases = jnp.zeros((local, 16, width), f32)
    biases = biases.at[:, 0, :hidden].set(b_in).at[:, 1, :depth].set(b_back)
    wback = jnp.concatenate([w_back, biases], axis=1).astype(bf16)
    win = lax.all_gather(w_in.astype(bf16), "group")
    wback = lax.all_gather(wback, "group")

    qkv, mixed, lse, first, routed, gates, gate_rows = forward(core, tokens, marks, packed, labels)
    sent = dispatch(rows, routed, gate_rows, cap, capp, owners, local)
    cots, *sent = lax.optimization_barrier((cots, *sent))
    sent = [exchange(block) for block in sent]
    outcomes, backs, share_in, share_back = [], [], [], []
    for l in range(local):
        bias = wback[:, l, hidden + 1, :depth].reshape(1, width)
        outcome, back, grad_in, grad_back = expert(sent[l], cots, win, wback, bias, l, cap)
        if l + 1 < local:
            back, sent[l + 1] = lax.optimization_barrier((back, sent[l + 1]))
        if l:
            back, backs[-1] = lax.optimization_barrier((back, backs[-1]))
        backs.append(exchange(back))
        outcomes.append(outcome)
        share_in.append(lax.psum_scatter(grad_in, "group", scatter_dimension=0))
        share_back.append(lax.psum_scatter(grad_back, "group", scatter_dimension=0))
    joined = jnp.concatenate(outcomes, axis=1)
    joined, *backs = lax.optimization_barrier((joined, *backs))
    joined = exchange(joined)
    share_in = jnp.stack(share_in).astype(f32)
    share_back = jnp.stack(share_back).astype(f32)
    grad_tokens, *halves = backward(
        core,
        tokens,
        cotangent,
        cols,
        qkv,
        mixed,
        lse,
        first,
        routed,
        gates,
        cap,
        packed,
        backs,
        labels,
    )
    output = combine(first, cols, gates, joined, local)
    sums = []
    for keep, away, path in (
        (halves[0], halves[1], routes_one[::-1]),
        (halves[2], halves[3], routes_two[::-1]),
    ):
        total = keep + swap(away, sibling, sizes).astype(f32)
        total = total.reshape(*[2] * len(order_of_hops), own, keep.shape[2])
        first_hops = path[: len(path) - len(near)]
        sums.append(gather_back(total, first_hops, order_of_hops, sizes))
    one, two, output = lax.optimization_barrier((*sums, output))
    rest = [hop for hop in order_of_hops if hop in near]
    sums = [gather_back(part, near[::-1], rest, sizes) for part in (one, two)]
    one, two = sums
    small = two[:, 2 * width :]
    grad_router = small[:, :labels].reshape(own, local, owners).swapaxes(1, 2).reshape(own, labels)
    place = lax.axis_index("group") * depth
    return (
        output,
        grad_tokens,
        small[:, labels],
        small[:, labels + 1],
        jnp.concatenate([one, two[:, :width]], axis=1),
        two[:, width : 2 * width],
        small[:, labels + 2],
        small[:, labels + 3],
        small[:, labels + 4],
        grad_router,
        share_in,
        share_back[:, hidden, :hidden],
        share_back[:, :hidden],
        lax.dynamic_slice_in_dim(share_back[:, hidden + 1], place, depth, axis=1),
    )


def solution(mesh):
    rows = P(BOTH, None)
    line = P(BOTH)
    tall = P(BOTH, None, None)
    deep = P("expert", "group", None)
    flat = P("expert", "group")
    groups, owners = mesh.shape["group"], mesh.shape["expert"]
    return jax.shard_map(
        functools.partial(per_device, groups, owners),
        mesh=mesh,
        in_specs=(
            tall,
            tall,
            tall,
            rows,
            line,
            line,
            rows,
            rows,
            line,
            line,
            line,
            rows,
            deep,
            flat,
            deep,
            flat,
        ),
        out_specs=(
            tall,
            tall,
            line,
            line,
            rows,
            rows,
            line,
            line,
            line,
            rows,
            deep,
            flat,
            deep,
            flat,
        ),
        check_vma=False,
    )
```

time: 1030 us -> 540 us (0.52)
  local copies, waits for them, and re-layouts: 256 us -> 32 us
  matrix products: 177 us -> 0 us
  Pallas kernels: 0 us -> 160 us
  waiting for transfers between devices: 300 us -> 174 us
  blocking collectives: 170 us -> 85.2 us
  other arithmetic: 89.3 us -> 24.3 us
  starting transfers between devices: 17.7 us -> 42.3 us
    all_to_all x4, waiting for transfers between devices: 211 us -> 31.8 us  [per_device(): exchange = lambda block: lax.all_to_all(block, 'expert', 0, 0, tiled=True)]
    dot_general x21 -> x0, matrix products: 177 us -> none  [the longest x1 30.8 us: per_device(): jnp.einsum('lrd,lhd->lrh', grad_arrived, second_w, preferred_element_type...]
    pallas_call x0 -> x8, Pallas kernels: none -> 160 us  [the longest x2 78.7 us: expert(): pl.pallas_call(functools.partial(expert_kernel, cap), grid=(groups,), in_...]
    ppermute x0 -> x20, waiting for transfers between devices: none -> 130 us  [swap(): lax.ppermute(block, axis, [(d, d ^ 1 << bit) for d in range(sizes[axis])])]
    all_gather x3 -> x0, blocking collectives: 88.9 us -> none  [the longest x1 78.7 us: per_device(): lax.all_gather(w_router.astype(jnp.bfloat16), ('group', 'expert'), axis=0...]
    all_to_all x0 -> x2, blocking collectives: none -> 85.2 us  [per_device(): exchange = lambda block: lax.all_to_all(block, 'expert', 0, 0, tiled=True)]
    unnamed x2 -> x0, blocking collectives: 81.4 us -> none
    gather x12 -> x0, local copies, waits for them, and re-layouts: 78.3 us -> none  [the longest x5 36.3 us: pick_rows(): return padded[slot_index]]
  transfers between devices with their start and end apart: 14 -> 30, of which waited for: 5 -> 15; matrix products, arithmetic and copies ran while one was open for 49% -> 6% of each run, Pallas kernels for 0% -> 21%
where the time goes in v1:
time: 540 us; the launch traced here: 533 us
  waiting for transfers between devices  174 us (32%)
  Pallas kernels  160 us (30%)
  blocking collectives  85.2 us (16%)
  starting transfers between devices  42.3 us (8%)
  local copies, waits for them, and re-layouts  32 us (6%)
  other arithmetic  24.3 us (4%)
  between operations  15.3 us (3%)
    ppermute x20, waiting for transfers between devices, swap(): lax.ppermute(block, axis, [(d, d ^ 1 << bit) for d in range(sizes[axis])])  130 us
    all_to_all x2, blocking collectives, per_device(): exchange = lambda block: lax.all_to_all(block, 'expert', 0, 0, tiled=True)  85.2 us
    pallas_call x2, Pallas kernels, expert(): pl.pallas_call(functools.partial(expert_kernel, cap), grid=(groups,), in_...  78.7 us
    pallas_call x1, Pallas kernels, backward(): pl.pallas_call(functools.partial(backward_kernel, labels, local, cap), gr...  43.1 us
    all_to_all x4, waiting for transfers between devices, per_device(): exchange = lambda block: lax.all_to_all(block, 'expert', 0, 0, tiled=True)  31.8 us
    ppermute x20, starting transfers between devices, swap(): lax.ppermute(block, axis, [(d, d ^ 1 << bit) for d in range(sizes[axis])])  25.3 us
    unnamed x75, local copies, waits for them, and re-layouts  22.1 us
    all_to_all x4, starting transfers between devices, per_device(): exchange = lambda block: lax.all_to_all(block, 'expert', 0, 0, tiled=True)  16.6 us
  transfers between devices with their start and end apart: 30, of which 15 were waited for; matrix products, arithmetic and copies ran while one was open for 6% of the time, Pallas kernels for 21%

profile of v1, /device:TPU:0, one launch (start us, length us, event | category | flops | bytes accessed | tf_op | source)
XLA Modules:
  0.0 532.7 jit_solution(15070944482629326274)
XLA Ops:
  18.2 4.1 collective-permute-start
  25.7 5.7 %fill_slots.2 = bf16[8,256,768]{2,1,0:T(8,128)(2,1)} custom-call(s32[4,8,197]{2,1,0:T(8,128)S(1)} %get-tuple-element.79.rows_ref, bf16[4,197,768]{2,1,0:T(8,128)(2,1)S(1)} %copy.107.value_ref.cot_ref), custom_call_target="tpu_custom_call" | custom-call | tf_op jit(solution)/shard_map/fill_slots/pallas_call | solution.py:188
  33.7 4.6 collective-permute-done.1
  43.5 5.5 %all-to-all-start = ((bf16[8,256,768]{2,1,0:T(8,128)(2,1)}), bf16[8,256,768]{2,1,0:T(8,128)(2,1)}, u32[]{:S(2)}, u32[]{:S(2)}) async-start(bf16[8,256,768]{2,1,0:T(8,128)(2,1)} %fill_slots.2), calls=%async_computation | async-start | bytes 6291456 | tf_op jit(solution)/shard_map/all_to_all | solution.py:831
  49.7 9.5 %collective-permute-done.7 = bf16[2,2,24,1664]{3,2,0,1:T(8,128)(2,1)S(1)} collective-permute-done((bf16[2,2,24,1664]{3,2,0,1:T(8,128)(2,1)S(1)}, bf16[2,2,24,1664]{3,2,0,1:T(8,128)(2,1)S(1)}, u32[]{:S(2)}, u32[]{:S(2)}) %collective-permute-start.7) | collective-permute-done | bytes 319520 | tf_op jit(solution)/shard_map/ppermute | solution.py:749
  59.9 23.7 %collective-permute-done.5 = bf16[2,2,2,24,1536]{4,3,0,1,2:T(8,128)(2,1)S(1)} collective-permute-done((bf16[2,2,2,24,1536]{4,3,0,1,2:T(8,128)(2,1)S(1)}, bf16[2,2,2,24,1536]{4,3,0,1,2:T(8,128)(2,1)S(1)}, u32[]{:S(2)}, u32[]{:S(2)}) %collective-permute-start.5) | collective-permute-done | bytes 589856 | tf_op jit(solution)/shard_map/ppermute | solution.py:749
  83.7 11.9 %collective-permute-done.8 = bf16[2,2,2,24,1664]{4,3,1,2,0:T(8,128)(2,1)S(1)} collective-permute-done((bf16[2,2,2,24,1664]{4,3,1,2,0:T(8,128)(2,1)S(1)}, bf16[2,2,2,24,1664]{4,3,1,2,0:T(8,128)(2,1)S(1)}, u32[]{:S(2)}, u32[]{:S(2)}) %collective-permute-start.8) | collective-permute-done | bytes 639008 | tf_op jit(solution)/shard_map/ppermute | solution.py:749
  100.9 16.4 %attention_forward.1 = (bf16[4,197,2304]{2,1,0:T(8,128)(2,1)}, bf16[4,197,768]{2,1,0:T(8,128)(2,1)S(1)}, f32[4,16,256]{2,1,0:T(8,128)S(1)}, f32[4,197,768]{2,1,0...) custom-call(s32[1]{0:T(128)} %bitcast.core_ref, ...), custom_call_target="tpu_custom_call" | custom-call | flops 16000000000 | bytes 20000000 | tf_op jit(solution)/shard_map/attention_forward/pallas_call | solution.py:297
  121.2 7.1 %fill_slots.3 = (bf16[8,128,768]{2,1,0:T(8,128)(2,1)S(1)}, bf16[8,128,768]{2,1,0:T(8,128)(2,1)}) custom-call(s32[4,8,197]{2,1,0:T(8,128)S(1)} %get-tuple-element.79.rows_ref, bf16[4,197,768]{2,1,0:T(8,128)(2,1)S(1)} %get-tuple-element.86.value_ref.routed_ref, bf16[4,16,197]{2,1,0:T(8,128)(2,1)S(1)} %get-tuple-element.89.refs_0_), custom_call_target="tpu_custom_call" | custom-call | tf_op jit(solution)/shard_map/fill_slots/pallas_call | solution.py:188
  129.4 43.2 %all_to_all.30.rows_ref = bf16[8,128,768]{2,1,0:T(8,128)(2,1)} all-to-all(bf16[8,128,768]{2,1,0:T(8,128)(2,1)S(1)} %get-tuple-element.92), channel_id=1, replica_groups=mesh['group'=4,'expert'=8] {'expert'}, dimensions={0} | all-to-all | bytes 3145728 | tf_op jit(solution)/shard_map/all_to_all | solution.py:831
  177.9 39.2 %expert_rows.2 = (bf16[8,128,768]{2,1,0:T(8,128)(2,1)}, bf16[8,128,768]{2,1,0:T(8,128)(2,1)}, bf16[4,192,3072]{2,1,0:T(8,128)(2,1)}, bf16[4,784,768]{2,1,0:T(8,128)(2,1)}) custom-call(bf16[8,128,768]{2,1,0:T(8,128)(2,1)} %all_to_all.30.rows_ref, bf16[8,256,768]{2,1,0:T(8,128)(2,1)} %all-to-all-done.cot_ref, bf16[4,2,192,3072]{3,2,1,0:T(8,128)(2,1)} %bitcast.128, ...), custom_call_target="tpu_custom_call" | custom-call | flops 28991029248 | bytes 30000000 | tf_op jit(solution)/shard_map/expert_rows/pallas_call | solution.py:436
  218.3 39.5 %expert_rows.3 = (bf16[8,128,768]{2,1,0:T(8,128)(2,1)}, bf16[8,128,768]{2,1,0:T(8,128)(2,1)}, bf16[4,192,3072]{2,1,0:T(8,128)(2,1)}, bf16[4,784,768]{2,1,0:T(8,128)(2,1)}) custom-call(bf16[8,128,768]{2,1,0:T(8,128)(2,1)} %copy-done.22, bf16[8,256,768]{2,1,0:T(8,128)(2,1)} %all-to-all-done.cot_ref, bf16[4,2,192,3072]{3,2,1,0:T(8,128)(2,1)} %bitcast.129, ...), custom_call_target="tpu_custom_call" | custom-call | flops 28991029248 | bytes 30000000 | tf_op jit(solution)/shard_map/expert_rows/pallas_call | solution.py:436
  259.8 42.0 %all_to_all.31.refs_0_ = bf16[8,128,768]{2,1,0:T(8,128)(2,1)} all-to-all(bf16[8,128,768]{2,1,0:T(8,128)(2,1)S(1)} %copy-done.20), channel_id=1, replica_groups=mesh['group'=4,'expert'=8] {'expert'}, dimensions={0} | all-to-all | bytes 3145728 | tf_op jit(solution)/shard_map/all_to_all | solution.py:831
  310.1 31.7 %all-to-all-done.4.refs_1_ = bf16[8,128,768]{2,1,0:T(8,128)(2,1)S(1)} async-done(((bf16[8,128,768]{2,1,0:T(8,128)(2,1)}), bf16[8,128,768]{2,1,0:T(8,128)(2,1)S(1)}, u32[]{:S(2)}, u32[]{:S(2)}) %all-to-all-start.4) | async-done | bytes 1572896 | tf_op jit(solution)/shard_map/all_to_all | solution.py:831
  343.0 43.1 %attention_backward.1 = (f32[4,197,768]{2,1,0:T(8,128)}, f32[2,192,1536]{2,1,0:T(8,128)}, bf16[2,192,1536]{2,1,0:T(8,128)(2,1)}, f32[2,192,1664]{2,1,0:T(8,128)}, bf16[2,192,1664]{2,1,0:T(8,128)(2,1)}) custom-call(s32[1]{0:T(128)} %bitcast.core_ref, bf16[4,197,768]{2,1,0:T(8,128)(2,1)} %copy-done.5, bf16[4,197,768]{2,1,0:T(8,128)(2,1)} %copy-done, ...), custom_call_target="tpu_custom_call" | custom-call | flops 40000000000 | bytes 40000000 | tf_op jit(solution)/shard_map/attention_backward/pallas_call | solution.py:646
  390.7 4.2 copy.116
  401.8 18.2 %collective-permute-done.11 = bf16[2,2,2,24,1536]{4,3,0,1,2:T(8,128)(2,1)S(1)} collective-permute-done((bf16[2,2,2,24,1536]{4,3,0,1,2:T(8,128)(2,1)S(1)}, bf16[2,2,2,24,1536]{4,3,0,1,2:T(8,128)(2,1)S(1)}, u32[]{:S(2)}, u32[]{:S(2)}) %collective-permute-start.11) | collective-permute-done | bytes 589856 | tf_op jit(solution)/shard_map/ppermute | solution.py:749
  421.6 19.8 %collective-permute-done.14 = bf16[2,2,2,24,1664]{4,3,2,1,0:T(8,128)(2,1)S(1)} collective-permute-done((bf16[2,2,2,24,1664]{4,3,2,1,0:T(8,128)(2,1)S(1)}, bf16[2,2,2,24,1664]{4,3,2,1,0:T(8,128)(2,1)S(1)}, u32[]{:S(2)}, u32[]{:S(2)}) %collective-permute-start.14) | collective-permute-done | bytes 639008 | tf_op jit(solution)/shard_map/ppermute | solution.py:749
  448.1 10.1 %collective-permute-done.15 = bf16[2,2,24,1664]{3,2,1,0:T(8,128)(2,1)S(1)} collective-permute-done((bf16[2,2,24,1664]{3,2,1,0:T(8,128)(2,1)S(1)}, bf16[2,2,24,1664]{3,2,1,0:T(8,128)(2,1)S(1)}, u32[]{:S(2)}, u32[]{:S(2)}) %collective-permute-start.15) | collective-permute-done | bytes 319520 | tf_op jit(solution)/shard_map/ppermute | solution.py:749
  459.1 4.1 maximum_convert_fusion.1
  463.2 10.9 %reduce-scatter.9.cloned.1.call-done = bf16[1,784,768]{2,1,0:T(8,128)(2,1)} async-done(((bf16[4,784,768]{2,1,0:T(8,128)(2,1)}), bf16[1,784,768]{2,1,0:T(8,128)(2,1)}) %reduce-scatter.9.cloned.1.call-update) | async-done | bytes 1204240 | tf_op jit(solution)/shard_map/reduce_scatter | solution.py:861
  482.3 6.3 %combine_outputs.1 = bf16[4,197,768]{2,1,0:T(8,128)(2,1)S(1)} custom-call(f32[4,197,768]{2,1,0:T(8,128)S(1)} %copy-done.2, s32[4,197,8]{2,1,0:T(8,128)S(1)} %copy-done.8, f32[4,197,16]{2,1,0:T(8,128)S(1)} %copy-done.10, bf16[8,256,768]{2,1,0:T(8,128)(2,1)S(1)} %all-to-all-done.5.slots_ref), custom_call_target="tpu_custom_call" | custom-call | tf_op jit(solution)/shard_map/combine_outputs/pallas_call | solution.py:725
  493.4 4.6 collective-permute-done.18
  504.2 18.3 %collective-permute-done.17 = bf16[24,1664]{0,1:T(8,128)(2,1)S(1)} collective-permute-done((bf16[24,1664]{0,1:T(8,128)(2,1)S(1)}, bf16[24,1664]{0,1:T(8,128)(2,1)S(1)}, u32[]{:S(2)}, u32[]{:S(2)}) %collective-permute-start.17) | collective-permute-done | bytes 79904 | tf_op jit(solution)/shard_map/ppermute | solution.py:749
  (209 shorter events, 93.6 us)
Async XLA Ops:
  7.2 169.2 %all-gather.4.cloned.1.call-start = ((), (), s32[]{:S(2)}) async-start(), calls=%async_computation.10 | async-start | bytes 12042240 | tf_op jit(solution)/shard_map/all_gather | solution.py:844
  13.1 164.8 %all-gather.6.cloned.1.call-start = ((), (), s32[]{:S(2)}) async-start(), calls=%async_computation.15 | async-start | bytes 11796480 | tf_op jit(solution)/shard_map/all_gather | solution.py:843
  18.2 13.3 %collective-permute-start = (bf16[24,1536]{1,0:T(8,128)(2,1)S(1)}, bf16[24,1536]{1,0:T(8,128)(2,1)S(1)}, u32[]{:S(2)}, u32[]{:S(2)}) collective-permute-start(bf16[24,1536]{1,0:T(8,128)(2,1)S(1)} %slice.114), channel_id=1, source_target_pairs={{0,4},{1,5},{2,6},{3,7},{4,0},{5,1},{6,2},{7,3},{8,12},{9,13},{10,... | collective-permute-start | bytes 221192 | tf_op jit(solution)/shard_map/ppermute | solution.py:749
  23.0 10.4 %collective-permute-start.2 = (bf16[24,1664]{1,0:T(8,128)(2,1)S(1)}, bf16[24,1664]{1,0:T(8,128)(2,1)S(1)}, u32[]{:S(2)}, u32[]{:S(2)}) collective-permute-start(bf16[24,1664]{1,0:T(8,128)(2,1)S(1)} %concatenate.33), channel_id=1, source_target_pairs={{0,4},{1,5},{2,6},{3,7},{4,0},{5,1},{6,2},{7,3},{8,12},{9,13},{10,... | collective-permute-start | bytes 239624 | tf_op jit(solution)/shard_map/ppermute | solution.py:749
  40.4 8.6 %collective-permute-start.4 = (bf16[2,2,24,1536]{3,2,0,1:T(8,128)(2,1)S(1)}, bf16[2,2,24,1536]{3,2,0,1:T(8,128)(2,1)S(1)}, u32[]{:S(2)}, u32[]{:S(2)}) collective-permute-start(bf16[2,2,24,1536]{3,2,0,1:T(8,128)(2,1)S(1)} %pad_maximum_fusion.7), channel_id=1, source_target_pairs={{0,1},{1,0},{2,3},{3,2},{4,5},{5,4},{6,7},{7,6},{8,9},{9,8},{10,11... | collective-permute-start | bytes 884744 | tf_op jit(solution)/shard_map/ppermute | solution.py:749
  42.0 17.2 %collective-permute-start.7 = (bf16[2,2,24,1664]{3,2,0,1:T(8,128)(2,1)S(1)}, bf16[2,2,24,1664]{3,2,0,1:T(8,128)(2,1)S(1)}, u32[]{:S(2)}, u32[]{:S(2)}) collective-permute-start(bf16[2,2,24,1664]{3,2,0,1:T(8,128)(2,1)S(1)} %pad_maximum_fusion.6), channel_id=1, source_target_pairs={{0,16},{8,24},{16,0},{24,8},{1,17},{9,25},{17,1},{25,9},{2,18},{10... | collective-permute-start | bytes 958472 | tf_op jit(solution)/shard_map/ppermute | solution.py:749
  43.5 85.9 %all-to-all-start = ((bf16[8,256,768]{2,1,0:T(8,128)(2,1)}), bf16[8,256,768]{2,1,0:T(8,128)(2,1)}, u32[]{:S(2)}, u32[]{:S(2)}) async-start(bf16[8,256,768]{2,1,0:T(8,128)(2,1)} %fill_slots.2), calls=%async_computation | async-start | bytes 6291456 | tf_op jit(solution)/shard_map/all_to_all | solution.py:831
  49.1 34.5 %collective-permute-start.5 = (bf16[2,2,2,24,1536]{4,3,0,1,2:T(8,128)(2,1)S(1)}, bf16[2,2,2,24,1536]{4,3,0,1,2:T(8,128)(2,1)S(1)}, u32[]{:S(2)}, u32[]{:S(2)}) collective-permute-start(bf16[2,2,2,24,1536]{4,3,0,1,2:T(8,128)(2,1)S(1)} %pad_maximum_fusion.5), channel_id=1, source_target_pairs={{0,16},{8,24},{16,0},{24,8},{1,17},{9,25},{17,1},{25,9},{2,18},{10... | collective-permute-start | bytes 1769480 | tf_op jit(solution)/shard_map/ppermute | solution.py:749
  59.3 36.3 %collective-permute-start.8 = (bf16[2,2,2,24,1664]{4,3,1,2,0:T(8,128)(2,1)S(1)}, bf16[2,2,2,24,1664]{4,3,1,2,0:T(8,128)(2,1)S(1)}, u32[]{:S(2)}, u32[]{:S(2)}) collective-permute-start(bf16[2,2,2,24,1664]{4,3,1,2,0:T(8,128)(2,1)S(1)} %pad_maximum_fusion.4), channel_id=1, source_target_pairs={{0,1},{1,0},{2,3},{3,2},{4,5},{5,4},{6,7},{7,6},{8,9},{9,8},{10,11... | collective-permute-start | bytes 1916936 | tf_op jit(solution)/shard_map/ppermute | solution.py:749
  172.5 44.6 %all-to-all-start.2 = ((bf16[8,128,768]{2,1,0:T(8,128)(2,1)}), bf16[8,128,768]{2,1,0:T(8,128)(2,1)S(1)}, u32[]{:S(2)}, u32[]{:S(2)}) async-start(bf16[8,128,768]{2,1,0:T(8,128)(2,1)} %get-tuple-element.96), calls=%async_computation.2 | async-start | bytes 3145728 | tf_op jit(solution)/shard_map/all_to_all | solution.py:831
  176.2 282.9 %reduce-scatter.7.cloned.1.call-start = ((), (), s32[]{:S(2)}) async-start(), calls=%async_computation.12 | async-start | bytes 5898240 | tf_op jit(solution)/shard_map/reduce_scatter | solution.py:860
  257.8 201.3 %reduce-scatter.5.cloned.1.call-start = ((), (), s32[]{:S(2)}) async-start(), calls=%async_computation.11 | async-start | bytes 5898240 | tf_op jit(solution)/shard_map/reduce_scatter | solution.py:860
  258.3 204.9 %reduce-scatter.11.cloned.1.call-start = ((), (), s32[]{:S(2)}) async-start(), calls=%async_computation.14 | async-start | bytes 6021120 | tf_op jit(solution)/shard_map/reduce_scatter | solution.py:861
  301.8 40.1 %all-to-all-start.4 = ((bf16[8,128,768]{2,1,0:T(8,128)(2,1)}), bf16[8,128,768]{2,1,0:T(8,128)(2,1)S(1)}, u32[]{:S(2)}, u32[]{:S(2)}) async-start(bf16[8,128,768]{2,1,0:T(8,128)(2,1)} %get-tuple-element.102), calls=%async_computation.4 | async-start | bytes 3145728 | tf_op jit(solution)/shard_map/all_to_all | solution.py:831
  305.4 168.8 %reduce-scatter.9.cloned.1.call-start = ((), (), s32[]{:S(2)}) async-start(), calls=%async_computation.13 | async-start | bytes 6021120 | tf_op jit(solution)/shard_map/reduce_scatter | solution.py:861
  386.1 8.8 %collective-permute-start.10 = (bf16[2,192,1536]{2,1,0:T(8,128)(2,1)}, bf16[2,192,1536]{2,1,0:T(8,128)(2,1)}, u32[]{:S(2)}, u32[]{:S(2)}) collective-permute-start(bf16[2,192,1536]{2,1,0:T(8,128)(2,1)} %get-tuple-element.106), channel_id=1, source_target_pairs={{0,8},{8,0},{16,24},{24,16},{1,9},{9,1},{17,25},{25,17},{2,10},{10... | collective-permute-start | bytes 3538952 | tf_op jit(solution)/shard_map/ppermute | solution.py:749
  386.2 11.9 %collective-permute-start.13 = (bf16[2,192,1664]{2,1,0:T(8,128)(2,1)}, bf16[2,192,1664]{2,1,0:T(8,128)(2,1)}, u32[]{:S(2)}, u32[]{:S(2)}) collective-permute-start(bf16[2,192,1664]{2,1,0:T(8,128)(2,1)} %get-tuple-element.108), channel_id=1, source_target_pairs={{0,8},{8,0},{16,24},{24,16},{1,9},{9,1},{17,25},{25,17},{2,10},{10... | collective-permute-start | bytes 3833864 | tf_op jit(solution)/shard_map/ppermute | solution.py:749
  386.7 92.6 %all-to-all-start.5 = ((bf16[8,256,768]{2,1,0:T(8,128)(2,1)}), bf16[8,256,768]{2,1,0:T(8,128)(2,1)S(1)}, u32[]{:S(2)}, u32[]{:S(2)}) async-start(bf16[8,256,768]{2,1,0:T(8,128)(2,1)} %pad_maximum_fusion), calls=%async_computation.5 | async-start | bytes 6291456 | tf_op jit(solution)/shard_map/all_to_all | solution.py:831
  396.8 23.1 %collective-permute-start.11 = (bf16[2,2,2,24,1536]{4,3,0,1,2:T(8,128)(2,1)S(1)}, bf16[2,2,2,24,1536]{4,3,0,1,2:T(8,128)(2,1)S(1)}, u32[]{:S(2)}, u32[]{:S(2)}) collective-permute-start(bf16[2,2,2,24,1536]{4,3,0,1,2:T(8,128)(2,1)S(1)} %fusion.1), channel_id=1, source_target_pairs={{0,16},{8,24},{16,0},{24,8},{1,17},{9,25},{17,1},{25,9},{2,18},{10... | collective-permute-start | bytes 1769480 | tf_op jit(solution)/shard_map/ppermute | solution.py:749
  399.7 41.7 %collective-permute-start.14 = (bf16[2,2,2,24,1664]{4,3,2,1,0:T(8,128)(2,1)S(1)}, bf16[2,2,2,24,1664]{4,3,2,1,0:T(8,128)(2,1)S(1)}, u32[]{:S(2)}, u32[]{:S(2)}) collective-permute-start(bf16[2,2,2,24,1664]{4,3,2,1,0:T(8,128)(2,1)S(1)} %fusion), channel_id=1, source_target_pairs={{0,1},{1,0},{2,3},{3,2},{4,5},{5,4},{6,7},{7,6},{8,9},{9,8},{10,11... | collective-permute-start | bytes 1916936 | tf_op jit(solution)/shard_map/ppermute | solution.py:749
  420.1 27.0 %collective-permute-start.12 = (bf16[2,2,24,1536]{3,2,0,1:T(8,128)(2,1)S(1)}, bf16[2,2,24,1536]{3,2,0,1:T(8,128)(2,1)S(1)}, u32[]{:S(2)}, u32[]{:S(2)}) collective-permute-start(bf16[2,2,24,1536]{3,2,0,1:T(8,128)(2,1)S(1)} %fusion.4), channel_id=1, source_target_pairs={{0,1},{1,0},{2,3},{3,2},{4,5},{5,4},{6,7},{7,6},{8,9},{9,8},{10,11... | collective-permute-start | bytes 884744 | tf_op jit(solution)/shard_map/ppermute | solution.py:749
  441.6 16.6 %collective-permute-start.15 = (bf16[2,2,24,1664]{3,2,1,0:T(8,128)(2,1)S(1)}, bf16[2,2,24,1664]{3,2,1,0:T(8,128)(2,1)S(1)}, u32[]{:S(2)}, u32[]{:S(2)}) collective-permute-start(bf16[2,2,24,1664]{3,2,1,0:T(8,128)(2,1)S(1)} %fusion.3), channel_id=1, source_target_pairs={{0,16},{8,24},{16,0},{24,8},{1,17},{9,25},{17,1},{25,9},{2,18},{10... | collective-permute-start | bytes 958472 | tf_op jit(solution)/shard_map/ppermute | solution.py:749
  492.8 8.3 %collective-permute-start.16 = (bf16[2,24,1664]{2,1,0:T(8,128)(2,1)S(1)}, bf16[2,24,1664]{2,1,0:T(8,128)(2,1)S(1)}, u32[]{:S(2)}, u32[]{:S(2)}) collective-permute-start(bf16[2,24,1664]{2,1,0:T(8,128)(2,1)S(1)} %fusion.5), channel_id=1, source_target_pairs={{0,2},{1,3},{2,0},{3,1},{4,6},{5,7},{6,4},{7,5},{8,10},{9,11},{10,... | collective-permute-start | bytes 479240 | tf_op jit(solution)/shard_map/ppermute | solution.py:749
  501.7 20.8 %collective-permute-start.17 = (bf16[24,1664]{0,1:T(8,128)(2,1)S(1)}, bf16[24,1664]{0,1:T(8,128)(2,1)S(1)}, u32[]{:S(2)}, u32[]{:S(2)}) collective-permute-start(bf16[24,1664]{0,1:T(8,128)(2,1)S(1)} %fusion.2), channel_id=1, source_target_pairs={{0,4},{1,5},{2,6},{3,7},{4,0},{5,1},{6,2},{7,3},{8,12},{9,13},{10,... | collective-permute-start | bytes 239624 | tf_op jit(solution)/shard_map/ppermute | solution.py:749
  (40 other events, 176.9 us)
Sparse Core Ops, SparseCore 0:
  13.2 88.0 all-gather.3
  103.4 64.0 all-gather.5
  257.9 48.9 reduce-scatter.6
  310.0 47.8 reduce-scatter.4
  360.3 56.1 reduce-scatter.10
  419.0 55.0 reduce-scatter.8

commit v2 on v1

--- a/solution.py
+++ b/solution.py
@@ -70,6 +70,71 @@
             copy.start()
         for copy in copies:
             copy.wait()
+
+
+def pack_kernel(owners, qkv_ref, out_ref, router_ref, vec_ref, one_ref, two_ref):
+    own, width = out_ref.shape
+    labels = router_ref.shape[1]
+    local = labels // owners
+    one_ref[...] = qkv_ref[:, 0 : 2 * width].astype(bf16)
+    two_ref[:, 0:width] = qkv_ref[:, 2 * width :].astype(bf16)
+    two_ref[:, width : 2 * width] = out_ref[...].astype(bf16)
+    router = router_ref[...]
+    columns = [
+        router[:, o * local + l : o * local + l + 1] for l in range(local) for o in range(owners)
+    ]
+    vectors = jnp.concatenate([vec_ref[...], jnp.zeros((LANES - VECTORS, own), f32)], axis=0)
+    if own < LANES:
+        vectors = jnp.concatenate([vectors, jnp.zeros((LANES, LANES - own), f32)], axis=1)
+    vectors = jnp.transpose(vectors)[0:own, 0:VECTORS]
+    blank = jnp.zeros((own, LANES - labels - VECTORS), f32)
+    two_ref[:, 2 * width :] = jnp.concatenate([*columns, vectors, blank], axis=1).astype(bf16)
+
+
+def pack(w_qkv, w_out, w_router, vectors, owners):
+    own, width = w_out.shape
+    return pl.pallas_call(
+        functools.partial(pack_kernel, owners),
+        out_shape=[
+            jax.ShapeDtypeStruct((own, 2 * width), bf16),
+            jax.ShapeDtypeStruct((own, 2 * width + LANES), bf16),
+        ],
+        name="pack_weights",
+    )(w_qkv, w_out, w_router, vectors)
+
+
+def dense_out_kernel(owners, one_ref, one_in, two_ref, two_in, qkv_ref, out_ref, router_ref, vec_ref):
+    own, width = out_ref.shape
+    labels = router_ref.shape[1]
+    local = labels // owners
+    one = one_ref[...] + one_in[...].astype(f32)
+    two = two_ref[...] + two_in[...].astype(f32)
+    qkv_ref[:, 0 : 2 * width] = one
+    qkv_ref[:, 2 * width :] = two[:, 0:width]
+    out_ref[...] = two[:, width : 2 * width]
+    small = two[:, 2 * width :]
+    columns = [
+        small[:, l * owners + o : l * owners + o + 1] for o in range(owners) for l in range(local)
+    ]
+    router_ref[...] = jnp.concatenate(columns, axis=1)
+    if own < LANES:
+        small = jnp.concatenate([small, jnp.zeros((LANES - own, LANES), f32)], axis=0)
+    vec_ref[...] = jnp.transpose(small)[labels : labels + 8, 0:own]
+
+
+def dense_out(one, two, labels, owners):
+    own = one[0].shape[0]
+    width = one[0].shape[1] // 2
+    return pl.pallas_call(
+        functools.partial(dense_out_kernel, owners),
+        out_shape=[
+            jax.ShapeDtypeStruct((own, 3 * width), f32),
+            jax.ShapeDtypeStruct((own, width), f32),
+            jax.ShapeDtypeStruct((own, labels), f32),
+            jax.ShapeDtypeStruct((8, own), f32),
+        ],
+        name="dense_gradients",
+    )(*one, *two)
 
 
 def route_kernel(labels, cap, capp, routes_ref, order_ref, rows_ref, cols_ref):
@@ -143,11 +208,11 @@
     )(routes, order)
 
 
-def dispatch_kernel(cap, capp, owners, local, gated, joint, rows_ref, value_ref, *refs):
+def dispatch_kernel(cap, capp, owners, which, gated, joint, rows_ref, value_ref, *refs):
     images, length, width = value_ref.shape
     outs = refs[1:] if gated else refs
     span = owners * capp
-    for l in range(local):
+    for place, l in enumerate(which):
         slots = iota((span, length), 0) + l * span
         total = None
         gate_rows = None
@@ -166,27 +231,25 @@
         for o in range(owners):
             block = total[o * capp : (o + 1) * capp]
             if joint:
-                outs[0][o, l * capp : (l + 1) * capp, :] = block.astype(bf16)
+                outs[0][o, place * capp : (place + 1) * capp, :] = block.astype(bf16)
             else:
-                outs[l][o] = block.astype(bf16)
+                outs[0][o] = block.astype(bf16)
             if gated:
                 tail = block[capp - 16 :, 0:capp]
                 spare = gate_rows[:, o * capp : (o + 1) * capp]
                 line = iota((16, capp), 0) - (cap - (capp - 16))
                 for k in range(3):
                     tail = jnp.where(line == k, spare[k : k + 1], tail)
-                outs[l][o, capp - 16 :, 0:capp] = tail.astype(bf16)
-
-
-def dispatch(rows, values, gates, cap, capp, owners, local):
+                outs[0][o, capp - 16 :, 0:capp] = tail.astype(bf16)
+
+
+def dispatch(rows, values, gates, cap, capp, owners, which):
     width = values.shape[2]
     joint = gates is None
     operands = (rows, values) if joint else (rows, values, gates)
-    out_shape = [jax.ShapeDtypeStruct((owners, capp, width), bf16)] * local
-    if joint:
-        out_shape = [jax.ShapeDtypeStruct((owners, local * capp, width), bf16)]
+    out_shape = jax.ShapeDtypeStruct((owners, len(which) * capp, width), bf16)
     return pl.pallas_call(
-        functools.partial(dispatch_kernel, cap, capp, owners, local, not joint, joint),
+        functools.partial(dispatch_kernel, cap, capp, owners, tuple(which), not joint, joint),
         out_shape=out_shape,
         compiler_params=pltpu.CompilerParams(vmem_limit_bytes=40 * 1024 * 1024),
         name="fill_slots",
@@ -341,25 +404,51 @@
     cot_ref,
     win_ref,
     wback_ref,
-    bback_ref,
-    out_ref,
-    grad_ref,
-    gwin_ref,
-    gwback_ref,
-    turned_ref,
-    grad_out_ref,
-    out_acc_ref,
-    grad_acc_ref,
-    active_ref,
-    inner_ref,
-    bias_ref,
+    biases_ref,
+    *refs,
 ):
+    (
+        out_ref,
+        grad_ref,
+        weights_ref,
+        turned_ref,
+        grad_out_ref,
+        out_acc_ref,
+        grad_acc_ref,
+        active_ref,
+        inner_ref,
+        bias_ref,
+        gwin_ref,
+        gwback_ref,
+        gbias_ref,
+        sems,
+    ) = refs[-14:]
     owners, capp, width = rows_ref.shape
-    hidden = win_ref.shape[-1]
-    total = owners * capp
+    groups, depth, hidden = win_ref.shape
     spare = cap - (capp - 16)
     step = pl.program_id(0)
     last = pl.num_programs(0) - 1
+    slot = lax.rem(step, 2)
+    across = width // hidden
+
+    def copies(step, slot):
+        at = pl.multiple_of(hidden + lax.div(step, across) * depth, 16)
+        start = pl.multiple_of(lax.rem(step, across) * hidden, LANES)
+        return (
+            pltpu.make_async_copy(
+                gwback_ref.at[slot], weights_ref.at[step, pl.ds(0, hidden)], sems.at[0, slot]
+            ),
+            pltpu.make_async_copy(
+                gwin_ref.at[slot],
+                weights_ref.at[:, pl.ds(at, depth), pl.ds(start, hidden)],
+                sems.at[1, slot],
+            ),
+        )
+
+    @pl.when(step >= 2)
+    def _():
+        for copy in copies(step - 2, slot):
+            copy.wait()
 
     @pl.when(step == 0)
     def _():
@@ -379,8 +468,8 @@
         grad_acc_ref[...] = jnp.zeros_like(grad_acc_ref)
 
     first = win_ref[...].reshape(width, hidden)
-    second = wback_ref[0, 0, 0:hidden, :]
-    bias = wback_ref[0, 0, hidden : hidden + 16, :].astype(f32)[0:1, 0:hidden]
+    second = wback_ref[0]
+    bias = biases_ref[step].astype(f32)[0:1, 0:hidden]
     bias_sum = jnp.zeros((1, hidden), f32)
     per = max(1, 256 // capp)
     k0 = 0.7978845608028654
@@ -401,19 +490,28 @@
         inner_ref[at, :] = grad_low
         out_acc_ref[at, :] += dot(low, second)
         grad_acc_ref[at, :] += dot_nt(grad_low, first)
-    gwin_ref[...] = dot(turned_ref[...], inner_ref[...]).astype(bf16).reshape(gwin_ref.shape)
-    gwback_ref[0, 0:hidden, :] = dot_tn(active_ref[...], grad_out_ref[...]).astype(bf16)
+    gwin_ref[slot] = dot(turned_ref[...], inner_ref[...]).astype(bf16).reshape(win_ref.shape)
+    gwback_ref[slot] = dot_tn(active_ref[...], grad_out_ref[...]).astype(bf16)
     row = iota((16, width), 0)
     if hidden < width:
         bias_sum = jnp.concatenate([bias_sum, jnp.zeros((1, width - hidden), f32)], axis=1)
     pad = jnp.where(row == 0, bias_sum, jnp.where(row == 1, bias_ref[0:1, :], 0.0))
-    gwback_ref[0, hidden : hidden + 16, :] = pad.astype(bf16)
+    gbias_ref[step] = pad.astype(bf16)
+    for copy in copies(step, slot):
+        copy.start()
 
     @pl.when(step == last)
     def _():
+        end = pltpu.make_async_copy(
+            gbias_ref, weights_ref.at[:, pl.ds(weights_ref.shape[1] - 16, 16)], sems.at[2, 0]
+        )
+        end.start()
+        whole = jnp.concatenate(
+            [biases_ref[g].astype(f32)[1:2, 0:depth] for g in range(groups)], axis=1
+        )
         for b in range(owners):
             at = slice(b * capp, (b + 1) * capp)
-            result = (out_acc_ref[at, :] + bback_ref[...].astype(f32)).astype(bf16)
+            result = (out_acc_ref[at, :] + whole).astype(bf16)
             out_ref[b] = result
             score = jnp.sum(result.astype(f32) * cot_ref[b].astype(f32), axis=1, keepdims=True)
             score = jnp.transpose(jnp.broadcast_to(score, (capp, LANES)))[0:1, :]
@@ -424,37 +522,46 @@
             for k, part in enumerate(three_parts(score)):
                 tail = jnp.where(line == k, part, tail)
             grad_ref[b, capp - 16 :, 0:capp] = tail.astype(bf16)
-
-
-def expert(rows, cots, win, wback, bback, which, cap):
+        for back in range(2):
+            for copy in copies(step - back, lax.rem(step + back, 2)):
+                copy.wait()
+        end.wait()
+
+
+def expert(rows, cots, weights, outcomes, which, local, cap):
     owners, capp, width = rows.shape
-    groups, _, depth, wide = win.shape
-    hidden = wide // groups
+    groups, height, _ = weights.shape
+    depth = width // groups
+    hidden = height - 16 - (height - 16) // 2
+    across = width // hidden
     total = owners * capp
     full = lambda shape: pl.BlockSpec(shape, lambda j: (0,) * len(shape))
-    flops = 2 * 6 * total * width * wide
+    anywhere = pl.BlockSpec(memory_space=pl.ANY)
+    extra = [] if outcomes is None else [outcomes]
     return pl.pallas_call(
         functools.partial(expert_kernel, cap),
         grid=(groups,),
         in_specs=[
             full((owners, capp, width)),
+            full((owners, capp, width)),
+            pl.BlockSpec(
+                (groups, depth, hidden), lambda j: (0, hidden // depth + j // across, j % across)
+            ),
+            pl.BlockSpec((1, hidden, width), lambda j: (j, 0, 0)),
+            pl.BlockSpec((groups, 16, width), lambda j: (0, (height - 16) // 16, 0)),
+            *[anywhere] * len(extra),
+        ],
+        out_specs=[
             pl.BlockSpec((owners, capp, width), lambda j: (0, which, 0)),
-            pl.BlockSpec((groups, 1, depth, hidden), lambda j: (0, which, 0, j)),
-            pl.BlockSpec((1, 1, hidden + 16, width), lambda j: (j, which, 0, 0)),
-            full((1, width)),
-        ],
-        out_specs=[
             full((owners, capp, width)),
-            full((owners, capp, width)),
-            pl.BlockSpec((groups, depth, hidden), lambda j: (0, 0, j)),
-            pl.BlockSpec((1, hidden + 16, width), lambda j: (j, 0, 0)),
+            anywhere,
         ],
         out_shape=[
+            jax.ShapeDtypeStruct((owners, local * capp, width), bf16),
             jax.ShapeDtypeStruct((owners, capp, width), bf16),
-            jax.ShapeDtypeStruct((owners, capp, width), bf16),
-            jax.ShapeDtypeStruct((groups, depth, wide), bf16),
-            jax.ShapeDtypeStruct((groups, hidden + 16, width), bf16),
-        ],
+            jax.ShapeDtypeStruct(weights.shape, bf16),
+        ],
+        input_output_aliases={5: 0} if extra else {},
         scratch_shapes=[
             pltpu.VMEM((width, total), bf16),
             pltpu.VMEM((total, width), bf16),
@@ -463,13 +570,57 @@
             pltpu.VMEM((total, hidden), bf16),
             pltpu.VMEM((total, hidden), bf16),
             pltpu.VMEM((8, width), f32),
+            pltpu.VMEM((2, groups, depth, hidden), bf16),
+            pltpu.VMEM((2, hidden, width), bf16),
+            pltpu.VMEM((groups, 16, width), bf16),
+            pltpu.SemaphoreType.DMA((3, 2)),
         ],
         compiler_params=params(56),
         cost_estimate=pl.CostEstimate(
-            flops=flops, bytes_accessed=30_000_000, transcendentals=total * wide
+            flops=2 * 6 * total * width * hidden * groups,
+            bytes_accessed=30_000_000,
+            transcendentals=total * hidden * groups,
         ),
         name="expert_rows",
-    )(rows, cots, win, wback, bback)
+    )(rows, cots, weights, weights, weights, *extra)
+
+
+def share_kernel(*refs):
+    parts, (back_ref, in_ref, bias_ref) = refs[:3], refs[-3:]
+    value = [part[...] for part in parts]
+    back_ref[0] = value[0].astype(f32)
+    in_ref[0] = value[1].astype(f32)
+    bias_ref[0] = value[2].astype(f32)
+
+
+def share_out(share, outs, which, local, depth):
+    height, width = share.shape
+    hidden = (height - 16) // 2
+    steps = hidden // depth
+    extra = [] if outs is None else list(outs)
+    return pl.pallas_call(
+        share_kernel,
+        grid=(steps,),
+        in_specs=[
+            pl.BlockSpec((depth, width), lambda j: (j, 0)),
+            pl.BlockSpec((depth, width), lambda j: (steps + j, 0)),
+            pl.BlockSpec((16, width), lambda j: (2 * hidden // 16, 0)),
+            *[pl.BlockSpec(memory_space=pl.ANY)] * len(extra),
+        ],
+        out_specs=[
+            pl.BlockSpec((1, depth, width), lambda j: (which, j, 0)),
+            pl.BlockSpec((1, depth, width), lambda j: (which, 0, j)),
+            pl.BlockSpec((1, 16, width), lambda j: (which, 0, 0)),
+        ],
+        out_shape=[
+            jax.ShapeDtypeStruct((local, hidden, width), f32),
+            jax.ShapeDtypeStruct((local, depth, steps * width), f32),
+            jax.ShapeDtypeStruct((local, 16, width), f32),
+        ],
+        input_output_aliases={3 + k: k for k in range(len(extra))},
+        compiler_params=params(32),
+        name="expert_gradients",
+    )(share, share, share, *extra)
 
 
 def add_to(ref, columns, value):
@@ -628,8 +779,8 @@
         stack_ref[labels : labels + 8, :] = vec_ref[...]
         add_to(grad_two_ref, slice(2 * width, None), jnp.transpose(stack_ref[...]))
         mine, other = core_ref[0], 1 - core_ref[0]
-        keep_one_ref[...] = grad_one_ref[:, mine]
-        keep_two_ref[...] = grad_two_ref[:, mine]
+        keep_one_ref[...] = grad_one_ref[:, mine].astype(bf16)
+        keep_two_ref[...] = grad_two_ref[:, mine].astype(bf16)
         send_one_ref[...] = grad_one_ref[:, other].astype(bf16)
         send_two_ref[...] = grad_two_ref[:, other].astype(bf16)
 
@@ -666,7 +817,7 @@
         ],
         out_shape=[
             jax.ShapeDtypeStruct((images, length, width), f32),
-            *[jax.ShapeDtypeStruct(shape, kind) for shape in shapes for kind in (f32, bf16)],
+            *[jax.ShapeDtypeStruct(shape, bf16) for shape in shapes for _ in range(2)],
         ],
         scratch_shapes=[
             *[pltpu.VMEM((shape[0], 2, *shape[1:]), f32) for shape in shapes],
@@ -765,15 +916,20 @@
     return block, have
 
 
+def halve(total, hop, at, sizes):
+    bit = own_bit(hop)
+    away = lax.dynamic_index_in_dim(total, 1 - bit, at, keepdims=False)
+    stay = lax.dynamic_index_in_dim(total, bit, at, keepdims=False)
+    return stay, swap(away.astype(bf16), hop, sizes)
+
+
 def gather_back(total, hops, order, sizes):
     have = list(order)
     for hop in hops:
         at = have.index(hop)
         have.remove(hop)
-        bit = own_bit(hop)
-        away = lax.dynamic_index_in_dim(total, 1 - bit, at, keepdims=False)
-        stay = lax.dynamic_index_in_dim(total, bit, at, keepdims=False)
-        total = stay + swap(away.astype(bf16), hop, sizes).astype(f32)
+        stay, other = halve(total, hop, at, sizes)
+        total = stay + other.astype(f32)
     return total
 
 
@@ -814,56 +970,61 @@
     core = own_bit(sibling).astype(jnp.int32).reshape(1)
     routes_one = [*inner, *outer]
     routes_two = [*inner[:-1], *outer, *inner[-1:]]
-    router = w_router.reshape(own, owners, local).swapaxes(1, 2).reshape(own, labels)
-    vectors = jnp.stack([ln1_gain, ln1_bias, b_out, ln2_gain, ln2_bias], axis=1)
-    blank = jnp.zeros((own, LANES - labels - VECTORS), f32)
-    slices = [
-        w_qkv[:, : 2 * width].astype(bf16),
-        jnp.concatenate([w_qkv[:, 2 * width :], w_out, router, vectors, blank], axis=1).astype(bf16),
-    ]
+    vectors = jnp.stack([ln1_gain, ln1_bias, b_out, ln2_gain, ln2_bias])
+    slices = pack(w_qkv, w_out, w_router, vectors, owners)
     near = inner[:-1]
-    slices = [spread(block, [], near, order_of_hops, sizes) for block in slices]
-
     marks = (routes % local) * owners + routes // local
     marks = marks.swapaxes(1, 2)
     rows, cols = route(marks, order, labels, cap, capp)
-    cots = dispatch(rows, cotangent, None, cap, capp, owners, local)[0]
     exchange = lambda block: lax.all_to_all(block, "expert", 0, 0, tiled=True)
-    cots, one, two = lax.optimization_barrier((cots, slices[0][0], slices[1][0]))
-    cots = exchange(cots)
-    packed = []
+    slices = [spread(block, [], near[:1], order_of_hops, sizes)[0] for block in slices]
+    rows, one, two = lax.optimization_barrier((rows, *slices))
+    slices = [spread(block, near[:1], near[1:], order_of_hops, sizes) for block in (one, two)]
+    cots = [dispatch(rows, cotangent, None, cap, capp, owners, [l]) for l in range(local)]
+    cots[0], w_in, w_back, one, two = lax.optimization_barrier(
+        (cots[0], w_in, w_back, slices[0][0], slices[1][0])
+    )
+    cots[0] = exchange(cots[0])
+    halves = []
     for block, (_, have), path in ((one, slices[0], routes_one), (two, slices[1], routes_two)):
         half, _ = spread(block, have, path[len(near) :], order_of_hops, sizes)
-        half = half.reshape(groups // 2, owners * own, block.shape[-1])
-        packed.append((half, swap(half, sibling, sizes)))
-
+        halves.append(half.reshape(groups // 2, owners * own, block.shape[-1]))
     biases = jnp.zeros((local, 16, width), f32)
     biases = biases.at[:, 0, :hidden].set(b_in).at[:, 1, :depth].set(b_back)
-    wback = jnp.concatenate([w_back, biases], axis=1).astype(bf16)
-    win = lax.all_gather(w_in.astype(bf16), "group")
-    wback = lax.all_gather(wback, "group")
-
+    wide = w_in.reshape(local, depth, -1, width).swapaxes(1, 2).reshape(local, -1, width)
+    height = hidden + wide.shape[1] + 16
+    experts = [
+        jnp.concatenate([w_back[l], wide[l], biases[l]], axis=0).astype(bf16)
+        for l in range(local)
+    ]
+    cots[0], cots[-1], *moved = lax.optimization_barrier((cots[0], cots[-1], *experts, *halves))
+    experts, halves = moved[:local], moved[local:]
+    cots[1:] = [exchange(block) for block in cots[1:]]
+    experts = [lax.all_gather(block, "group") for block in experts]
+    packed = [(half, swap(half, sibling, sizes)) for half in halves]
     qkv, mixed, lse, first, routed, gates, gate_rows = forward(core, tokens, marks, packed, labels)
-    sent = dispatch(rows, routed, gate_rows, cap, capp, owners, local)
-    cots, *sent = lax.optimization_barrier((cots, *sent))
-    sent = [exchange(block) for block in sent]
-    outcomes, backs, share_in, share_back = [], [], [], []
+    sent = [dispatch(rows, routed, gate_rows, cap, capp, owners, [l]) for l in range(local)]
+    cots[-1], sent[0] = lax.optimization_barrier((cots[-1], sent[0]))
+    sent[0] = exchange(sent[0])
+    for l in range(1, local):
+        sent[l - 1], sent[l] = lax.optimization_barrier((sent[l - 1], sent[l]))
+        sent[l] = exchange(sent[l])
+    joined, backs, shares = None, [], []
     for l in range(local):
-        bias = wback[:, l, hidden + 1, :depth].reshape(1, width)
-        outcome, back, grad_in, grad_back = expert(sent[l], cots, win, wback, bias, l, cap)
+        joined, back, grads = expert(sent[l], cots[l], experts[l], joined, l, local, cap)
+        if l:
+            back, backs[-1] = lax.optimization_barrier((back, backs[-1]))
         if l + 1 < local:
             back, sent[l + 1] = lax.optimization_barrier((back, sent[l + 1]))
-        if l:
-            back, backs[-1] = lax.optimization_barrier((back, backs[-1]))
-        backs.append(exchange(back))
-        outcomes.append(outcome)
-        share_in.append(lax.psum_scatter(grad_in, "group", scatter_dimension=0))
-        share_back.append(lax.psum_scatter(grad_back, "group", scatter_dimension=0))
-    joined = jnp.concatenate(outcomes, axis=1)
+            grads, sent[l + 1] = lax.optimization_barrier((grads, sent[l + 1]))
+            back = exchange(back)
+        else:
+            back = exchange(back)
+            grads, back = lax.optimization_barrier((grads, back))
+        backs.append(back)
+        shares.append(lax.psum_scatter(grads, "group", scatter_dimension=0))
     joined, *backs = lax.optimization_barrier((joined, *backs))
     joined = exchange(joined)
-    share_in = jnp.stack(share_in).astype(f32)
-    share_back = jnp.stack(share_back).astype(f32)
     grad_tokens, *halves = backward(
         core,
         tokens,
@@ -880,38 +1041,46 @@
         backs,
         labels,
     )
-    output = combine(first, cols, gates, joined, local)
-    sums = []
+    sums, later = [], []
     for keep, away, path in (
         (halves[0], halves[1], routes_one[::-1]),
         (halves[2], halves[3], routes_two[::-1]),
     ):
-        total = keep + swap(away, sibling, sizes).astype(f32)
+        total = keep.astype(f32) + swap(away, sibling, sizes).astype(f32)
         total = total.reshape(*[2] * len(order_of_hops), own, keep.shape[2])
-        first_hops = path[: len(path) - len(near)]
-        sums.append(gather_back(total, first_hops, order_of_hops, sizes))
-    one, two, output = lax.optimization_barrier((*sums, output))
+        sums.append(gather_back(total, path[:1], order_of_hops, sizes))
+        later.append((path[1 : len(path) - len(near)], [h for h in order_of_hops if h != path[0]]))
+    share = list(share_out(shares[0], None, 0, local, depth))
+    *sums, joined, grad_tokens, share[0] = lax.optimization_barrier(
+        (*sums, joined, grad_tokens, share[0])
+    )
+    one, two = [gather_back(part, *where, sizes) for part, where in zip(sums, later)]
+    output = combine(first, cols, gates, joined, local)
+    one, two, output = lax.optimization_barrier((one, two, output))
     rest = [hop for hop in order_of_hops if hop in near]
-    sums = [gather_back(part, near[::-1], rest, sizes) for part in (one, two)]
-    one, two = sums
-    small = two[:, 2 * width :]
-    grad_router = small[:, :labels].reshape(own, local, owners).swapaxes(1, 2).reshape(own, labels)
+    one, two = [gather_back(part, near[:0:-1], rest, sizes) for part in (one, two)]
+    for l in range(1, local):
+        share = share_out(shares[l], share, l, local, depth)
+    one, two, *share = lax.optimization_barrier((one, two, *share))
+    one, two = [halve(part, near[0], 0, sizes) for part in (one, two)]
+    share_back, share_in, share_bias = share
+    grad_qkv, grad_out, grad_router, small = dense_out(one, two, labels, owners)
     place = lax.axis_index("group") * depth
     return (
         output,
         grad_tokens,
-        small[:, labels],
-        small[:, labels + 1],
-        jnp.concatenate([one, two[:, :width]], axis=1),
-        two[:, width : 2 * width],
-        small[:, labels + 2],
-        small[:, labels + 3],
-        small[:, labels + 4],
+        small[0],
+        small[1],
+        grad_qkv,
+        grad_out,
+        small[2],
+        small[3],
+        small[4],
         grad_router,
         share_in,
-        share_back[:, hidden, :hidden],
-        share_back[:, :hidden],
-        lax.dynamic_slice_in_dim(share_back[:, hidden + 1], place, depth, axis=1),
+        share_bias[:, 0, :hidden],
+        share_back,
+        lax.dynamic_slice_in_dim(share_bias[:, 1], place, depth, axis=1),
     )
 
 

time: 540 us -> 461 us (0.85)
  waiting for transfers between devices: 174 us -> 112 us
  blocking collectives: 85.2 us -> 42.2 us
  starting transfers between devices: 42.3 us -> 57.8 us
  Pallas kernels: 160 us -> 171 us
  other arithmetic: 24.3 us -> 18.3 us
    ppermute x20, waiting for transfers between devices: 130 us -> 68.4 us  [swap(): lax.ppermute(block, axis, [(d, d ^ 1 << bit) for d in range(sizes[axis])])]
    all_to_all x2 -> x1, blocking collectives: 85.2 us -> 42.2 us  [per_device(): exchange = lambda block: lax.all_to_all(block, 'expert', 0, 0, tiled=True)]
    all_to_all x4 -> x6, starting transfers between devices: 16.6 us -> 32.8 us  [per_device(): exchange = lambda block: lax.all_to_all(block, 'expert', 0, 0, tiled=True)]
    reduce_scatter x4 -> x2, waiting for transfers between devices: 10.9 us -> 0.02 us  [per_device(): shares.append(lax.psum_scatter(grads, 'group', scatter_dimension=0))]
    all_to_all x4 -> x6, waiting for transfers between devices: 31.8 us -> 42.4 us  [per_device(): exchange = lambda block: lax.all_to_all(block, 'expert', 0, 0, tiled=True)]
    pallas_call x2 -> x8, Pallas kernels: 12.8 us -> 23.1 us  [the longest x4 14.5 us: dispatch(): pl.pallas_call(functools.partial(dispatch_kernel, cap, capp, owners, tupl...]
    convert_element_type x3 -> x0, other arithmetic: 8.51 us -> none  [the longest x1 4.12 us: per_device(): share_in = jnp.stack(share_in).astype(f32)]
    convert_element_type x8, local copies, waits for them, and re-layouts: 0.35 us -> 6.04 us  [halve(): return (stay, swap(away.astype(bf16), hop, sizes))]
  transfers between devices with their start and end apart: 30 -> 30, of which waited for: 15 -> 15; matrix products, arithmetic and copies ran while one was open for 6% -> 7% of each run, Pallas kernels for 21% -> 36%
where the time goes in v2:
time: 461 us; the launch traced here: 453 us
  Pallas kernels  171 us (37%)
  waiting for transfers between devices  112 us (24%)
  starting transfers between devices  57.8 us (13%)
  blocking collectives  42.2 us (9%)
  local copies, waits for them, and re-layouts  37.1 us (8%)
  other arithmetic  18.3 us (4%)
  between operations  14.9 us (3%)
    pallas_call x2, Pallas kernels, expert(): pl.pallas_call(functools.partial(expert_kernel, cap), grid=(groups,), in_...  77.8 us
    ppermute x20, waiting for transfers between devices, swap(): lax.ppermute(block, axis, [(d, d ^ 1 << bit) for d in range(sizes[axis])])  68.4 us
    pallas_call x1, Pallas kernels, backward(): pl.pallas_call(functools.partial(backward_kernel, labels, local, cap), gr...  44.3 us
    all_to_all x6, waiting for transfers between devices, per_device(): exchange = lambda block: lax.all_to_all(block, 'expert', 0, 0, tiled=True)  42.4 us
    all_to_all x1, blocking collectives, per_device(): exchange = lambda block: lax.all_to_all(block, 'expert', 0, 0, tiled=True)  42.2 us
    all_to_all x6, starting transfers between devices, per_device(): exchange = lambda block: lax.all_to_all(block, 'expert', 0, 0, tiled=True)  32.8 us
    unnamed x78, local copies, waits for them, and re-layouts  26 us
    ppermute x20, starting transfers between devices, swap(): lax.ppermute(block, axis, [(d, d ^ 1 << bit) for d in range(sizes[axis])])  24.5 us
  transfers between devices with their start and end apart: 30, of which 15 were waited for; matrix products, arithmetic and copies ran while one was open for 7% of the time, Pallas kernels for 36%

profile of v2, /device:TPU:0, one launch (start us, length us, event | category | flops | bytes accessed | tf_op | source)
XLA Modules:
  0.0 452.8 jit_solution(8803848528228968657)
XLA Ops:
  11.7 4.0 collective-permute-start
  31.6 4.3 collective-permute-done.3
  36.1 5.5 %all-to-all-start = ((bf16[8,128,768]{2,1,0:T(8,128)(2,1)}), bf16[8,128,768]{2,1,0:T(8,128)(2,1)}, u32[]{:S(2)}, u32[]{:S(2)}) async-start(bf16[8,128,768]{2,1,0:T(8,128)(2,1)} %fill_slots.4), calls=%async_computation | async-start | bytes 3145728 | tf_op jit(solution)/shard_map/all_to_all | solution.py:979
  52.1 11.6 %collective-permute-done.4 = bf16[2,2,24,1536]{3,2,0,1:T(8,128)(2,1)S(1)} collective-permute-done((bf16[2,2,24,1536]{3,2,0,1:T(8,128)(2,1)S(1)}, bf16[2,2,24,1536]{3,2,0,1:T(8,128)(2,1)S(1)}, u32[]{:S(2)}, u32[]{:S(2)}) %collective-permute-start.4) | collective-permute-done | bytes 294944 | tf_op jit(solution)/shard_map/ppermute | solution.py:900
  65.7 12.1 %collective-permute-done.5 = bf16[2,2,2,24,1536]{4,3,0,1,2:T(8,128)(2,1)S(1)} collective-permute-done((bf16[2,2,2,24,1536]{4,3,0,1,2:T(8,128)(2,1)S(1)}, bf16[2,2,2,24,1536]{4,3,0,1,2:T(8,128)(2,1)S(1)}, u32[]{:S(2)}, u32[]{:S(2)}) %collective-permute-start.5) | collective-permute-done | bytes 589856 | tf_op jit(solution)/shard_map/ppermute | solution.py:900
  78.1 3.5 collective-permute-done.7
  82.8 9.5 %all-to-all-start.1 = ((bf16[8,128,768]{2,1,0:T(8,128)(2,1)}), bf16[8,128,768]{2,1,0:T(8,128)(2,1)}, u32[]{:S(2)}, u32[]{:S(2)}) async-start(bf16[8,128,768]{2,1,0:T(8,128)(2,1)} %fill_slots.5), calls=%async_computation.1 | async-start | bytes 3145728 | tf_op jit(solution)/shard_map/all_to_all | solution.py:979
  95.4 16.7 %attention_forward.1 = (bf16[4,197,2304]{2,1,0:T(8,128)(2,1)}, bf16[4,197,768]{2,1,0:T(8,128)(2,1)S(1)}, f32[4,16,256]{2,1,0:T(8,128)S(1)}, f32[4,197,768]{2,1,0...) custom-call(s32[1]{0:T(128)} %bitcast.core_ref, ...), custom_call_target="tpu_custom_call" | custom-call | flops 16000000000 | bytes 20000000 | tf_op jit(solution)/shard_map/attention_forward/pallas_call | solution.py:360
  116.0 4.4 fill_slots.6
  120.3 9.6 %all-to-all-done.1.cot_ref = bf16[8,128,768]{2,1,0:T(8,128)(2,1)} async-done(((bf16[8,128,768]{2,1,0:T(8,128)(2,1)}), bf16[8,128,768]{2,1,0:T(8,128)(2,1)}, u32[]{:S(2)}, u32[]{:S(2)}) %all-to-all-start.1) | async-done | bytes 1572896 | tf_op jit(solution)/shard_map/all_to_all | solution.py:979
  130.0 4.3 all-to-all-start.2
  134.3 4.0 fill_slots.7
  138.3 32.8 %all-to-all-done.2.rows_ref = bf16[8,128,768]{2,1,0:T(8,128)(2,1)} async-done(((bf16[8,128,768]{2,1,0:T(8,128)(2,1)}), bf16[8,128,768]{2,1,0:T(8,128)(2,1)}, u32[]{:S(2)}, u32[]{:S(2)}) %all-to-all-start.2) | async-done | bytes 1572896 | tf_op jit(solution)/shard_map/all_to_all | solution.py:979
  171.1 3.6 all-to-all-start.3
  175.0 38.8 %expert_rows.2 = (bf16[8,256,768]{2,1,0:T(8,128)(2,1)}, bf16[8,128,768]{2,1,0:T(8,128)(2,1)}, bf16[4,1552,768]{2,1,0:T(8,128)(2,1)}) custom-call(bf16[8,128,768]{2,1,0:T(8,128)(2,1)} %all-to-all-done.2.rows_ref, bf16[8,128,768]{2,1,0:T(8,128)(2,1)} %all-to-all-done.cot_ref, bf16[4,1552,768]{2,1,0:T(8,128)(2,1)} %bitcast.141, ...), custom_call_target="tpu_custom_call" | custom-call | flops 28991029248 | bytes 30000000 | tf_op jit(solution)/shard_map/expert_rows/pallas_call | solution.py:541
  215.0 6.0 %all-to-all-start.4 = ((bf16[8,128,768]{2,1,0:T(8,128)(2,1)}), bf16[8,128,768]{2,1,0:T(8,128)(2,1)S(1)}, u32[]{:S(2)}, u32[]{:S(2)}) async-start(bf16[8,128,768]{2,1,0:T(8,128)(2,1)} %get-tuple-element.148), calls=%async_computation.4 | async-start | bytes 3145728 | tf_op jit(solution)/shard_map/all_to_all | solution.py:979
  221.2 38.9 %expert_rows.3 = (bf16[8,256,768]{2,1,0:T(8,128)(2,1)}, bf16[8,128,768]{2,1,0:T(8,128)(2,1)}, bf16[4,1552,768]{2,1,0:T(8,128)(2,1)}) custom-call(bf16[8,128,768]{2,1,0:T(8,128)(2,1)} %copy-done.25, bf16[8,128,768]{2,1,0:T(8,128)(2,1)} %all-to-all-done.1.cot_ref, bf16[4,1552,768]{2,1,0:T(8,128)(2,1)} %bitcast.138, ...), custom_call_target="tpu_custom_call", output_to_operand_aliasing={{0}: (5, {})} | custom-call | flops 28991029248 | bytes 30000000 | tf_op jit(solution)/shard_map/expert_rows/pallas_call | solution.py:541
  260.2 42.2 %all_to_all.35.refs_1_ = bf16[8,128,768]{2,1,0:T(8,128)(2,1)} all-to-all(bf16[8,128,768]{2,1,0:T(8,128)(2,1)} %get-tuple-element.151), channel_id=1, replica_groups=mesh['group'=4,'expert'=8] {'expert'}, dimensions={0} | all-to-all | bytes 3145728 | tf_op jit(solution)/shard_map/all_to_all | solution.py:979
  302.4 3.9 all-to-all-start.6
  306.3 44.3 %attention_backward.1 = (f32[4,197,768]{2,1,0:T(8,128)}, bf16[2,192,1536]{2,1,0:T(8,128)(2,1)}, bf16[2,192,1536]{2,1,0:T(8,128)(2,1)}, bf16[2,192,1664]{2,1,0:T(8,128)(2,1)}, bf16[2,192,1664]{2,1,0:T(8,128)(2,1)}) custom-call(s32[1]{0:T(128)} %bitcast.core_ref, bf16[4,197,768]{2,1,0:T(8,128)(2,1)} %copy-done.7, bf16[4,197,768]{2,1,0:T(8,128)(2,1)} %copy-done.2, ...), custom_call_target="tpu_custom_call" | custom-call | flops 40000000000 | bytes 40000000 | tf_op jit(solution)/shard_map/attention_backward/pallas_call | solution.py:797
  353.9 3.5 convert_add_fusion.1
  367.0 21.4 %collective-permute-done.11 = bf16[2,2,2,24,1536]{4,3,0,1,2:T(8,128)(2,1)} collective-permute-done((bf16[2,2,2,24,1536]{4,3,0,1,2:T(8,128)(2,1)}, bf16[2,2,2,24,1536]{4,3,0,1,2:T(8,128)(2,1)}, u32[]{:S(2)}, u32[]{:S(2)}) %collective-permute-start.11) | collective-permute-done | bytes 589856 | tf_op jit(solution)/shard_map/ppermute | solution.py:900
  407.3 6.6 %combine_outputs.1 = bf16[4,197,768]{2,1,0:T(8,128)(2,1)S(1)} custom-call(f32[4,197,768]{2,1,0:T(8,128)S(1)} %copy-done.5, s32[4,197,8]{2,1,0:T(8,128)S(1)} %copy-done.11, f32[4,197,16]{2,1,0:T(8,128)S(1)} %copy-done.13, bf16[8,256,768]{2,1,0:T(8,128)(2,1)S(1)} %all-to-all-done.6.slots_ref), custom_call_target="tpu_custom_call" | custom-call | tf_op jit(solution)/shard_map/combine_outputs/pallas_call | solution.py:876
  421.5 4.0 collective-permute-done.16
  (187 shorter events, 102.4 us)
Async XLA Ops:
  11.7 9.3 %collective-permute-start = (bf16[24,1536]{1,0:T(8,128)(2,1)}, bf16[24,1536]{1,0:T(8,128)(2,1)S(1)}, u32[]{:S(2)}, u32[]{:S(2)}) collective-permute-start(bf16[24,1536]{1,0:T(8,128)(2,1)} %get-tuple-element.114), channel_id=1, source_target_pairs={{0,4},{1,5},{2,6},{3,7},{4,0},{5,1},{6,2},{7,3},{8,12},{9,13},{10,... | collective-permute-start | bytes 221192 | tf_op jit(solution)/shard_map/ppermute | solution.py:900
  15.7 7.6 %collective-permute-start.1 = (bf16[24,1664]{1,0:T(8,128)(2,1)}, bf16[24,1664]{1,0:T(8,128)(2,1)S(1)}, u32[]{:S(2)}, u32[]{:S(2)}) collective-permute-start(bf16[24,1664]{1,0:T(8,128)(2,1)} %get-tuple-element.115), channel_id=1, source_target_pairs={{0,4},{1,5},{2,6},{3,7},{4,0},{5,1},{6,2},{7,3},{8,12},{9,13},{10,... | collective-permute-start | bytes 239624 | tf_op jit(solution)/shard_map/ppermute | solution.py:900
  23.4 8.2 %collective-permute-start.2 = (bf16[2,24,1536]{2,1,0:T(8,128)(2,1)S(1)}, bf16[2,24,1536]{2,1,0:T(8,128)(2,1)S(1)}, u32[]{:S(2)}, u32[]{:S(2)}) collective-permute-start(bf16[2,24,1536]{2,1,0:T(8,128)(2,1)S(1)} %pad_maximum_fusion.9), channel_id=1, source_target_pairs={{0,2},{1,3},{2,0},{3,1},{4,6},{5,7},{6,4},{7,5},{8,10},{9,11},{10,... | collective-permute-start | bytes 442376 | tf_op jit(solution)/shard_map/ppermute | solution.py:900
  36.1 45.9 %all-to-all-start = ((bf16[8,128,768]{2,1,0:T(8,128)(2,1)}), bf16[8,128,768]{2,1,0:T(8,128)(2,1)}, u32[]{:S(2)}, u32[]{:S(2)}) async-start(bf16[8,128,768]{2,1,0:T(8,128)(2,1)} %fill_slots.4), calls=%async_computation | async-start | bytes 3145728 | tf_op jit(solution)/shard_map/all_to_all | solution.py:979
  41.6 133.4 %all-gather.5.cloned.1.call-start = ((), (), s32[]{:S(2)}) async-start(), calls=%async_computation.11 | async-start | bytes 11919360 | tf_op jit(solution)/shard_map/all_gather | solution.py:1003
  46.1 17.6 %collective-permute-start.4 = (bf16[2,2,24,1536]{3,2,0,1:T(8,128)(2,1)S(1)}, bf16[2,2,24,1536]{3,2,0,1:T(8,128)(2,1)S(1)}, u32[]{:S(2)}, u32[]{:S(2)}) collective-permute-start(bf16[2,2,24,1536]{3,2,0,1:T(8,128)(2,1)S(1)} %pad_maximum_fusion.7), channel_id=1, source_target_pairs={{0,1},{1,0},{2,3},{3,2},{4,5},{5,4},{6,7},{7,6},{8,9},{9,8},{10,11... | collective-permute-start | bytes 884744 | tf_op jit(solution)/shard_map/ppermute | solution.py:900
  48.1 17.2 %collective-permute-start.6 = (bf16[2,2,24,1664]{3,2,0,1:T(8,128)(2,1)S(1)}, bf16[2,2,24,1664]{3,2,0,1:T(8,128)(2,1)S(1)}, u32[]{:S(2)}, u32[]{:S(2)}) collective-permute-start(bf16[2,2,24,1664]{3,2,0,1:T(8,128)(2,1)S(1)} %pad_maximum_fusion.6), channel_id=1, source_target_pairs={{0,16},{8,24},{16,0},{24,8},{1,17},{9,25},{17,1},{25,9},{2,18},{10... | collective-permute-start | bytes 958472 | tf_op jit(solution)/shard_map/ppermute | solution.py:900
  63.8 14.0 %collective-permute-start.5 = (bf16[2,2,2,24,1536]{4,3,0,1,2:T(8,128)(2,1)S(1)}, bf16[2,2,2,24,1536]{4,3,0,1,2:T(8,128)(2,1)S(1)}, u32[]{:S(2)}, u32[]{:S(2)}) collective-permute-start(bf16[2,2,2,24,1536]{4,3,0,1,2:T(8,128)(2,1)S(1)} %pad_maximum_fusion.5), channel_id=1, source_target_pairs={{0,16},{8,24},{16,0},{24,8},{1,17},{9,25},{17,1},{25,9},{2,18},{10... | collective-permute-start | bytes 1769480 | tf_op jit(solution)/shard_map/ppermute | solution.py:900
  65.5 16.1 %collective-permute-start.7 = (bf16[2,2,2,24,1664]{4,3,1,2,0:T(8,128)(2,1)S(1)}, bf16[2,2,2,24,1664]{4,3,1,2,0:T(8,128)(2,1)S(1)}, u32[]{:S(2)}, u32[]{:S(2)}) collective-permute-start(bf16[2,2,2,24,1664]{4,3,1,2,0:T(8,128)(2,1)S(1)} %pad_maximum_fusion.4), channel_id=1, source_target_pairs={{0,1},{1,0},{2,3},{3,2},{4,5},{5,4},{6,7},{7,6},{8,9},{9,8},{10,11... | collective-permute-start | bytes 1916936 | tf_op jit(solution)/shard_map/ppermute | solution.py:900
  82.0 139.2 %all-gather.7.cloned.1.call-start = ((), (), s32[]{:S(2)}) async-start(), calls=%async_computation.12 | async-start | bytes 11919360 | tf_op jit(solution)/shard_map/all_gather | solution.py:1003
  82.7 12.6 %collective-permute-start.9 = (bf16[2,192,1664]{2,1,0:T(8,128)(2,1)S(1)}, bf16[2,192,1664]{2,1,0:T(8,128)(2,1)}, u32[]{:S(2)}, u32[]{:S(2)}) collective-permute-start(bf16[2,192,1664]{2,1,0:T(8,128)(2,1)S(1)} %bitcast.117), channel_id=1, source_target_pairs={{0,8},{8,0},{16,24},{24,16},{1,9},{9,1},{17,25},{25,17},{2,10},{10... | collective-permute-start | bytes 3833864 | tf_op jit(solution)/shard_map/ppermute | solution.py:900
  82.8 47.2 %all-to-all-start.1 = ((bf16[8,128,768]{2,1,0:T(8,128)(2,1)}), bf16[8,128,768]{2,1,0:T(8,128)(2,1)}, u32[]{:S(2)}, u32[]{:S(2)}) async-start(bf16[8,128,768]{2,1,0:T(8,128)(2,1)} %fill_slots.5), calls=%async_computation.1 | async-start | bytes 3145728 | tf_op jit(solution)/shard_map/all_to_all | solution.py:979
  130.0 41.1 %all-to-all-start.2 = ((bf16[8,128,768]{2,1,0:T(8,128)(2,1)}), bf16[8,128,768]{2,1,0:T(8,128)(2,1)}, u32[]{:S(2)}, u32[]{:S(2)}) async-start(bf16[8,128,768]{2,1,0:T(8,128)(2,1)} %fill_slots.6), calls=%async_computation.2 | async-start | bytes 3145728 | tf_op jit(solution)/shard_map/all_to_all | solution.py:979
  171.1 42.7 %all-to-all-start.3 = ((bf16[8,128,768]{2,1,0:T(8,128)(2,1)}), bf16[8,128,768]{2,1,0:T(8,128)(2,1)S(1)}, u32[]{:S(2)}, u32[]{:S(2)}) async-start(bf16[8,128,768]{2,1,0:T(8,128)(2,1)} %fill_slots.7), calls=%async_computation.3 | async-start | bytes 3145728 | tf_op jit(solution)/shard_map/all_to_all | solution.py:979
  174.7 218.6 %reduce-scatter.3.cloned.1.call-start = ((), (), s32[]{:S(2)}) async-start(), calls=%async_computation.9 | async-start | bytes 11919360 | tf_op jit(solution)/shard_map/reduce_scatter | solution.py:1025
  215.0 45.2 %all-to-all-start.4 = ((bf16[8,128,768]{2,1,0:T(8,128)(2,1)}), bf16[8,128,768]{2,1,0:T(8,128)(2,1)S(1)}, u32[]{:S(2)}, u32[]{:S(2)}) async-start(bf16[8,128,768]{2,1,0:T(8,128)(2,1)} %get-tuple-element.148), calls=%async_computation.4 | async-start | bytes 3145728 | tf_op jit(solution)/shard_map/all_to_all | solution.py:979
  220.9 206.3 %reduce-scatter.5.cloned.1.call-start = ((), (), s32[]{:S(2)}) async-start(), calls=%async_computation.10 | async-start | bytes 11919360 | tf_op jit(solution)/shard_map/reduce_scatter | solution.py:1025
  302.4 95.8 %all-to-all-start.6 = ((bf16[8,256,768]{2,1,0:T(8,128)(2,1)}), bf16[8,256,768]{2,1,0:T(8,128)(2,1)S(1)}, u32[]{:S(2)}, u32[]{:S(2)}) async-start(bf16[8,256,768]{2,1,0:T(8,128)(2,1)} %get-tuple-element.159), calls=%async_computation.6 | async-start | bytes 6291456 | tf_op jit(solution)/shard_map/all_to_all | solution.py:979
  350.7 10.1 %collective-permute-start.12 = (bf16[2,192,1664]{2,1,0:T(8,128)(2,1)}, bf16[2,192,1664]{2,1,0:T(8,128)(2,1)}, u32[]{:S(2)}, u32[]{:S(2)}) collective-permute-start(bf16[2,192,1664]{2,1,0:T(8,128)(2,1)} %get-tuple-element.158), channel_id=1, source_target_pairs={{0,8},{8,0},{16,24},{24,16},{1,9},{9,1},{17,25},{25,17},{2,10},{10... | collective-permute-start | bytes 3833864 | tf_op jit(solution)/shard_map/ppermute | solution.py:900
  359.5 28.9 %collective-permute-start.11 = (bf16[2,2,2,24,1536]{4,3,0,1,2:T(8,128)(2,1)}, bf16[2,2,2,24,1536]{4,3,0,1,2:T(8,128)(2,1)}, u32[]{:S(2)}, u32[]{:S(2)}) collective-permute-start(bf16[2,2,2,24,1536]{4,3,0,1,2:T(8,128)(2,1)} %fusion.1), channel_id=1, source_target_pairs={{0,16},{8,24},{16,0},{24,8},{1,17},{9,25},{17,1},{25,9},{2,18},{10... | collective-permute-start | bytes 1769480 | tf_op jit(solution)/shard_map/ppermute | solution.py:900
  364.8 26.2 %collective-permute-start.13 = (bf16[2,2,2,24,1664]{4,3,1,2,0:T(8,128)(2,1)}, bf16[2,2,2,24,1664]{4,3,1,2,0:T(8,128)(2,1)}, u32[]{:S(2)}, u32[]{:S(2)}) collective-permute-start(bf16[2,2,2,24,1664]{4,3,1,2,0:T(8,128)(2,1)} %fusion), channel_id=1, source_target_pairs={{0,1},{1,0},{2,3},{3,2},{4,5},{5,4},{6,7},{7,6},{8,9},{9,8},{10,11... | collective-permute-start | bytes 1916936 | tf_op jit(solution)/shard_map/ppermute | solution.py:900
  400.1 16.3 %collective-permute-start.14 = (bf16[2,2,24,1536]{3,2,0,1:T(8,128)(2,1)}, bf16[2,2,24,1536]{3,2,0,1:T(8,128)(2,1)}, u32[]{:S(2)}, u32[]{:S(2)}) collective-permute-start(bf16[2,2,24,1536]{3,2,0,1:T(8,128)(2,1)} %fusion.3), channel_id=1, source_target_pairs={{0,1},{1,0},{2,3},{3,2},{4,5},{5,4},{6,7},{7,6},{8,9},{9,8},{10,11... | collective-permute-start | bytes 884744 | tf_op jit(solution)/shard_map/ppermute | solution.py:900
  403.5 14.0 %collective-permute-start.15 = (bf16[2,2,24,1664]{3,2,0,1:T(8,128)(2,1)S(1)}, bf16[2,2,24,1664]{3,2,0,1:T(8,128)(2,1)S(1)}, u32[]{:S(2)}, u32[]{:S(2)}) collective-permute-start(bf16[2,2,24,1664]{3,2,0,1:T(8,128)(2,1)S(1)} %fusion.2), channel_id=1, source_target_pairs={{0,16},{8,24},{16,0},{24,8},{1,17},{9,25},{17,1},{25,9},{2,18},{10... | collective-permute-start | bytes 958472 | tf_op jit(solution)/shard_map/ppermute | solution.py:900
  432.8 6.7 %collective-permute-start.18 = (bf16[24,1536]{1,0:T(8,128)(2,1)S(1)}, bf16[24,1536]{1,0:T(8,128)(2,1)S(1)}, u32[]{:S(2)}, u32[]{:S(2)}) collective-permute-start(bf16[24,1536]{1,0:T(8,128)(2,1)S(1)} %fusion.7), channel_id=1, source_target_pairs={{0,4},{1,5},{2,6},{3,7},{4,0},{5,1},{6,2},{7,3},{8,12},{9,13},{10,... | collective-permute-start | bytes 221192 | tf_op jit(solution)/shard_map/ppermute | solution.py:900
  (41 other events, 281.8 us)
Sparse Core Ops, SparseCore 0:
  82.1 68.9 all-gather.4
  153.2 64.7 all-gather.6
  220.7 79.0 reduce-scatter.2
  302.5 91.3 reduce-scatter.4

commit v3 on v2

--- a/solution.py
+++ b/solution.py
@@ -72,23 +72,23 @@
             copy.wait()
 
 
-def pack_kernel(owners, qkv_ref, out_ref, router_ref, vec_ref, one_ref, two_ref):
+def pack_kernel(owners, qkv_ref, out_ref, router_ref, *refs):
+    vec_refs, (one_ref, two_ref) = refs[:VECTORS], refs[VECTORS:]
     own, width = out_ref.shape
-    labels = router_ref.shape[1]
+    labels = router_ref.shape[0]
     local = labels // owners
     one_ref[...] = qkv_ref[:, 0 : 2 * width].astype(bf16)
     two_ref[:, 0:width] = qkv_ref[:, 2 * width :].astype(bf16)
     two_ref[:, width : 2 * width] = out_ref[...].astype(bf16)
-    router = router_ref[...]
-    columns = [
-        router[:, o * local + l : o * local + l + 1] for l in range(local) for o in range(owners)
+    lines = [
+        router_ref[o * local + l : o * local + l + 1, :] for l in range(local) for o in range(owners)
     ]
-    vectors = jnp.concatenate([vec_ref[...], jnp.zeros((LANES - VECTORS, own), f32)], axis=0)
+    lines += [vec_ref[...] for vec_ref in vec_refs]
+    lines.append(jnp.zeros((LANES - labels - VECTORS, own), f32))
+    small = jnp.concatenate(lines, axis=0)
     if own < LANES:
-        vectors = jnp.concatenate([vectors, jnp.zeros((LANES, LANES - own), f32)], axis=1)
-    vectors = jnp.transpose(vectors)[0:own, 0:VECTORS]
-    blank = jnp.zeros((own, LANES - labels - VECTORS), f32)
-    two_ref[:, 2 * width :] = jnp.concatenate([*columns, vectors, blank], axis=1).astype(bf16)
+        small = jnp.concatenate([small, jnp.zeros((LANES, LANES - own), f32)], axis=1)
+    two_ref[:, 2 * width :] = jnp.transpose(small)[0:own].astype(bf16)
 
 
 def pack(w_qkv, w_out, w_router, vectors, owners):
@@ -100,12 +100,14 @@
             jax.ShapeDtypeStruct((own, 2 * width + LANES), bf16),
         ],
         name="pack_weights",
-    )(w_qkv, w_out, w_router, vectors)
-
-
-def dense_out_kernel(owners, one_ref, one_in, two_ref, two_in, qkv_ref, out_ref, router_ref, vec_ref):
+    )(w_qkv, w_out, w_router.T, *[vector.reshape(1, own) for vector in vectors])
+
+
+def dense_out_kernel(
+    owners, one_ref, one_in, two_ref, two_in, qkv_ref, out_ref, router_ref, *vec_refs
+):
     own, width = out_ref.shape
-    labels = router_ref.shape[1]
+    labels = router_ref.shape[0]
     local = labels // owners
     one = one_ref[...] + one_in[...].astype(f32)
     two = two_ref[...] + two_in[...].astype(f32)
@@ -113,13 +115,15 @@
     qkv_ref[:, 2 * width :] = two[:, 0:width]
     out_ref[...] = two[:, width : 2 * width]
     small = two[:, 2 * width :]
-    columns = [
-        small[:, l * owners + o : l * owners + o + 1] for o in range(owners) for l in range(local)
-    ]
-    router_ref[...] = jnp.concatenate(columns, axis=1)
     if own < LANES:
         small = jnp.concatenate([small, jnp.zeros((LANES - own, LANES), f32)], axis=0)
-    vec_ref[...] = jnp.transpose(small)[labels : labels + 8, 0:own]
+    small = jnp.transpose(small)[:, 0:own]
+    for o in range(owners):
+        for l in range(local):
+            at = o * local + l
+            router_ref[at : at + 1, :] = small[l * owners + o : l * owners + o + 1]
+    for k, vec_ref in enumerate(vec_refs):
+        vec_ref[...] = small[labels + k : labels + k + 1]
 
 
 def dense_out(one, two, labels, owners):
@@ -130,8 +134,8 @@
         out_shape=[
             jax.ShapeDtypeStruct((own, 3 * width), f32),
             jax.ShapeDtypeStruct((own, width), f32),
-            jax.ShapeDtypeStruct((own, labels), f32),
-            jax.ShapeDtypeStruct((8, own), f32),
+            jax.ShapeDtypeStruct((labels, own), f32),
+            *[jax.ShapeDtypeStruct((1, own), f32)] * VECTORS,
         ],
         name="dense_gradients",
     )(*one, *two)
@@ -495,13 +499,18 @@
     row = iota((16, width), 0)
     if hidden < width:
         bias_sum = jnp.concatenate([bias_sum, jnp.zeros((1, width - hidden), f32)], axis=1)
-    pad = jnp.where(row == 0, bias_sum, jnp.where(row == 1, bias_ref[0:1, :], 0.0))
+    pad = jnp.where(row == 0, bias_sum, 0.0)
     gbias_ref[step] = pad.astype(bf16)
     for copy in copies(step, slot):
         copy.start()
 
     @pl.when(step == last)
     def _():
+        for g in range(groups):
+            part = bias_ref[0:1, g * depth : (g + 1) * depth]
+            part = jnp.concatenate([part, jnp.zeros((1, width - depth), f32)], axis=1)
+            block = gbias_ref[g].astype(f32)
+            gbias_ref[g] = jnp.where(row == 1, part, block).astype(bf16)
         end = pltpu.make_async_copy(
             gbias_ref, weights_ref.at[:, pl.ds(weights_ref.shape[1] - 16, 16)], sems.at[2, 0]
         )
@@ -585,26 +594,254 @@
     )(rows, cots, weights, weights, weights, *extra)
 
 
-def share_kernel(*refs):
-    parts, (back_ref, in_ref, bias_ref) = refs[:3], refs[-3:]
-    value = [part[...] for part in parts]
-    back_ref[0] = value[0].astype(f32)
-    in_ref[0] = value[1].astype(f32)
-    bias_ref[0] = value[2].astype(f32)
-
-
-def share_out(share, outs, which, local, depth):
-    height, width = share.shape
+def parted_kernel(
+    cap,
+    core_ref,
+    rows_ref,
+    cot_ref,
+    win_ref,
+    wback_ref,
+    biases_ref,
+    *refs,
+):
+    (
+        out_ref,
+        grad_ref,
+        keep_ref,
+        away_ref,
+        turned_ref,
+        grad_out_ref,
+        out_acc_ref,
+        grad_acc_ref,
+        active_ref,
+        inner_ref,
+        bias_ref,
+        gwin_ref,
+        gwback_ref,
+        gbias_ref,
+        sems,
+    ) = refs[-15:]
+    owners, capp, width = rows_ref.shape
+    groups, depth, hidden = win_ref.shape
+    spare = cap - (capp - 16)
+    step = pl.program_id(0)
+    last = pl.num_programs(0) - 1
+    slot = lax.rem(step, 2)
+    across = width // hidden
+
+    mine = core_ref[0]
+    targets = ((keep_ref, mine, 0), (away_ref, 1 - mine, 1))
+
+    def copies(step, slot):
+        at = pl.multiple_of(hidden + lax.div(step, across) * depth, 16)
+        start = pl.multiple_of(lax.rem(step, across) * hidden, LANES)
+        return [
+            pltpu.make_async_copy(
+                gwin_ref.at[slot, :, part],
+                target.at[:, pl.ds(at, depth), pl.ds(start, hidden)],
+                sems.at[1 + k, slot],
+            )
+            for target, part, k in targets
+        ]
+
+    def whole_chunk(step, slot, act):
+        for target, part, _ in targets:
+
+            @pl.when(lax.rem(step, 2) == part)
+            def _():
+                act(
+                    pltpu.make_async_copy(
+                        gwback_ref.at[slot],
+                        target.at[lax.div(step, 2), pl.ds(0, hidden)],
+                        sems.at[0, slot],
+                    )
+                )
+
+    def finish(step, slot):
+        for copy in copies(step, slot):
+            copy.wait()
+        whole_chunk(step, slot, lambda copy: copy.wait())
+
+    @pl.when(step >= 2)
+    def _():
+        finish(step - 2, slot)
+
+    @pl.when(step == 0)
+    def _():
+        summed = jnp.zeros((1, width), f32)
+        for b in range(owners):
+            tail = rows_ref[b, capp - 16 :, 0:capp].astype(f32)
+            gate = (
+                tail[spare : spare + 1] + tail[spare + 1 : spare + 2] + tail[spare + 2 : spare + 3]
+            )
+            gate = jnp.transpose(jnp.broadcast_to(gate, (LANES, capp)))[:, 0:1]
+            part = (cot_ref[b].astype(f32) * gate).astype(bf16)
+            grad_out_ref[b * capp : (b + 1) * capp, :] = part
+            summed = summed + jnp.sum(part.astype(f32), axis=0, keepdims=True)
+            turned_ref[:, b * capp : (b + 1) * capp] = jnp.transpose(rows_ref[b])
+        bias_ref[...] = jnp.broadcast_to(summed, bias_ref.shape)
+        out_acc_ref[...] = jnp.zeros_like(out_acc_ref)
+        grad_acc_ref[...] = jnp.zeros_like(grad_acc_ref)
+
+    first = win_ref[...].reshape(width, hidden)
+    second = wback_ref[0]
+    bias = biases_ref[step].astype(f32)[0:1, 0:hidden]
+    bias_sum = jnp.zeros((1, hidden), f32)
+    per = max(1, 256 // capp)
+    k0 = 0.7978845608028654
+    k1 = 0.044715
+    for c in range(owners // per):
+        at = slice(c * per * capp, (c + 1) * per * capp)
+        block = rows_ref[c * per : (c + 1) * per].reshape(per * capp, width)
+        inner = dot(block, first) + bias
+        square = inner * inner
+        curve = jnp.tanh(inner * (k0 + (k0 * k1) * square))
+        half = 0.5 * (1.0 + curve)
+        low = (inner * half).astype(bf16)
+        active_ref[at, :] = low
+        slope = half + (0.5 * inner) * (1.0 - curve * curve) * (k0 + (3.0 * k0 * k1) * square)
+        grad_inner = dot_nt(grad_out_ref[at, :], second) * slope
+        bias_sum = bias_sum + jnp.sum(grad_inner, axis=0, keepdims=True)
+        grad_low = grad_inner.astype(bf16)
+        inner_ref[at, :] = grad_low
+        out_acc_ref[at, :] += dot(low, second)
+        grad_acc_ref[at, :] += dot_nt(grad_low, first)
+    gwin_ref[slot] = dot(turned_ref[...], inner_ref[...]).astype(bf16).reshape(gwin_ref.shape[1:])
+    gwback_ref[slot] = dot_tn(active_ref[...], grad_out_ref[...]).astype(bf16)
+    row = iota((16, width), 0)
+    if hidden < width:
+        bias_sum = jnp.concatenate([bias_sum, jnp.zeros((1, width - hidden), f32)], axis=1)
+    pad = jnp.where(row == 0, bias_sum, 0.0)
+    gbias_ref[lax.div(step, 2), lax.rem(step, 2)] = pad.astype(bf16)
+    for copy in copies(step, slot):
+        copy.start()
+    whole_chunk(step, slot, lambda copy: copy.start())
+
+    @pl.when(step == last)
+    def _():
+        for g in range(groups):
+            part = bias_ref[0:1, g * depth : (g + 1) * depth]
+            part = jnp.concatenate([part, jnp.zeros((1, width - depth), f32)], axis=1)
+            block = gbias_ref[g // 2, g % 2].astype(f32)
+            gbias_ref[g // 2, g % 2] = jnp.where(row == 1, part, block).astype(bf16)
+        ends = [
+            pltpu.make_async_copy(
+                gbias_ref.at[:, part],
+                target.at[:, pl.ds(target.shape[1] - 16, 16)],
+                sems.at[3, k],
+            )
+            for target, part, k in targets
+        ]
+        for end in ends:
+            end.start()
+        whole = jnp.concatenate(
+            [biases_ref[g].astype(f32)[1:2, 0:depth] for g in range(groups)], axis=1
+        )
+        for b in range(owners):
+            at = slice(b * capp, (b + 1) * capp)
+            result = (out_acc_ref[at, :] + whole).astype(bf16)
+            out_ref[b] = result
+            score = jnp.sum(result.astype(f32) * cot_ref[b].astype(f32), axis=1, keepdims=True)
+            score = jnp.transpose(jnp.broadcast_to(score, (capp, LANES)))[0:1, :]
+            back = grad_acc_ref[at, :]
+            grad_ref[b] = back.astype(bf16)
+            tail = back[capp - 16 :, 0:capp]
+            line = iota((16, capp), 0) - spare
+            for k, part in enumerate(three_parts(score)):
+                tail = jnp.where(line == k, part, tail)
+            grad_ref[b, capp - 16 :, 0:capp] = tail.astype(bf16)
+        finish(step - 1, 1 - slot)
+        finish(step, slot)
+        for end in ends:
+            end.wait()
+
+
+def parted_expert(core, rows, cots, weights, outcomes, which, local, cap):
+    owners, capp, width = rows.shape
+    groups, height, _ = weights.shape
+    depth = width // groups
+    hidden = height - 16 - (height - 16) // 2
+    across = width // hidden
+    total = owners * capp
+    full = lambda shape: pl.BlockSpec(shape, lambda j: (0,) * len(shape))
+    anywhere = pl.BlockSpec(memory_space=pl.ANY)
+    extra = [] if outcomes is None else [outcomes]
+    return pl.pallas_call(
+        functools.partial(parted_kernel, cap),
+        grid=(groups,),
+        in_specs=[
+            pl.BlockSpec(memory_space=pltpu.SMEM),
+            full((owners, capp, width)),
+            full((owners, capp, width)),
+            pl.BlockSpec(
+                (groups, depth, hidden), lambda j: (0, hidden // depth + j // across, j % across)
+            ),
+            pl.BlockSpec((1, hidden, width), lambda j: (j, 0, 0)),
+            pl.BlockSpec((groups, 16, width), lambda j: (0, (height - 16) // 16, 0)),
+            *[anywhere] * len(extra),
+        ],
+        out_specs=[
+            pl.BlockSpec((owners, capp, width), lambda j: (0, which, 0)),
+            full((owners, capp, width)),
+            anywhere,
+            anywhere,
+        ],
+        out_shape=[
+            jax.ShapeDtypeStruct((owners, local * capp, width), bf16),
+            jax.ShapeDtypeStruct((owners, capp, width), bf16),
+            jax.ShapeDtypeStruct((groups // 2, height, width), bf16),
+            jax.ShapeDtypeStruct((groups // 2, height, width), bf16),
+        ],
+        input_output_aliases={6: 0} if extra else {},
+        scratch_shapes=[
+            pltpu.VMEM((width, total), bf16),
+            pltpu.VMEM((total, width), bf16),
+            pltpu.VMEM((total, width), f32),
+            pltpu.VMEM((total, width), f32),
+            pltpu.VMEM((total, hidden), bf16),
+            pltpu.VMEM((total, hidden), bf16),
+            pltpu.VMEM((8, width), f32),
+            pltpu.VMEM((2, groups // 2, 2, depth, hidden), bf16),
+            pltpu.VMEM((2, hidden, width), bf16),
+            pltpu.VMEM((groups // 2, 2, 16, width), bf16),
+            pltpu.SemaphoreType.DMA((4, 2)),
+        ],
+        compiler_params=params(56),
+        cost_estimate=pl.CostEstimate(
+            flops=2 * 6 * total * width * hidden * groups,
+            bytes_accessed=30_000_000,
+            transcendentals=total * hidden * groups,
+        ),
+        name="expert_rows_parted",
+    )(core, rows, cots, weights, weights, weights, *extra)
+
+
+def share_kernel(addends, *refs):
+    back_ref, in_ref, bias_ref = refs[-3:]
+    value = [refs[k][...].astype(f32) for k in range(3)]
+    if addends > 1:
+        value = [part + refs[3 + k][...].astype(f32) for k, part in enumerate(value)]
+    back_ref[0] = value[0]
+    in_ref[0] = value[1]
+    bias_ref[0] = value[2]
+
+
+def share_out(shares, outs, which, local, depth):
+    height, width = shares[0].shape
     hidden = (height - 16) // 2
     steps = hidden // depth
     extra = [] if outs is None else list(outs)
+    operands = [share for share in shares for _ in range(3)]
     return pl.pallas_call(
-        share_kernel,
+        functools.partial(share_kernel, len(shares)),
         grid=(steps,),
         in_specs=[
-            pl.BlockSpec((depth, width), lambda j: (j, 0)),
-            pl.BlockSpec((depth, width), lambda j: (steps + j, 0)),
-            pl.BlockSpec((16, width), lambda j: (2 * hidden // 16, 0)),
+            *[
+                pl.BlockSpec((depth, width), lambda j: (j, 0)),
+                pl.BlockSpec((depth, width), lambda j: (steps + j, 0)),
+                pl.BlockSpec((16, width), lambda j: (2 * hidden // 16, 0)),
+            ]
+            * len(shares),
             *[pl.BlockSpec(memory_space=pl.ANY)] * len(extra),
         ],
         out_specs=[
@@ -617,15 +854,164 @@
             jax.ShapeDtypeStruct((local, depth, steps * width), f32),
             jax.ShapeDtypeStruct((local, 16, width), f32),
         ],
-        input_output_aliases={3 + k: k for k in range(len(extra))},
+        input_output_aliases={len(operands) + k: k for k in range(len(extra))},
         compiler_params=params(32),
         name="expert_gradients",
-    )(share, share, share, *extra)
+    )(*operands, *extra)
+
+
+def stage_kernel(own_rows, *refs):
+    bits, refs = refs[: len(own_rows)], refs[len(own_rows) :]
+    for k, rows in enumerate(own_rows):
+        keep_ref, other_ref = refs[2 * k : 2 * k + 2]
+        stay_ref, away_ref = refs[2 * (len(own_rows) + k) : 2 * (len(own_rows) + k) + 2]
+        mine = bits[k][0] == 0
+        total = keep_ref[...].astype(f32) + other_ref[...].astype(f32)
+        if total.ndim == 3:
+            pairs = [(total[0], total[1])]
+        else:
+            pairs = [
+                (total[at : at + rows], total[at + rows : at + 2 * rows])
+                for at in range(0, total.shape[0], 2 * rows)
+            ]
+        stay = [jnp.where(mine, one, two) for one, two in pairs]
+        away = [jnp.where(mine, two, one) for one, two in pairs]
+        stay_ref[...] = jnp.concatenate(stay, axis=0)
+        away_ref[...] = jnp.concatenate(away, axis=0).astype(bf16)
+
+
+def stage(pairs, lengths, bits):
+    rows = [pair[0].size // pair[0].shape[-1] for pair in pairs]
+    turns = [count // (2 * length) for count, length in zip(rows, lengths)]
+
+    def fits(steps):
+        return all(
+            length % (16 * steps) == 0
+            if turn == 1
+            else turn % steps == 0 and length * (turn // steps) % 16 == 0
+            for turn, length in zip(turns, lengths)
+        )
+
+    steps = next((count for count in (4, 2) if fits(count)), 1)
+    operands, in_specs, out_specs, out_shape = [], [], [], []
+    for pair, count, length, turn in zip(pairs, rows, lengths, turns):
+        columns = pair[0].shape[-1]
+        if turn == 1 and length % 16 == 0:
+            shape, block = (2, length, columns), (2, length // steps, columns)
+            where = lambda j: (0, j, 0)
+        else:
+            shape, block = (count, columns), (count // steps, columns)
+            where = lambda j: (j, 0)
+        operands += [part.reshape(shape) for part in pair]
+        in_specs += [pl.BlockSpec(block, where)] * 2
+        half = pl.BlockSpec((count // 2 // steps, columns), lambda j: (j, 0))
+        out_specs += [half, half]
+        out_shape += [jax.ShapeDtypeStruct((count // 2, columns), kind) for kind in (f32, bf16)]
+    results = pl.pallas_call(
+        functools.partial(stage_kernel, tuple(lengths)),
+        grid=(steps,),
+        in_specs=[*[pl.BlockSpec(memory_space=pltpu.SMEM)] * len(pairs), *in_specs],
+        out_specs=out_specs,
+        out_shape=out_shape,
+        compiler_params=params(40),
+        name="add_and_halve",
+    )(*[bit.astype(jnp.int32).reshape(1) for bit in bits], *operands)
+    return [results[2 * k : 2 * k + 2] for k in range(len(pairs))]
 
 
 def add_to(ref, columns, value):
     shape = (*ref.shape[:-1], value.shape[-1])
     ref[..., columns] += value.reshape(shape)
+
+
+def pick(which, cap, cols_ref, slots, score_ref):
+    length = cols_ref.shape[1]
+    owners, capp, width = slots[0].shape
+    spare = cap - (capp - 16)
+    span = owners * capp
+    picked = gate_one = gate_two = None
+    for k, l in enumerate(which):
+        lane = iota((length, span), 1) + l * span
+        one = jnp.where(lane == cols_ref[0, :, 0:1], 1.0, 0.0)
+        two = jnp.where(lane == cols_ref[0, :, 1:2], 1.0, 0.0)
+        part = dot((one + two).astype(bf16), slots[k][...].reshape(span, width))
+        picked = part if picked is None else picked + part
+        score = score_ref[:, k * span : (k + 1) * span]
+        part_one = dot_nt(one.astype(bf16), score)
+        part_two = dot_nt(two.astype(bf16), score)
+        gate_one = part_one if gate_one is None else gate_one + part_one
+        gate_two = part_two if gate_two is None else gate_two + part_two
+    line = iota((length, 16), 1)
+    mine = (line >= spare) & (line < spare + 3)
+    gate_one = jnp.sum(jnp.where(mine, gate_one, 0.0), axis=1, keepdims=True)
+    gate_two = jnp.sum(jnp.where(mine, gate_two, 0.0), axis=1, keepdims=True)
+    return picked, gate_one, gate_two
+
+
+def load_scores(slots, score_ref):
+    owners, capp, _ = slots[0].shape
+    span = owners * capp
+    for k, block in enumerate(slots):
+        for o in range(owners):
+            at = k * span + o * capp
+            score_ref[:, at : at + capp] = block[o, capp - 16 :, 0:capp]
+
+
+def early_kernel(local, cap, cols_ref, qkv_ref, lse_ref, *refs):
+    slots = refs[:local]
+    picked_ref, gate_ref, probs_ref, score_ref = refs[local:]
+    _, length, width = picked_ref.shape
+
+    @pl.when(pl.program_id(0) == 0)
+    def _():
+        load_scores(slots, score_ref)
+
+    picked, gate_one, gate_two = pick(range(local), cap, cols_ref, slots, score_ref)
+    picked_ref[0] = picked
+    lane = iota((length, 8), 1)
+    gate_ref[0] = jnp.where(lane == 0, gate_one, jnp.where(lane == 1, gate_two, 0.0))
+    low_half = iota((length, LANES), 1) < HEAD_DIM
+    rate = jnp.asarray(HEAD_DIM**-0.5, bf16)
+    for pair in range(width // LANES):
+        at = pair * LANES
+        query = qkv_ref[0, :, at : at + LANES] * rate
+        keys = qkv_ref[0, :, width + at : width + at + LANES]
+        for half in range(2):
+            own = low_half if half == 0 else jnp.logical_not(low_half)
+            head = 2 * pair + half
+            scores = dot_nt(keys, jnp.where(own, query, jnp.zeros_like(query)))
+            probs = jnp.exp(scores - lse_ref[0, head : head + 1, 0:length])
+            probs_ref[0, head] = probs.astype(bf16)
+
+
+def early(cols, qkv, lse, slots, cap):
+    images, length, wide = qkv.shape
+    width = wide // 3
+    heads = width // HEAD_DIM
+    owners, capp, _ = slots[0].shape
+    whole = lambda *tail: pl.BlockSpec((1, *tail), lambda i: (i, *[0] * len(tail)))
+    return pl.pallas_call(
+        functools.partial(early_kernel, len(slots), cap),
+        grid=(images,),
+        in_specs=[
+            whole(length, 8),
+            whole(length, wide),
+            whole(*lse.shape[1:]),
+            *[pl.BlockSpec((owners, capp, width), lambda i: (0, 0, 0))] * len(slots),
+        ],
+        out_specs=[whole(length, width), whole(length, 8), whole(heads, length, length)],
+        out_shape=[
+            jax.ShapeDtypeStruct((images, length, width), f32),
+            jax.ShapeDtypeStruct((images, length, 8), f32),
+            jax.ShapeDtypeStruct((images, heads, length, length), bf16),
+        ],
+        scratch_shapes=[pltpu.VMEM((16, len(slots) * owners * capp), bf16)],
+        compiler_params=params(40),
+        cost_estimate=pl.CostEstimate(
+            flops=10_000_000_000, bytes_accessed=20_000_000, transcendentals=2_000_000
+        ),
+        name="attention_again",
+    )(cols, qkv, lse, *slots)
 
 
 def backward_kernel(
@@ -638,7 +1024,9 @@
     cols_ref,
     qkv_ref,
     mixed_ref,
-    lse_ref,
+    picked_ref,
+    scores_ref,
+    probs_ref,
     first_ref,
     routed_ref,
     gates_ref,
@@ -648,7 +1036,7 @@
     two_other,
     *refs,
 ):
-    slots = refs[:local]
+    slots = refs[:1]
     (
         grad_tokens_ref,
         keep_one_ref,
@@ -664,11 +1052,8 @@
         two_ref,
         misc_ref,
         sems,
-    ) = refs[local:]
+    ) = refs[1:]
     _, length, width = tokens_ref.shape
-    owners, capp, _ = slots[0].shape
-    spare = cap - (capp - 16)
-    span = owners * capp
     step = pl.program_id(0)
     parts = ((one_own, one_other), (two_own, two_other))
     load_weights(step, core_ref[0], parts, (one_ref, two_ref), sems)
@@ -685,33 +1070,14 @@
         grad_two_ref[...] = jnp.zeros_like(grad_two_ref)
         vec_ref[...] = jnp.zeros_like(vec_ref)
         stack_ref[...] = jnp.zeros_like(stack_ref)
-        for l in range(local):
-            for o in range(owners):
-                score_ref[:, l * span + o * capp : l * span + (o + 1) * capp] = slots[l][
-                    o, capp - 16 :, 0:capp
-                ]
+        load_scores(slots, score_ref)
 
     cot = cot_ref[0].astype(f32)
-    aim_one, aim_two = cols_ref[0, :, 0:1], cols_ref[0, :, 1:2]
     route_one, route_two = cols_ref[0, :, 2:3], cols_ref[0, :, 3:4]
-    picked = None
-    gate_one = None
-    gate_two = None
-    for l in range(local):
-        lane = iota((length, span), 1) + l * span
-        one = jnp.where(lane == aim_one, 1.0, 0.0)
-        two = jnp.where(lane == aim_two, 1.0, 0.0)
-        part = dot((one + two).astype(bf16), slots[l][...].reshape(span, width))
-        picked = part if picked is None else picked + part
-        score = score_ref[:, l * span : (l + 1) * span]
-        part_one = dot_nt(one.astype(bf16), score)
-        part_two = dot_nt(two.astype(bf16), score)
-        gate_one = part_one if gate_one is None else gate_one + part_one
-        gate_two = part_two if gate_two is None else gate_two + part_two
-    line = iota((length, 16), 1)
-    mine = (line >= spare) & (line < spare + 3)
-    gate_one = jnp.sum(jnp.where(mine, gate_one, 0.0), axis=1, keepdims=True)
-    gate_two = jnp.sum(jnp.where(mine, gate_two, 0.0), axis=1, keepdims=True)
+    picked, gate_one, gate_two = pick([local - 1], cap, cols_ref, slots, score_ref)
+    picked = picked + picked_ref[0]
+    gate_one = gate_one + scores_ref[0, :, 0:1]
+    gate_two = gate_two + scores_ref[0, :, 1:2]
     label = iota((length, labels), 1)
     grad_gates = jnp.where(label == route_one, gate_one, 0.0) + jnp.where(
         label == route_two, gate_two, 0.0
@@ -748,11 +1114,12 @@
             query_own = jnp.where(own, query, none)
             mix_own = jnp.where(own, mix, none)
             head = 2 * pair + half
-            probs = jnp.exp(dot_nt(keys, query_own) - lse_ref[0, head : head + 1, 0:length])
+            low = probs_ref[0, head]
+            probs = low.astype(f32)
             grad_probs = dot_nt(values, mix_own)
             inner = jnp.sum(grad_probs * probs, axis=0, keepdims=True)
             scores = (probs * (grad_probs - inner)).astype(bf16)
-            part = dot(probs.astype(bf16), mix_own)
+            part = dot(low, mix_own)
             grad_v = part if grad_v is None else grad_v + part
             part = dot(scores, query_own)
             grad_k = part if grad_k is None else grad_k + part
@@ -786,12 +1153,11 @@
 
 
 def backward(
-    core, tokens, cot, cols, qkv, mixed, lse, first, routed, gates, cap, packed, slots, labels
+    core, tokens, cot, cols, qkv, mixed, ahead, first, routed, gates, cap, packed, slots, local, labels
 ):
     images, length, width = tokens.shape
-    local = len(slots)
-    owners, capp, _ = slots[0].shape
-    whole = lambda *tail: pl.BlockSpec((1, *tail), lambda i: (i, 0, 0))
+    owners, capp, _ = slots.shape
+    whole = lambda *tail: pl.BlockSpec((1, *tail), lambda i: (i, *[0] * len(tail)))
     shapes = [part[0].shape for part in packed]
     still = lambda shape: pl.BlockSpec(shape, lambda i: (0, 0, 0))
     return pl.pallas_call(
@@ -804,12 +1170,12 @@
             whole(length, 8),
             whole(length, 3 * width),
             whole(length, width),
-            whole(*lse.shape[1:]),
+            *[whole(*part.shape[1:]) for part in ahead],
             whole(length, width),
             whole(length, width),
             whole(length, labels),
             *[pl.BlockSpec(memory_space=pl.ANY)] * 4,
-            *[pl.BlockSpec((owners, capp, width), lambda i: (0, 0, 0))] * local,
+            pl.BlockSpec((owners, capp, width), lambda i: (0, 0, 0)),
         ],
         out_specs=[
             whole(length, width),
@@ -823,7 +1189,7 @@
             *[pltpu.VMEM((shape[0], 2, *shape[1:]), f32) for shape in shapes],
             pltpu.VMEM((LANES, width), f32),
             pltpu.VMEM((8, width), f32),
-            pltpu.VMEM((16, local * owners * capp), bf16),
+            pltpu.VMEM((16, owners * capp), bf16),
             *weight_scratch(packed),
             pltpu.VMEM((LANES, width), bf16),
             pltpu.SemaphoreType.DMA((4,)),
@@ -840,13 +1206,13 @@
         cols,
         qkv,
         mixed,
-        lse,
+        *ahead,
         first,
         routed,
         gates,
         *packed[0],
         *packed[1],
-        *slots,
+        slots,
     )
 
 
@@ -970,7 +1336,7 @@
     core = own_bit(sibling).astype(jnp.int32).reshape(1)
     routes_one = [*inner, *outer]
     routes_two = [*inner[:-1], *outer, *inner[-1:]]
-    vectors = jnp.stack([ln1_gain, ln1_bias, b_out, ln2_gain, ln2_bias])
+    vectors = (ln1_gain, ln1_bias, b_out, ln2_gain, ln2_bias)
     slices = pack(w_qkv, w_out, w_router, vectors, owners)
     near = inner[:-1]
     marks = (routes % local) * owners + routes // local
@@ -978,17 +1344,25 @@
     rows, cols = route(marks, order, labels, cap, capp)
     exchange = lambda block: lax.all_to_all(block, "expert", 0, 0, tiled=True)
     slices = [spread(block, [], near[:1], order_of_hops, sizes)[0] for block in slices]
-    rows, one, two = lax.optimization_barrier((rows, *slices))
-    slices = [spread(block, near[:1], near[1:], order_of_hops, sizes) for block in (one, two)]
+    slices = [spread(block, near[:1], near[1:], order_of_hops, sizes) for block in slices]
+    haves = [have for _, have in slices]
+    rows, *slices = lax.optimization_barrier((rows, *[block for block, _ in slices]))
     cots = [dispatch(rows, cotangent, None, cap, capp, owners, [l]) for l in range(local)]
-    cots[0], w_in, w_back, one, two = lax.optimization_barrier(
-        (cots[0], w_in, w_back, slices[0][0], slices[1][0])
-    )
     cots[0] = exchange(cots[0])
+    columns = [block.shape[-1] for block in slices]
     halves = []
-    for block, (_, have), path in ((one, slices[0], routes_one), (two, slices[1], routes_two)):
-        half, _ = spread(block, have, path[len(near) :], order_of_hops, sizes)
-        halves.append(half.reshape(groups // 2, owners * own, block.shape[-1]))
+    for turn in range(len(outer) + 1):
+        moved = []
+        for k, path in enumerate((routes_one, routes_two)):
+            hop = path[len(near) + turn]
+            block, haves[k] = spread(slices[k], haves[k], [hop], order_of_hops, sizes)
+            moved.append(block)
+        if turn == 0:
+            w_in, w_back, *moved = lax.optimization_barrier((w_in, w_back, *moved))
+        slices = moved
+    halves = [
+        block.reshape(groups // 2, owners * own, count) for block, count in zip(slices, columns)
+    ]
     biases = jnp.zeros((local, 16, width), f32)
     biases = biases.at[:, 0, :hidden].set(b_in).at[:, 1, :depth].set(b_back)
     wide = w_in.reshape(local, depth, -1, width).swapaxes(1, 2).reshape(local, -1, width)
@@ -1011,19 +1385,33 @@
         sent[l] = exchange(sent[l])
     joined, backs, shares = None, [], []
     for l in range(local):
-        joined, back, grads = expert(sent[l], cots[l], experts[l], joined, l, local, cap)
+        if l + 1 < local:
+            joined, back, grads = expert(sent[l], cots[l], experts[l], joined, l, local, cap)
+        else:
+            joined, back, keep, away = parted_expert(
+                core, sent[l], cots[l], experts[l], joined, l, local, cap
+            )
         if l:
             back, backs[-1] = lax.optimization_barrier((back, backs[-1]))
         if l + 1 < local:
             back, sent[l + 1] = lax.optimization_barrier((back, sent[l + 1]))
             grads, sent[l + 1] = lax.optimization_barrier((grads, sent[l + 1]))
-            back = exchange(back)
+            shares.append([lax.psum_scatter(grads, "group", scatter_dimension=0)])
         else:
-            back = exchange(back)
-            grads, back = lax.optimization_barrier((grads, back))
+            if l:
+                away, backs[-1] = lax.optimization_barrier((away, backs[-1]))
+            total = keep.astype(f32) + swap(away, sibling, sizes).astype(f32)
+            total = total.reshape(*[2] * len(outer), height, width)
+            total = gather_back(total, outer[:-1], outer, sizes)
+            bit = own_bit(outer[-1])
+            stay = lax.dynamic_index_in_dim(total, bit, 0, keepdims=False).astype(bf16)
+            away = lax.dynamic_index_in_dim(total, 1 - bit, 0, keepdims=False).astype(bf16)
+        back = exchange(back)
+        if l == local - 1:
+            stay, away, back = lax.optimization_barrier((stay, away, back))
+            shares.append([stay, swap(away, outer[-1], sizes)])
         backs.append(back)
-        shares.append(lax.psum_scatter(grads, "group", scatter_dimension=0))
-    joined, *backs = lax.optimization_barrier((joined, *backs))
+    joined, backs[-1] = lax.optimization_barrier((joined, backs[-1]))
     joined = exchange(joined)
     grad_tokens, *halves = backward(
         core,
@@ -1032,55 +1420,66 @@
         cols,
         qkv,
         mixed,
-        lse,
+        early(cols, qkv, lse, backs[:-1], cap),
         first,
         routed,
         gates,
         cap,
         packed,
-        backs,
+        backs[-1],
+        local,
         labels,
     )
-    sums, later = [], []
-    for keep, away, path in (
-        (halves[0], halves[1], routes_one[::-1]),
-        (halves[2], halves[3], routes_two[::-1]),
-    ):
-        total = keep.astype(f32) + swap(away, sibling, sizes).astype(f32)
-        total = total.reshape(*[2] * len(order_of_hops), own, keep.shape[2])
-        sums.append(gather_back(total, path[:1], order_of_hops, sizes))
-        later.append((path[1 : len(path) - len(near)], [h for h in order_of_hops if h != path[0]]))
-    share = list(share_out(shares[0], None, 0, local, depth))
-    *sums, joined, grad_tokens, share[0] = lax.optimization_barrier(
-        (*sums, joined, grad_tokens, share[0])
-    )
-    one, two = [gather_back(part, *where, sizes) for part, where in zip(sums, later)]
-    output = combine(first, cols, gates, joined, local)
-    one, two, output = lax.optimization_barrier((one, two, output))
-    rest = [hop for hop in order_of_hops if hop in near]
-    one, two = [gather_back(part, near[:0:-1], rest, sizes) for part in (one, two)]
-    for l in range(1, local):
-        share = share_out(shares[l], share, l, local, depth)
-    one, two, *share = lax.optimization_barrier((one, two, *share))
-    one, two = [halve(part, near[0], 0, sizes) for part in (one, two)]
+    sums = []
+    for keep, away in (halves[:2], halves[2:]):
+        sums.append((keep, swap(away, sibling, sizes)))
+    left = [list(order_of_hops), list(order_of_hops)]
+    paths = [routes_one[::-1], routes_two[::-1]]
+    share = output = None
+    for turn, hops in enumerate(zip(*paths)):
+        lengths = [own << (len(have) - 1 - have.index(hop)) for have, hop in zip(left, hops)]
+        sums = stage(sums, lengths, [own_bit(hop) for hop in hops])
+        sums = [(stay, swap(away, hop, sizes)) for (stay, away), hop in zip(sums, hops)]
+        for have, hop in zip(left, hops):
+            have.remove(hop)
+        if turn == 0:
+            share = share_out(shares[0], None, 0, local, depth)
+            beside = [shares[-1][1], *share]
+        elif turn == 1:
+            output = combine(first, cols, gates, joined, local)
+            beside = [output]
+        elif turn == 2:
+            for l in range(1, local):
+                share = share_out(shares[l], share, l, local, depth)
+            beside = [*share, grad_tokens]
+        else:
+            continue
+        one, two, *beside = lax.optimization_barrier((sums[0][1], sums[1][1], *beside))
+        sums = [(sums[0][0], one), (sums[1][0], two)]
+        if turn == 0:
+            shares[-1][1], *share = beside
+        elif turn == 1:
+            output = beside[0]
+        else:
+            *share, grad_tokens = beside
+    one, two = sums
     share_back, share_in, share_bias = share
-    grad_qkv, grad_out, grad_router, small = dense_out(one, two, labels, owners)
-    place = lax.axis_index("group") * depth
+    grad_qkv, grad_out, grad_router, *small = dense_out(one, two, labels, owners)
     return (
         output,
         grad_tokens,
-        small[0],
-        small[1],
+        small[0].reshape(own),
+        small[1].reshape(own),
         grad_qkv,
         grad_out,
-        small[2],
-        small[3],
-        small[4],
-        grad_router,
+        small[2].reshape(own),
+        small[3].reshape(own),
+        small[4].reshape(own),
+        grad_router.T,
         share_in,
         share_bias[:, 0, :hidden],
         share_back,
-        lax.dynamic_slice_in_dim(share_bias[:, 1], place, depth, axis=1),
+        share_bias[:, 1, :depth],
     )
 
 

time: 461 us -> 431 us (0.935)
  blocking collectives: 42.2 us -> 0 us
  Pallas kernels: 171 us -> 178 us
  waiting for transfers between devices: 112 us -> 118 us
    pallas_call x2 -> x8, Pallas kernels: 5.03 us -> 56.1 us  [the longest x1 38.9 us: parted_expert(): pl.pallas_call(functools.partial(parted_kernel, cap), grid=(groups,), in_...]
    all_to_all x1 -> x0, blocking collectives: 42.2 us -> none  [per_device(): exchange = lambda block: lax.all_to_all(block, 'expert', 0, 0, tiled=True)]
    pallas_call x2 -> x1, Pallas kernels: 77.8 us -> 38.9 us  [expert(): pl.pallas_call(functools.partial(expert_kernel, cap), grid=(groups,), in_...]
    all_to_all x6 -> x7, waiting for transfers between devices: 42.4 us -> 65.1 us  [per_device(): exchange = lambda block: lax.all_to_all(block, 'expert', 0, 0, tiled=True)]
    ppermute x20 -> x22, waiting for transfers between devices: 68.4 us -> 52.4 us  [swap(): lax.ppermute(block, axis, [(d, d ^ 1 << bit) for d in range(sizes[axis])])]
    add x6 -> x0, other arithmetic: 6.19 us -> none  [gather_back(): total = stay + other.astype(f32)]
    pallas_call x1, Pallas kernels: 44.3 us -> 38.3 us  [backward(): pl.pallas_call(functools.partial(backward_kernel, labels, local, cap), gr...]
    unnamed x78 -> x84, local copies, waits for them, and re-layouts: 26 us -> 30 us
  transfers between devices with their start and end apart: 30 -> 32, of which waited for: 15 -> 16; matrix products, arithmetic and copies ran while one was open for 7% -> 6% of each run, Pallas kernels for 36% -> 41%
where the time goes in v3:
time: 431 us; the launch traced here: 423 us
  Pallas kernels  178 us (41%)
  waiting for transfers between devices  118 us (27%)
  starting transfers between devices  61.9 us (14%)
  local copies, waits for them, and re-layouts  32.7 us (8%)
  other arithmetic  16.7 us (4%)
  between operations  14.9 us (3%)
    all_to_all x7, waiting for transfers between devices, per_device(): exchange = lambda block: lax.all_to_all(block, 'expert', 0, 0, tiled=True)  65.1 us
    ppermute x22, waiting for transfers between devices, swap(): lax.ppermute(block, axis, [(d, d ^ 1 << bit) for d in range(sizes[axis])])  52.4 us
    pallas_call x1, Pallas kernels, parted_expert(): pl.pallas_call(functools.partial(parted_kernel, cap), grid=(groups,), in_...  38.9 us
    pallas_call x1, Pallas kernels, expert(): pl.pallas_call(functools.partial(expert_kernel, cap), grid=(groups,), in_...  38.9 us
    pallas_call x1, Pallas kernels, backward(): pl.pallas_call(functools.partial(backward_kernel, labels, local, cap), gr...  38.3 us
    all_to_all x7, starting transfers between devices, per_device(): exchange = lambda block: lax.all_to_all(block, 'expert', 0, 0, tiled=True)  35.2 us
    unnamed x84, local copies, waits for them, and re-layouts  30 us
    ppermute x22, starting transfers between devices, swap(): lax.ppermute(block, axis, [(d, d ^ 1 << bit) for d in range(sizes[axis])])  26.4 us
  transfers between devices with their start and end apart: 32, of which 16 were waited for; matrix products, arithmetic and copies ran while one was open for 6% of the time, Pallas kernels for 41%

profile of v3, /device:TPU:0, one launch (start us, length us, event | category | flops | bytes accessed | tf_op | source)
XLA Modules:
  0.0 423.0 jit_solution(14746029222112780282)
XLA Ops:
  37.6 5.6 %all-to-all-start = ((bf16[8,128,768]{2,1,0:T(8,128)(2,1)}), bf16[8,128,768]{2,1,0:T(8,128)(2,1)}, u32[]{:S(2)}, u32[]{:S(2)}) async-start(bf16[8,128,768]{2,1,0:T(8,128)(2,1)} %fill_slots.4), calls=%async_computation | async-start | bytes 3145728 | tf_op jit(solution)/shard_map/all_to_all | solution.py:1345
  45.9 5.4 %collective-permute-done.5 = bf16[2,2,24,1664]{3,2,0,1:T(8,128)(2,1)S(1)} collective-permute-done((bf16[2,2,24,1664]{3,2,0,1:T(8,128)(2,1)S(1)}, bf16[2,2,24,1664]{3,2,0,1:T(8,128)(2,1)S(1)}, u32[]{:S(2)}, u32[]{:S(2)}) %collective-permute-start.5) | collective-permute-done | bytes 319520 | tf_op jit(solution)/shard_map/ppermute | solution.py:1266
  61.3 7.0 %collective-permute-done.6 = bf16[2,2,2,24,1536]{4,3,0,1,2:T(8,128)(2,1)S(1)} collective-permute-done((bf16[2,2,2,24,1536]{4,3,0,1,2:T(8,128)(2,1)S(1)}, bf16[2,2,2,24,1536]{4,3,0,1,2:T(8,128)(2,1)S(1)}, u32[]{:S(2)}, u32[]{:S(2)}) %collective-permute-start.6) | collective-permute-done | bytes 589856 | tf_op jit(solution)/shard_map/ppermute | solution.py:1266
  68.6 9.2 %collective-permute-done.7 = bf16[2,2,2,24,1664]{4,3,1,2,0:T(8,128)(2,1)S(1)} collective-permute-done((bf16[2,2,2,24,1664]{4,3,1,2,0:T(8,128)(2,1)S(1)}, bf16[2,2,2,24,1664]{4,3,1,2,0:T(8,128)(2,1)S(1)}, u32[]{:S(2)}, u32[]{:S(2)}) %collective-permute-start.7) | collective-permute-done | bytes 639008 | tf_op jit(solution)/shard_map/ppermute | solution.py:1266
  80.3 4.8 %all-to-all-start.1 = ((bf16[8,128,768]{2,1,0:T(8,128)(2,1)}), bf16[8,128,768]{2,1,0:T(8,128)(2,1)}, u32[]{:S(2)}, u32[]{:S(2)}) async-start(bf16[8,128,768]{2,1,0:T(8,128)(2,1)} %fill_slots.5), calls=%async_computation.1 | async-start | bytes 3145728 | tf_op jit(solution)/shard_map/all_to_all | solution.py:1345
  88.3 16.7 %attention_forward.1 = (bf16[4,197,2304]{2,1,0:T(8,128)(2,1)}, bf16[4,197,768]{2,1,0:T(8,128)(2,1)S(1)}, f32[4,16,256]{2,1,0:T(8,128)S(1)}, f32[4,197,768]{2,1,0...) custom-call(s32[1]{0:T(128)} %bitcast.2.core_ref, ...), custom_call_target="tpu_custom_call" | custom-call | flops 16000000000 | bytes 20000000 | tf_op jit(solution)/shard_map/attention_forward/pallas_call | solution.py:364
  107.5 4.4 %fill_slots.6 = bf16[8,128,768]{2,1,0:T(8,128)(2,1)} custom-call(s32[4,8,197]{2,1,0:T(8,128)S(1)} %get-tuple-element.143.rows_ref, bf16[4,197,768]{2,1,0:T(8,128)(2,1)S(1)} %get-tuple-element.156.value_ref.routed_ref, bf16[4,16,197]{2,1,0:T(8,128)(2,1)S(1)} %get-tuple-element.157.refs_0_), custom_call_target="tpu_custom_call" | custom-call | tf_op jit(solution)/shard_map/fill_slots/pallas_call | solution.py:255
  111.9 11.1 %all-to-all-done.1.cot_ref = bf16[8,128,768]{2,1,0:T(8,128)(2,1)} async-done(((bf16[8,128,768]{2,1,0:T(8,128)(2,1)}), bf16[8,128,768]{2,1,0:T(8,128)(2,1)}, u32[]{:S(2)}, u32[]{:S(2)}) %all-to-all-start.1) | async-done | bytes 1572896 | tf_op jit(solution)/shard_map/all_to_all | solution.py:1345
  123.0 4.3 %all-to-all-start.2 = ((bf16[8,128,768]{2,1,0:T(8,128)(2,1)}), bf16[8,128,768]{2,1,0:T(8,128)(2,1)}, u32[]{:S(2)}, u32[]{:S(2)}) async-start(bf16[8,128,768]{2,1,0:T(8,128)(2,1)} %fill_slots.6), calls=%async_computation.2 | async-start | bytes 3145728 | tf_op jit(solution)/shard_map/all_to_all | solution.py:1345
  131.3 33.1 %all-to-all-done.2.rows_ref = bf16[8,128,768]{2,1,0:T(8,128)(2,1)} async-done(((bf16[8,128,768]{2,1,0:T(8,128)(2,1)}), bf16[8,128,768]{2,1,0:T(8,128)(2,1)}, u32[]{:S(2)}, u32[]{:S(2)}) %all-to-all-start.2) | async-done | bytes 1572896 | tf_op jit(solution)/shard_map/all_to_all | solution.py:1345
  168.3 38.9 %expert_rows.1 = (bf16[8,256,768]{2,1,0:T(8,128)(2,1)}, bf16[8,128,768]{2,1,0:T(8,128)(2,1)}, bf16[4,1552,768]{2,1,0:T(8,128)(2,1)}) custom-call(bf16[8,128,768]{2,1,0:T(8,128)(2,1)} %all-to-all-done.2.rows_ref, bf16[8,128,768]{2,1,0:T(8,128)(2,1)} %all-to-all-done.cot_ref, bf16[4,1552,768]{2,1,0:T(8,128)(2,1)} %bitcast.115, ...), custom_call_target="tpu_custom_call" | custom-call | flops 28991029248 | bytes 30000000 | tf_op jit(solution)/shard_map/expert_rows/pallas_call | solution.py:550
  208.4 6.2 %all-to-all-start.4 = ((bf16[8,128,768]{2,1,0:T(8,128)(2,1)}), bf16[8,128,768]{2,1,0:T(8,128)(2,1)S(1)}, u32[]{:S(2)}, u32[]{:S(2)}) async-start(bf16[8,128,768]{2,1,0:T(8,128)(2,1)} %get-tuple-element.172), calls=%async_computation.4 | async-start | bytes 3145728 | tf_op jit(solution)/shard_map/all_to_all | solution.py:1345
  214.6 38.9 %expert_rows_parted.1 = (bf16[8,256,768]{2,1,0:T(8,128)(2,1)}, bf16[8,128,768]{2,1,0:T(8,128)(2,1)}, bf16[2,1552,768]{2,1,0:T(8,128)(2,1)}, bf16[2,1552,768]{2,1,0:T(8,128)(2,1)}) custom-call(s32[1]{0:T(128)} %bitcast.2.core_ref, bf16[8,128,768]{2,1,0:T(8,128)(2,1)} %copy-done.32, ...), custom_call_target="tpu_custom_call", output_to_operand_aliasing={{0}: (6, {})} | custom-call | flops 28991029248 | bytes 30000000 | tf_op jit(solution)/shard_map/expert_rows_parted/pallas_call | solution.py:769
  253.6 6.1 %all-to-all-start.5 = ((bf16[8,128,768]{2,1,0:T(8,128)(2,1)}), bf16[8,128,768]{2,1,0:T(8,128)(2,1)}, u32[]{:S(2)}, u32[]{:S(2)}) async-start(bf16[8,128,768]{2,1,0:T(8,128)(2,1)} %get-tuple-element.183), calls=%async_computation.5 | async-start | bytes 3145728 | tf_op jit(solution)/shard_map/all_to_all | solution.py:1345
  261.9 5.1 %attention_again.1 = (f32[4,197,768]{2,1,0:T(8,128)S(1)}, f32[4,197,8]{2,1,0:T(8,128)S(1)}, bf16[4,12,197,197]{3,2,1,0:T(8,128)(2,1)S(1)}) custom-call(s32[4,197,8]{2,1,0:T(8,128)S(1)} %get-tuple-element.139.cols_ref, bf16[4,197,2304]{2,1,0:T(8,128)(2,1)S(1)} %copy-done.27, f32[4,16,256]{2,1,0:T(8,128)S(1)} %get-tuple-element.154.lse_ref, ...), custom_call_target="tpu_custom_call" | custom-call | flops 10000000000 | bytes 20000000 | tf_op jit(solution)/shard_map/attention_again/pallas_call | solution.py:993
  269.2 6.9 %convert_add_fusion = bf16[2,1552,768]{2,1,0:T(8,128)(2,1)S(1)} fusion(bf16[2,1552,768]{2,1,0:T(8,128)(2,1)} %collective-permute-done.10, bf16[2,1552,768]{2,1,0:T(8,128)(2,1)} %get-tuple-element.181), kind=kLoop, calls=%fused_computation | loop fusion | flops 9535488 | bytes 14303232 | tf_op jit(solution)/shard_map/add | solution.py:1403
  277.8 19.6 %all-to-all-done.5.refs_0_ = bf16[8,128,768]{2,1,0:T(8,128)(2,1)} async-done(((bf16[8,128,768]{2,1,0:T(8,128)(2,1)}), bf16[8,128,768]{2,1,0:T(8,128)(2,1)}, u32[]{:S(2)}, u32[]{:S(2)}) %all-to-all-start.5) | async-done | bytes 1572896 | tf_op jit(solution)/shard_map/all_to_all | solution.py:1345
  299.0 4.7 %all-to-all-start.6 = ((bf16[8,256,768]{2,1,0:T(8,128)(2,1)}), bf16[8,256,768]{2,1,0:T(8,128)(2,1)}, u32[]{:S(2)}, u32[]{:S(2)}) async-start(bf16[8,256,768]{2,1,0:T(8,128)(2,1)} %get-tuple-element.203), calls=%async_computation.7 | async-start | bytes 6291456 | tf_op jit(solution)/shard_map/all_to_all | solution.py:1345
  303.7 38.3 %attention_backward.1 = (f32[4,197,768]{2,1,0:T(8,128)}, bf16[2,192,1536]{2,1,0:T(8,128)(2,1)}, bf16[2,192,1536]{2,1,0:T(8,128)(2,1)}, bf16[2,192,1664]{2,1,0:T(8,128)(2,1)}, bf16[2,192,1664]{2,1,0:T(8,128)(2,1)}) custom-call(s32[1]{0:T(128)} %bitcast.2.core_ref, bf16[4,197,768]{2,1,0:T(8,128)(2,1)} %copy-done.9, bf16[4,197,768]{2,1,0:T(8,128)(2,1)} %copy-done.1, ...), custom_call_target="tpu_custom_call" | custom-call | flops 40000000000 | bytes 40000000 | tf_op jit(solution)/shard_map/attention_backward/pallas_call | solution.py:1163
  342.5 4.4 %collective-permute-done.11.refs_3_ = bf16[2,192,1536]{2,1,0:T(8,128)(2,1)S(1)} collective-permute-done((bf16[2,192,1536]{2,1,0:T(8,128)(2,1)}, bf16[2,192,1536]{2,1,0:T(8,128)(2,1)S(1)}, u32[]{:S(2)}, u32[]{:S(2)}) %collective-permute-start.11) | collective-permute-done | bytes 1179680 | tf_op jit(solution)/shard_map/ppermute | solution.py:1266
  360.2 10.7 %collective-permute-done.13.refs_3_ = bf16[192,1536]{1,0:T(8,128)(2,1)} collective-permute-done((bf16[192,1536]{1,0:T(8,128)(2,1)}, bf16[192,1536]{1,0:T(8,128)(2,1)}, u32[]{:S(2)}, u32[]{:S(2)}) %collective-permute-start.13) | collective-permute-done | bytes 589856 | tf_op jit(solution)/shard_map/ppermute | solution.py:1266
  370.9 5.8 %collective-permute-done.14 = bf16[192,1664]{1,0:T(8,128)(2,1)S(1)} collective-permute-done((bf16[192,1664]{1,0:T(8,128)(2,1)}, bf16[192,1664]{1,0:T(8,128)(2,1)S(1)}, u32[]{:S(2)}, u32[]{:S(2)}) %collective-permute-start.14) | collective-permute-done | bytes 639008 | tf_op jit(solution)/shard_map/ppermute | solution.py:1266
  387.0 8.3 %combine_outputs.1 = bf16[4,197,768]{2,1,0:T(8,128)(2,1)S(1)} custom-call(f32[4,197,768]{2,1,0:T(8,128)S(1)} %copy-done.4, s32[4,197,8]{2,1,0:T(8,128)S(1)} %copy-done.20, f32[4,197,16]{2,1,0:T(8,128)S(1)} %copy-done.22, bf16[8,256,768]{2,1,0:T(8,128)(2,1)} %all-to-all-done.6.slots_ref), custom_call_target="tpu_custom_call" | custom-call | tf_op jit(solution)/shard_map/combine_outputs/pallas_call | solution.py:1242
  398.6 4.3 %expert_gradients.3 = (f32[2,768,768]{2,1,0:T(8,128)}, f32[2,192,3072]{2,1,0:T(8,128)}, f32[2,16,768]{2,1,0:T(8,128)S(1)}) custom-call(bf16[1552,768]{1,0:T(8,128)(2,1)S(1)} %get-tuple-element.211.refs_0_.refs_1_.refs_2_, ...), custom_call_target="tpu_custom_call", output_to_operand_aliasing={{0}: (6, {}), {1}: (7, {}), {2}: (8, {})} | custom-call | tf_op jit(solution)/shard_map/expert_gradients/pallas_call | solution.py:835
  (182 shorter events, 108.6 us)
Async XLA Ops:
  8.9 9.2 %collective-permute-start = (bf16[24,1536]{1,0:T(8,128)(2,1)}, bf16[24,1536]{1,0:T(8,128)(2,1)S(1)}, u32[]{:S(2)}, u32[]{:S(2)}) collective-permute-start(bf16[24,1536]{1,0:T(8,128)(2,1)} %get-tuple-element.141), channel_id=1, source_target_pairs={{0,4},{1,5},{2,6},{3,7},{4,0},{5,1},{6,2},{7,3},{8,12},{9,13},{10,... | collective-permute-start | bytes 221192 | tf_op jit(solution)/shard_map/ppermute | solution.py:1266
  28.1 16.8 %collective-permute-start.4 = (bf16[2,2,24,1536]{3,2,0,1:T(8,128)(2,1)S(1)}, bf16[2,2,24,1536]{3,2,0,1:T(8,128)(2,1)}, u32[]{:S(2)}, u32[]{:S(2)}) collective-permute-start(bf16[2,2,24,1536]{3,2,0,1:T(8,128)(2,1)S(1)} %pad_maximum_fusion.7), channel_id=1, source_target_pairs={{0,1},{1,0},{2,3},{3,2},{4,5},{5,4},{6,7},{7,6},{8,9},{9,8},{10,11... | collective-permute-start | bytes 884744 | tf_op jit(solution)/shard_map/ppermute | solution.py:1266
  37.6 41.8 %all-to-all-start = ((bf16[8,128,768]{2,1,0:T(8,128)(2,1)}), bf16[8,128,768]{2,1,0:T(8,128)(2,1)}, u32[]{:S(2)}, u32[]{:S(2)}) async-start(bf16[8,128,768]{2,1,0:T(8,128)(2,1)} %fill_slots.4), calls=%async_computation | async-start | bytes 3145728 | tf_op jit(solution)/shard_map/all_to_all | solution.py:1345
  43.2 125.1 %all-gather.5.cloned.1.call-start = ((), (), s32[]{:S(2)}) async-start(), calls=%async_computation.9 | async-start | bytes 11919360 | tf_op jit(solution)/shard_map/all_gather | solution.py:1377
  43.3 8.0 %collective-permute-start.5 = (bf16[2,2,24,1664]{3,2,0,1:T(8,128)(2,1)S(1)}, bf16[2,2,24,1664]{3,2,0,1:T(8,128)(2,1)S(1)}, u32[]{:S(2)}, u32[]{:S(2)}) collective-permute-start(bf16[2,2,24,1664]{3,2,0,1:T(8,128)(2,1)S(1)} %pad_maximum_fusion.6), channel_id=1, source_target_pairs={{0,16},{8,24},{16,0},{24,8},{1,17},{9,25},{17,1},{25,9},{2,18},{10... | collective-permute-start | bytes 958472 | tf_op jit(solution)/shard_map/ppermute | solution.py:1266
  55.3 13.0 %collective-permute-start.6 = (bf16[2,2,2,24,1536]{4,3,0,1,2:T(8,128)(2,1)S(1)}, bf16[2,2,2,24,1536]{4,3,0,1,2:T(8,128)(2,1)S(1)}, u32[]{:S(2)}, u32[]{:S(2)}) collective-permute-start(bf16[2,2,2,24,1536]{4,3,0,1,2:T(8,128)(2,1)S(1)} %pad_maximum_fusion.5), channel_id=1, source_target_pairs={{0,16},{8,24},{16,0},{24,8},{1,17},{9,25},{17,1},{25,9},{2,18},{10... | collective-permute-start | bytes 1769480 | tf_op jit(solution)/shard_map/ppermute | solution.py:1266
  56.9 20.9 %collective-permute-start.7 = (bf16[2,2,2,24,1664]{4,3,1,2,0:T(8,128)(2,1)S(1)}, bf16[2,2,2,24,1664]{4,3,1,2,0:T(8,128)(2,1)S(1)}, u32[]{:S(2)}, u32[]{:S(2)}) collective-permute-start(bf16[2,2,2,24,1664]{4,3,1,2,0:T(8,128)(2,1)S(1)} %pad_maximum_fusion.4), channel_id=1, source_target_pairs={{0,1},{1,0},{2,3},{3,2},{4,5},{5,4},{6,7},{7,6},{8,9},{9,8},{10,11... | collective-permute-start | bytes 1916936 | tf_op jit(solution)/shard_map/ppermute | solution.py:1266
  79.5 135.1 %all-gather.7.cloned.1.call-start = ((), (), s32[]{:S(2)}) async-start(), calls=%async_computation.10 | async-start | bytes 11919360 | tf_op jit(solution)/shard_map/all_gather | solution.py:1377
  80.2 8.0 %collective-permute-start.9 = (bf16[2,192,1664]{2,1,0:T(8,128)(2,1)S(1)}, bf16[2,192,1664]{2,1,0:T(8,128)(2,1)}, u32[]{:S(2)}, u32[]{:S(2)}) collective-permute-start(bf16[2,192,1664]{2,1,0:T(8,128)(2,1)S(1)} %bitcast.90), channel_id=1, source_target_pairs={{0,8},{8,0},{16,24},{24,16},{1,9},{9,1},{17,25},{25,17},{2,10},{10... | collective-permute-start | bytes 3833864 | tf_op jit(solution)/shard_map/ppermute | solution.py:1266
  80.3 42.7 %all-to-all-start.1 = ((bf16[8,128,768]{2,1,0:T(8,128)(2,1)}), bf16[8,128,768]{2,1,0:T(8,128)(2,1)}, u32[]{:S(2)}, u32[]{:S(2)}) async-start(bf16[8,128,768]{2,1,0:T(8,128)(2,1)} %fill_slots.5), calls=%async_computation.1 | async-start | bytes 3145728 | tf_op jit(solution)/shard_map/all_to_all | solution.py:1345
  123.0 41.5 %all-to-all-start.2 = ((bf16[8,128,768]{2,1,0:T(8,128)(2,1)}), bf16[8,128,768]{2,1,0:T(8,128)(2,1)}, u32[]{:S(2)}, u32[]{:S(2)}) async-start(bf16[8,128,768]{2,1,0:T(8,128)(2,1)} %fill_slots.6), calls=%async_computation.2 | async-start | bytes 3145728 | tf_op jit(solution)/shard_map/all_to_all | solution.py:1345
  164.5 42.7 %all-to-all-start.3 = ((bf16[8,128,768]{2,1,0:T(8,128)(2,1)}), bf16[8,128,768]{2,1,0:T(8,128)(2,1)S(1)}, u32[]{:S(2)}, u32[]{:S(2)}) async-start(bf16[8,128,768]{2,1,0:T(8,128)(2,1)} %fill_slots.7), calls=%async_computation.3 | async-start | bytes 3145728 | tf_op jit(solution)/shard_map/all_to_all | solution.py:1345
  168.1 187.9 %reduce-scatter.2.cloned.1.call-start = ((), (), s32[]{:S(2)}) async-start(), calls=%async_computation.8 | async-start | bytes 11919360 | tf_op jit(solution)/shard_map/reduce_scatter | solution.py:1399
  208.4 45.1 %all-to-all-start.4 = ((bf16[8,128,768]{2,1,0:T(8,128)(2,1)}), bf16[8,128,768]{2,1,0:T(8,128)(2,1)S(1)}, u32[]{:S(2)}, u32[]{:S(2)}) async-start(bf16[8,128,768]{2,1,0:T(8,128)(2,1)} %get-tuple-element.172), calls=%async_computation.4 | async-start | bytes 3145728 | tf_op jit(solution)/shard_map/all_to_all | solution.py:1345
  253.5 15.7 %collective-permute-start.10 = (bf16[2,1552,768]{2,1,0:T(8,128)(2,1)}, bf16[2,1552,768]{2,1,0:T(8,128)(2,1)}, u32[]{:S(2)}, u32[]{:S(2)}) collective-permute-start(bf16[2,1552,768]{2,1,0:T(8,128)(2,1)} %get-tuple-element.182), channel_id=1, source_target_pairs={{0,8},{8,0},{16,24},{24,16},{1,9},{9,1},{17,25},{25,17},{2,10},{10... | collective-permute-start | bytes 14303240 | tf_op jit(solution)/shard_map/ppermute | solution.py:1266
  253.6 43.8 %all-to-all-start.5 = ((bf16[8,128,768]{2,1,0:T(8,128)(2,1)}), bf16[8,128,768]{2,1,0:T(8,128)(2,1)}, u32[]{:S(2)}, u32[]{:S(2)}) async-start(bf16[8,128,768]{2,1,0:T(8,128)(2,1)} %get-tuple-element.183), calls=%async_computation.5 | async-start | bytes 3145728 | tf_op jit(solution)/shard_map/all_to_all | solution.py:1345
  297.4 80.2 %collective-permute-start.15 = (bf16[1552,768]{1,0:T(8,128)(2,1)}, bf16[1552,768]{1,0:T(8,128)(2,1)}, u32[]{:S(2)}, u32[]{:S(2)}) collective-permute-start(bf16[1552,768]{1,0:T(8,128)(2,1)} %get-tuple-element.193), channel_id=1, source_target_pairs={{0,16},{8,24},{16,0},{24,8},{1,17},{9,25},{17,1},{25,9},{2,18},{10... | collective-permute-start | bytes 7151624 | tf_op jit(solution)/shard_map/ppermute | solution.py:1266
  299.0 85.3 %all-to-all-start.6 = ((bf16[8,256,768]{2,1,0:T(8,128)(2,1)}), bf16[8,256,768]{2,1,0:T(8,128)(2,1)}, u32[]{:S(2)}, u32[]{:S(2)}) async-start(bf16[8,256,768]{2,1,0:T(8,128)(2,1)} %get-tuple-element.203), calls=%async_computation.7 | async-start | bytes 6291456 | tf_op jit(solution)/shard_map/all_to_all | solution.py:1345
  353.6 23.2 %collective-permute-start.14 = (bf16[192,1664]{1,0:T(8,128)(2,1)}, bf16[192,1664]{1,0:T(8,128)(2,1)S(1)}, u32[]{:S(2)}, u32[]{:S(2)}) collective-permute-start(bf16[192,1664]{1,0:T(8,128)(2,1)} %get-tuple-element.192), channel_id=1, source_target_pairs={{0,1},{1,0},{2,3},{3,2},{4,5},{5,4},{6,7},{7,6},{8,9},{9,8},{10,11... | collective-permute-start | bytes 1916936 | tf_op jit(solution)/shard_map/ppermute | solution.py:1266
  355.5 15.4 %collective-permute-start.13 = (bf16[192,1536]{1,0:T(8,128)(2,1)}, bf16[192,1536]{1,0:T(8,128)(2,1)}, u32[]{:S(2)}, u32[]{:S(2)}) collective-permute-start(bf16[192,1536]{1,0:T(8,128)(2,1)} %get-tuple-element.191), channel_id=1, source_target_pairs={{0,16},{8,24},{16,0},{24,8},{1,17},{9,25},{17,1},{25,9},{2,18},{10... | collective-permute-start | bytes 1769480 | tf_op jit(solution)/shard_map/ppermute | solution.py:1266
  381.5 13.8 %collective-permute-start.17 = (bf16[96,1664]{1,0:T(8,128)(2,1)}, bf16[96,1664]{1,0:T(8,128)(2,1)}, u32[]{:S(2)}, u32[]{:S(2)}) collective-permute-start(bf16[96,1664]{1,0:T(8,128)(2,1)} %get-tuple-element.202), channel_id=1, source_target_pairs={{0,16},{8,24},{16,0},{24,8},{1,17},{9,25},{17,1},{25,9},{2,18},{10... | collective-permute-start | bytes 958472 | tf_op jit(solution)/shard_map/ppermute | solution.py:1266
  381.9 13.3 %collective-permute-start.16 = (bf16[96,1536]{1,0:T(8,128)(2,1)}, bf16[96,1536]{1,0:T(8,128)(2,1)}, u32[]{:S(2)}, u32[]{:S(2)}) collective-permute-start(bf16[96,1536]{1,0:T(8,128)(2,1)} %get-tuple-element.201), channel_id=1, source_target_pairs={{0,1},{1,0},{2,3},{3,2},{4,5},{5,4},{6,7},{7,6},{8,9},{9,8},{10,11... | collective-permute-start | bytes 884744 | tf_op jit(solution)/shard_map/ppermute | solution.py:1266
  396.5 8.0 %collective-permute-start.19 = (bf16[48,1664]{1,0:T(8,128)(2,1)S(1)}, bf16[48,1664]{1,0:T(8,128)(2,1)S(1)}, u32[]{:S(2)}, u32[]{:S(2)}) collective-permute-start(bf16[48,1664]{1,0:T(8,128)(2,1)S(1)} %get-tuple-element.210), channel_id=1, source_target_pairs={{0,2},{1,3},{2,0},{3,1},{4,6},{5,7},{6,4},{7,5},{8,10},{9,11},{10,... | collective-permute-start | bytes 479240 | tf_op jit(solution)/shard_map/ppermute | solution.py:1266
  404.6 9.0 %collective-permute-start.21 = (bf16[24,1664]{1,0:T(8,128)(2,1)S(1)}, bf16[24,1664]{1,0:T(8,128)(2,1)S(1)}, u32[]{:S(2)}, u32[]{:S(2)}) collective-permute-start(bf16[24,1664]{1,0:T(8,128)(2,1)S(1)} %get-tuple-element.228), channel_id=1, source_target_pairs={{0,4},{1,5},{2,6},{3,7},{4,0},{5,1},{6,2},{7,3},{8,12},{9,13},{10,... | collective-permute-start | bytes 239624 | tf_op jit(solution)/shard_map/ppermute | solution.py:1266
  (47 other events, 529.0 us)
Sparse Core Ops, SparseCore 0:
  79.6 63.8 all-gather.4
  145.6 64.7 all-gather.6
  213.0 79.0 reduce-scatter.1

commit v4 on v3

--- a/solution.py
+++ b/solution.py
@@ -61,13 +61,25 @@
 def load_weights(step, core, parts, scratch, sems):
     copies = []
     for k, (own, other) in enumerate(parts):
-        copies.append(pltpu.make_async_copy(own, scratch[k].at[:, core], sems.at[2 * k]))
-        copies.append(pltpu.make_async_copy(other, scratch[k].at[:, 1 - core], sems.at[2 * k + 1]))
+        copies.append(
+            [
+                pltpu.make_async_copy(own, scratch[k].at[:, core], sems.at[2 * k]),
+                pltpu.make_async_copy(other, scratch[k].at[:, 1 - core], sems.at[2 * k + 1]),
+            ]
+        )
 
     @pl.when(step == 0)
     def _():
-        for copy in copies:
-            copy.start()
+        for pair in reversed(copies):
+            for copy in pair:
+                copy.start()
+
+    return copies
+
+
+def arrive(step, copies):
+    @pl.when(step == 0)
+    def _():
         for copy in copies:
             copy.wait()
 
@@ -77,9 +89,11 @@
     own, width = out_ref.shape
     labels = router_ref.shape[0]
     local = labels // owners
-    one_ref[...] = qkv_ref[:, 0 : 2 * width].astype(bf16)
-    two_ref[:, 0:width] = qkv_ref[:, 2 * width :].astype(bf16)
-    two_ref[:, width : 2 * width] = out_ref[...].astype(bf16)
+    cut = one_ref.shape[1]
+    rest = 3 * width - cut
+    one_ref[...] = qkv_ref[:, 0:cut].astype(bf16)
+    two_ref[:, 0:rest] = qkv_ref[:, cut:].astype(bf16)
+    two_ref[:, rest : rest + width] = out_ref[...].astype(bf16)
     lines = [
         router_ref[o * local + l : o * local + l + 1, :] for l in range(local) for o in range(owners)
     ]
@@ -88,16 +102,17 @@
     small = jnp.concatenate(lines, axis=0)
     if own < LANES:
         small = jnp.concatenate([small, jnp.zeros((LANES, LANES - own), f32)], axis=1)
-    two_ref[:, 2 * width :] = jnp.transpose(small)[0:own].astype(bf16)
+    two_ref[:, rest + width :] = jnp.transpose(small)[0:own].astype(bf16)
 
 
 def pack(w_qkv, w_out, w_router, vectors, owners):
     own, width = w_out.shape
+    cut = 2 * width
     return pl.pallas_call(
         functools.partial(pack_kernel, owners),
         out_shape=[
-            jax.ShapeDtypeStruct((own, 2 * width), bf16),
-            jax.ShapeDtypeStruct((own, 2 * width + LANES), bf16),
+            jax.ShapeDtypeStruct((own, cut), bf16),
+            jax.ShapeDtypeStruct((own, 4 * width - cut + LANES), bf16),
         ],
         name="pack_weights",
     )(w_qkv, w_out, w_router.T, *[vector.reshape(1, own) for vector in vectors])
@@ -111,10 +126,12 @@
     local = labels // owners
     one = one_ref[...] + one_in[...].astype(f32)
     two = two_ref[...] + two_in[...].astype(f32)
-    qkv_ref[:, 0 : 2 * width] = one
-    qkv_ref[:, 2 * width :] = two[:, 0:width]
-    out_ref[...] = two[:, width : 2 * width]
-    small = two[:, 2 * width :]
+    cut = one.shape[1]
+    rest = 3 * width - cut
+    qkv_ref[:, 0:cut] = one
+    qkv_ref[:, cut:] = two[:, 0:rest]
+    out_ref[...] = two[:, rest : rest + width]
+    small = two[:, rest + width :]
     if own < LANES:
         small = jnp.concatenate([small, jnp.zeros((LANES - own, LANES), f32)], axis=0)
     small = jnp.transpose(small)[:, 0:own]
@@ -128,7 +145,7 @@
 
 def dense_out(one, two, labels, owners):
     own = one[0].shape[0]
-    width = one[0].shape[1] // 2
+    width = (one[0].shape[1] + two[0].shape[1] - LANES) // 4
     return pl.pallas_call(
         functools.partial(dense_out_kernel, owners),
         out_shape=[
@@ -285,20 +302,24 @@
     _, length, width = tokens_ref.shape
     step = pl.program_id(0)
     parts = ((one_own, one_other), (two_own, two_other))
-    load_weights(step, core_ref[0], parts, (one_ref, two_ref), sems)
+    copies = load_weights(step, core_ref[0], parts, (one_ref, two_ref), sems)
+    cut = one_ref.shape[-1]
+    rest = 3 * width - cut
+    rows = tokens_ref[0].astype(f32)
+    unit, _ = norm_parts(rows)
+    arrive(step, copies[1])
 
     @pl.when(step == 0)
     def _():
-        misc_ref[...] = jnp.transpose(two_ref[..., 2 * width :].reshape(width, LANES))
+        misc_ref[...] = jnp.transpose(two_ref[..., rest + width :].reshape(width, LANES))
 
     vec = [misc_ref[labels + k : labels + k + 1, :].astype(f32) for k in range(VECTORS)]
-    rows = tokens_ref[0].astype(f32)
-    unit, _ = norm_parts(rows)
     normed = (unit * vec[0] + vec[1]).astype(bf16)
+    arrive(step, copies[0])
     projected = jnp.concatenate(
         [
-            dot(normed, one_ref[...].reshape(width, 2 * width)).astype(bf16),
-            dot(normed, two_ref[..., 0:width].reshape(width, width)).astype(bf16),
+            dot(normed, one_ref[...].reshape(width, cut)).astype(bf16),
+            dot(normed, two_ref[..., 0:rest].reshape(width, rest)).astype(bf16),
         ],
         axis=1,
     )
@@ -329,7 +350,7 @@
     mixed = jnp.concatenate(pieces, axis=1)
     mixed_ref[0] = mixed
     lse_ref[0] = jnp.transpose(total_ref[...])[0:16]
-    w_out = two_ref[..., width : 2 * width].reshape(width, width)
+    w_out = two_ref[..., rest : rest + width].reshape(width, width)
     first = rows + dot(mixed, w_out) + vec[2]
     first_ref[0] = first
     unit, _ = norm_parts(first)
@@ -1056,13 +1077,11 @@
     _, length, width = tokens_ref.shape
     step = pl.program_id(0)
     parts = ((one_own, one_other), (two_own, two_other))
-    load_weights(step, core_ref[0], parts, (one_ref, two_ref), sems)
-
-    @pl.when(step == 0)
-    def _():
-        misc_ref[...] = jnp.transpose(two_ref[..., 2 * width :].reshape(width, LANES))
-
-    vec = [misc_ref[labels + k : labels + k + 1, :].astype(f32) for k in range(VECTORS)]
+    copies = load_weights(step, core_ref[0], parts, (one_ref, two_ref), sems)
+    cut = one_ref.shape[-1]
+    rest = 3 * width - cut
+    grad_cut = grad_one_ref.shape[-1]
+    grad_rest = 3 * width - grad_cut
 
     @pl.when(step == 0)
     def _():
@@ -1078,6 +1097,13 @@
     picked = picked + picked_ref[0]
     gate_one = gate_one + scores_ref[0, :, 0:1]
     gate_two = gate_two + scores_ref[0, :, 1:2]
+    arrive(step, copies[1])
+
+    @pl.when(step == 0)
+    def _():
+        misc_ref[...] = jnp.transpose(two_ref[..., rest + width :].reshape(width, LANES))
+
+    vec = [misc_ref[labels + k : labels + k + 1, :].astype(f32) for k in range(VECTORS)]
     label = iota((length, labels), 1)
     grad_gates = jnp.where(label == route_one, gate_one, 0.0) + jnp.where(
         label == route_two, gate_two, 0.0
@@ -1095,8 +1121,8 @@
     grad_first = cot + norm_backward(grad_routed, unit, scale, vec[3])
     vec_ref[2:3, :] += jnp.sum(grad_first, axis=0, keepdims=True)
     first_low = grad_first.astype(bf16)
-    add_to(grad_two_ref, slice(width, 2 * width), dot_tn(mixed_ref[0], first_low))
-    w_out = two_ref[..., width : 2 * width].reshape(width, width)
+    add_to(grad_two_ref, slice(grad_rest, grad_rest + width), dot_tn(mixed_ref[0], first_low))
+    w_out = two_ref[..., rest : rest + width].reshape(width, width)
     grad_mixed = dot_nt(first_low, w_out).astype(bf16)
     low_half = iota((length, LANES), 1) < HEAD_DIM
     rate = jnp.asarray(HEAD_DIM**-0.5, bf16)
@@ -1128,15 +1154,15 @@
         grads[0].append((grad_q * HEAD_DIM**-0.5).astype(bf16))
         grads[1].append(grad_k.astype(bf16))
         grads[2].append(grad_v.astype(bf16))
-    grad_one = jnp.concatenate(grads[0] + grads[1], axis=1)
-    grad_two = jnp.concatenate(grads[2], axis=1)
+    grad_qkv = jnp.concatenate(grads[0] + grads[1] + grads[2], axis=1)
     rows = tokens_ref[0].astype(f32)
     unit, scale = norm_parts(rows)
     normed = (unit * vec[0] + vec[1]).astype(bf16)
-    add_to(grad_one_ref, slice(None), dot_tn(normed, grad_one))
-    add_to(grad_two_ref, slice(0, width), dot_tn(normed, grad_two))
-    grad_normed = dot_nt(grad_one, one_ref[...].reshape(width, 2 * width))
-    grad_normed += dot_nt(grad_two, two_ref[..., 0:width].reshape(width, width))
+    add_to(grad_one_ref, slice(None), dot_tn(normed, grad_qkv[:, 0:grad_cut]))
+    add_to(grad_two_ref, slice(0, grad_rest), dot_tn(normed, grad_qkv[:, grad_cut:]))
+    arrive(step, copies[0])
+    grad_normed = dot_nt(grad_qkv[:, 0:cut], one_ref[...].reshape(width, cut))
+    grad_normed += dot_nt(grad_qkv[:, cut:], two_ref[..., 0:rest].reshape(width, rest))
     vec_ref[0:1, :] += jnp.sum(grad_normed * unit, axis=0, keepdims=True)
     vec_ref[1:2, :] += jnp.sum(grad_normed, axis=0, keepdims=True)
     grad_tokens_ref[0] = grad_first + norm_backward(grad_normed, unit, scale, vec[0])
@@ -1144,7 +1170,7 @@
     @pl.when(step == pl.num_programs(0) - 1)
     def _():
         stack_ref[labels : labels + 8, :] = vec_ref[...]
-        add_to(grad_two_ref, slice(2 * width, None), jnp.transpose(stack_ref[...]))
+        add_to(grad_two_ref, slice(grad_rest + width, None), jnp.transpose(stack_ref[...]))
         mine, other = core_ref[0], 1 - core_ref[0]
         keep_one_ref[...] = grad_one_ref[:, mine].astype(bf16)
         keep_two_ref[...] = grad_two_ref[:, mine].astype(bf16)
@@ -1158,7 +1184,9 @@
     images, length, width = tokens.shape
     owners, capp, _ = slots.shape
     whole = lambda *tail: pl.BlockSpec((1, *tail), lambda i: (i, *[0] * len(tail)))
-    shapes = [part[0].shape for part in packed]
+    spare = sum(part[0].shape[2] for part in packed)
+    grad_cut = 2 * width + width // 3 // LANES * LANES
+    shapes = [(*packed[0][0].shape[:2], count) for count in (grad_cut, spare - grad_cut)]
     still = lambda shape: pl.BlockSpec(shape, lambda i: (0, 0, 0))
     return pl.pallas_call(
         functools.partial(backward_kernel, labels, local, cap),
@@ -1347,8 +1375,7 @@
     slices = [spread(block, near[:1], near[1:], order_of_hops, sizes) for block in slices]
     haves = [have for _, have in slices]
     rows, *slices = lax.optimization_barrier((rows, *[block for block, _ in slices]))
-    cots = [dispatch(rows, cotangent, None, cap, capp, owners, [l]) for l in range(local)]
-    cots[0] = exchange(cots[0])
+    cots = [exchange(dispatch(rows, cotangent, None, cap, capp, owners, [0]))]
     columns = [block.shape[-1] for block in slices]
     halves = []
     for turn in range(len(outer) + 1):
@@ -1358,7 +1385,10 @@
             block, haves[k] = spread(slices[k], haves[k], [hop], order_of_hops, sizes)
             moved.append(block)
         if turn == 0:
-            w_in, w_back, *moved = lax.optimization_barrier((w_in, w_back, *moved))
+            w_in, w_back, rows, *moved = lax.optimization_barrier((w_in, w_back, rows, *moved))
+            cots += [
+                dispatch(rows, cotangent, None, cap, capp, owners, [l]) for l in range(1, local)
+            ]
         slices = moved
     halves = [
         block.reshape(groups // 2, owners * own, count) for block, count in zip(slices, columns)

time: 431 us -> 424 us (0.984)
  waiting for transfers between devices: 118 us -> 110 us
    ppermute x22, waiting for transfers between devices: 52.4 us -> 47 us  [swap(): lax.ppermute(block, axis, [(d, d ^ 1 << bit) for d in range(sizes[axis])])]
    unnamed x84 -> x86, local copies, waits for them, and re-layouts: 30 us -> 29.1 us
  transfers between devices with their start and end apart: 32 -> 32, of which waited for: 16 -> 15; matrix products, arithmetic and copies ran while one was open for 6% -> 6% of each run, Pallas kernels for 41% -> 42%
where the time goes in v4:
time: 424 us; the launch traced here: 416 us
  Pallas kernels  178 us (42%)
  waiting for transfers between devices  110 us (26%)
  starting transfers between devices  63.9 us (15%)
  local copies, waits for them, and re-layouts  31.7 us (7%)
  other arithmetic  17.5 us (4%)
  between operations  14.9 us (4%)
    all_to_all x7, waiting for transfers between devices, per_device(): exchange = lambda block: lax.all_to_all(block, 'expert', 0, 0, tiled=True)  62.6 us
    ppermute x22, waiting for transfers between devices, swap(): lax.ppermute(block, axis, [(d, d ^ 1 << bit) for d in range(sizes[axis])])  47 us
    pallas_call x1, Pallas kernels, expert(): pl.pallas_call(functools.partial(expert_kernel, cap), grid=(groups,), in_...  38.9 us
    pallas_call x1, Pallas kernels, parted_expert(): pl.pallas_call(functools.partial(parted_kernel, cap), grid=(groups,), in_...  38.9 us
    pallas_call x1, Pallas kernels, backward(): pl.pallas_call(functools.partial(backward_kernel, labels, local, cap), gr...  38 us
    all_to_all x7, starting transfers between devices, per_device(): exchange = lambda block: lax.all_to_all(block, 'expert', 0, 0, tiled=True)  36 us
    unnamed x86, local copies, waits for them, and re-layouts  29.1 us
    ppermute x22, starting transfers between devices, swap(): lax.ppermute(block, axis, [(d, d ^ 1 << bit) for d in range(sizes[axis])])  27.6 us
  transfers between devices with their start and end apart: 32, of which 15 were waited for; matrix products, arithmetic and copies ran while one was open for 6% of the time, Pallas kernels for 42%

profile of v4, /device:TPU:0, one launch (start us, length us, event | category | flops | bytes accessed | tf_op | source)
XLA Modules:
  0.0 416.0 jit_solution(9040020997189008098)
XLA Ops:
  33.3 5.6 %all-to-all-start = ((bf16[8,128,768]{2,1,0:T(8,128)(2,1)}), bf16[8,128,768]{2,1,0:T(8,128)(2,1)}, u32[]{:S(2)}, u32[]{:S(2)}) async-start(bf16[8,128,768]{2,1,0:T(8,128)(2,1)} %fill_slots.4), calls=%async_computation | async-start | bytes 3145728 | tf_op jit(solution)/shard_map/all_to_all | solution.py:1373
  41.7 5.3 %collective-permute-done.5 = bf16[2,2,24,1664]{3,2,0,1:T(8,128)(2,1)S(1)} collective-permute-done((bf16[2,2,24,1664]{3,2,0,1:T(8,128)(2,1)S(1)}, bf16[2,2,24,1664]{3,2,0,1:T(8,128)(2,1)S(1)}, u32[]{:S(2)}, u32[]{:S(2)}) %collective-permute-start.5) | collective-permute-done | bytes 319520 | tf_op jit(solution)/shard_map/ppermute | solution.py:1294
  60.0 7.0 %collective-permute-done.6 = bf16[2,2,2,24,1536]{4,3,0,1,2:T(8,128)(2,1)S(1)} collective-permute-done((bf16[2,2,2,24,1536]{4,3,0,1,2:T(8,128)(2,1)S(1)}, bf16[2,2,2,24,1536]{4,3,0,1,2:T(8,128)(2,1)S(1)}, u32[]{:S(2)}, u32[]{:S(2)}) %collective-permute-start.6) | collective-permute-done | bytes 589856 | tf_op jit(solution)/shard_map/ppermute | solution.py:1294
  67.3 7.3 %collective-permute-done.7 = bf16[2,2,2,24,1664]{4,3,1,2,0:T(8,128)(2,1)S(1)} collective-permute-done((bf16[2,2,2,24,1664]{4,3,1,2,0:T(8,128)(2,1)S(1)}, bf16[2,2,2,24,1664]{4,3,1,2,0:T(8,128)(2,1)S(1)}, u32[]{:S(2)}, u32[]{:S(2)}) %collective-permute-start.7) | collective-permute-done | bytes 639008 | tf_op jit(solution)/shard_map/ppermute | solution.py:1294
  76.0 5.6 %all-to-all-start.1 = ((bf16[8,128,768]{2,1,0:T(8,128)(2,1)}), bf16[8,128,768]{2,1,0:T(8,128)(2,1)}, u32[]{:S(2)}, u32[]{:S(2)}) async-start(bf16[8,128,768]{2,1,0:T(8,128)(2,1)} %fill_slots.5), calls=%async_computation.1 | async-start | bytes 3145728 | tf_op jit(solution)/shard_map/all_to_all | solution.py:1373
  84.7 16.8 %attention_forward.1 = (bf16[4,197,2304]{2,1,0:T(8,128)(2,1)}, bf16[4,197,768]{2,1,0:T(8,128)(2,1)S(1)}, f32[4,16,256]{2,1,0:T(8,128)S(1)}, f32[4,197,768]{2,1,0...) custom-call(s32[1]{0:T(128)} %bitcast.2.core_ref, ...), custom_call_target="tpu_custom_call" | custom-call | flops 16000000000 | bytes 20000000 | tf_op jit(solution)/shard_map/attention_forward/pallas_call | solution.py:385
  104.8 4.4 %fill_slots.6 = bf16[8,128,768]{2,1,0:T(8,128)(2,1)} custom-call(s32[4,8,197]{2,1,0:T(8,128)S(1)} %get-tuple-element.147.rows_ref, bf16[4,197,768]{2,1,0:T(8,128)(2,1)S(1)} %get-tuple-element.158.value_ref.routed_ref, bf16[4,16,197]{2,1,0:T(8,128)(2,1)S(1)} %get-tuple-element.159.refs_0_), custom_call_target="tpu_custom_call" | custom-call | tf_op jit(solution)/shard_map/fill_slots/pallas_call | solution.py:272
  109.2 10.1 %all-to-all-done.1.cot_ref = bf16[8,128,768]{2,1,0:T(8,128)(2,1)} async-done(((bf16[8,128,768]{2,1,0:T(8,128)(2,1)}), bf16[8,128,768]{2,1,0:T(8,128)(2,1)}, u32[]{:S(2)}, u32[]{:S(2)}) %all-to-all-start.1) | async-done | bytes 1572896 | tf_op jit(solution)/shard_map/all_to_all | solution.py:1373
  119.3 4.3 %all-to-all-start.2 = ((bf16[8,128,768]{2,1,0:T(8,128)(2,1)}), bf16[8,128,768]{2,1,0:T(8,128)(2,1)}, u32[]{:S(2)}, u32[]{:S(2)}) async-start(bf16[8,128,768]{2,1,0:T(8,128)(2,1)} %fill_slots.6), calls=%async_computation.2 | async-start | bytes 3145728 | tf_op jit(solution)/shard_map/all_to_all | solution.py:1373
  127.6 32.8 %all-to-all-done.2.rows_ref = bf16[8,128,768]{2,1,0:T(8,128)(2,1)} async-done(((bf16[8,128,768]{2,1,0:T(8,128)(2,1)}), bf16[8,128,768]{2,1,0:T(8,128)(2,1)}, u32[]{:S(2)}, u32[]{:S(2)}) %all-to-all-start.2) | async-done | bytes 1572896 | tf_op jit(solution)/shard_map/all_to_all | solution.py:1373
  164.3 38.9 %expert_rows.1 = (bf16[8,256,768]{2,1,0:T(8,128)(2,1)}, bf16[8,128,768]{2,1,0:T(8,128)(2,1)}, bf16[4,1552,768]{2,1,0:T(8,128)(2,1)}) custom-call(bf16[8,128,768]{2,1,0:T(8,128)(2,1)} %all-to-all-done.2.rows_ref, bf16[8,128,768]{2,1,0:T(8,128)(2,1)} %all-to-all-done.cot_ref, bf16[4,1552,768]{2,1,0:T(8,128)(2,1)} %bitcast.114, ...), custom_call_target="tpu_custom_call" | custom-call | flops 28991029248 | bytes 30000000 | tf_op jit(solution)/shard_map/expert_rows/pallas_call | solution.py:571
  204.4 6.2 %all-to-all-start.4 = ((bf16[8,128,768]{2,1,0:T(8,128)(2,1)}), bf16[8,128,768]{2,1,0:T(8,128)(2,1)S(1)}, u32[]{:S(2)}, u32[]{:S(2)}) async-start(bf16[8,128,768]{2,1,0:T(8,128)(2,1)} %get-tuple-element.174), calls=%async_computation.4 | async-start | bytes 3145728 | tf_op jit(solution)/shard_map/all_to_all | solution.py:1373
  210.6 38.9 %expert_rows_parted.1 = (bf16[8,256,768]{2,1,0:T(8,128)(2,1)}, bf16[8,128,768]{2,1,0:T(8,128)(2,1)}, bf16[2,1552,768]{2,1,0:T(8,128)(2,1)}, bf16[2,1552,768]{2,1,0:T(8,128)(2,1)}) custom-call(s32[1]{0:T(128)} %bitcast.2.core_ref, bf16[8,128,768]{2,1,0:T(8,128)(2,1)} %copy-done.32, ...), custom_call_target="tpu_custom_call", output_to_operand_aliasing={{0}: (6, {})} | custom-call | flops 28991029248 | bytes 30000000 | tf_op jit(solution)/shard_map/expert_rows_parted/pallas_call | solution.py:790
  249.6 6.0 %all-to-all-start.5 = ((bf16[8,128,768]{2,1,0:T(8,128)(2,1)}), bf16[8,128,768]{2,1,0:T(8,128)(2,1)}, u32[]{:S(2)}, u32[]{:S(2)}) async-start(bf16[8,128,768]{2,1,0:T(8,128)(2,1)} %get-tuple-element.185), calls=%async_computation.5 | async-start | bytes 3145728 | tf_op jit(solution)/shard_map/all_to_all | solution.py:1373
  257.9 5.0 %attention_again.1 = (f32[4,197,768]{2,1,0:T(8,128)S(1)}, f32[4,197,8]{2,1,0:T(8,128)S(1)}, bf16[4,12,197,197]{3,2,1,0:T(8,128)(2,1)S(1)}) custom-call(s32[4,197,8]{2,1,0:T(8,128)S(1)} %get-tuple-element.140.cols_ref, bf16[4,197,2304]{2,1,0:T(8,128)(2,1)S(1)} %copy-done.27, f32[4,16,256]{2,1,0:T(8,128)S(1)} %get-tuple-element.156.lse_ref, ...), custom_call_target="tpu_custom_call" | custom-call | flops 10000000000 | bytes 20000000 | tf_op jit(solution)/shard_map/attention_again/pallas_call | solution.py:1014
  265.2 6.9 %convert_add_fusion = bf16[2,1552,768]{2,1,0:T(8,128)(2,1)S(1)} fusion(bf16[2,1552,768]{2,1,0:T(8,128)(2,1)} %collective-permute-done.10, bf16[2,1552,768]{2,1,0:T(8,128)(2,1)} %get-tuple-element.183), kind=kLoop, calls=%fused_computation | loop fusion | flops 9535488 | bytes 14303232 | tf_op jit(solution)/shard_map/add | solution.py:1433
  273.8 19.6 %all-to-all-done.5.refs_0_ = bf16[8,128,768]{2,1,0:T(8,128)(2,1)} async-done(((bf16[8,128,768]{2,1,0:T(8,128)(2,1)}), bf16[8,128,768]{2,1,0:T(8,128)(2,1)}, u32[]{:S(2)}, u32[]{:S(2)}) %all-to-all-start.5) | async-done | bytes 1572896 | tf_op jit(solution)/shard_map/all_to_all | solution.py:1373
  294.3 4.7 %all-to-all-start.6 = ((bf16[8,256,768]{2,1,0:T(8,128)(2,1)}), bf16[8,256,768]{2,1,0:T(8,128)(2,1)}, u32[]{:S(2)}, u32[]{:S(2)}) async-start(bf16[8,256,768]{2,1,0:T(8,128)(2,1)} %get-tuple-element.205), calls=%async_computation.7 | async-start | bytes 6291456 | tf_op jit(solution)/shard_map/all_to_all | solution.py:1373
  299.0 38.0 %attention_backward.1 = (f32[4,197,768]{2,1,0:T(8,128)}, bf16[2,192,1792]{2,1,0:T(8,128)(2,1)}, bf16[2,192,1792]{2,1,0:T(8,128)(2,1)}, bf16[2,192,1408]{2,1,0:T(8,128)(2,1)}, bf16[2,192,1408]{2,1,0:T(8,128)(2,1)}) custom-call(s32[1]{0:T(128)} %bitcast.2.core_ref, bf16[4,197,768]{2,1,0:T(8,128)(2,1)} %copy-done.9, bf16[4,197,768]{2,1,0:T(8,128)(2,1)} %copy-done.1, ...), custom_call_target="tpu_custom_call" | custom-call | flops 40000000000 | bytes 40000000 | tf_op jit(solution)/shard_map/attention_backward/pallas_call | solution.py:1191
  337.6 4.4 %collective-permute-done.12 = bf16[2,192,1408]{2,1,0:T(8,128)(2,1)S(1)} collective-permute-done((bf16[2,192,1408]{2,1,0:T(8,128)(2,1)}, bf16[2,192,1408]{2,1,0:T(8,128)(2,1)S(1)}, u32[]{:S(2)}, u32[]{:S(2)}) %collective-permute-start.12) | collective-permute-done | bytes 1081376 | tf_op jit(solution)/shard_map/ppermute | solution.py:1294
  355.6 14.0 %collective-permute-done.14 = bf16[192,1408]{1,0:T(8,128)(2,1)} collective-permute-done((bf16[192,1408]{1,0:T(8,128)(2,1)}, bf16[192,1408]{1,0:T(8,128)(2,1)}, u32[]{:S(2)}, u32[]{:S(2)}) %collective-permute-start.14) | collective-permute-done | bytes 540704 | tf_op jit(solution)/shard_map/ppermute | solution.py:1294
  380.4 8.3 %combine_outputs.1 = bf16[4,197,768]{2,1,0:T(8,128)(2,1)S(1)} custom-call(f32[4,197,768]{2,1,0:T(8,128)S(1)} %copy-done.4, s32[4,197,8]{2,1,0:T(8,128)S(1)} %copy-done.18, f32[4,197,16]{2,1,0:T(8,128)S(1)} %copy-done.20, bf16[8,256,768]{2,1,0:T(8,128)(2,1)} %all-to-all-done.6.slots_ref), custom_call_target="tpu_custom_call" | custom-call | tf_op jit(solution)/shard_map/combine_outputs/pallas_call | solution.py:1270
  391.1 4.3 %expert_gradients.3 = (f32[2,768,768]{2,1,0:T(8,128)}, f32[2,192,3072]{2,1,0:T(8,128)}, f32[2,16,768]{2,1,0:T(8,128)S(1)}) custom-call(bf16[1552,768]{1,0:T(8,128)(2,1)S(1)} %get-tuple-element.213.refs_0_.refs_1_.refs_2_, ...), custom_call_target="tpu_custom_call", output_to_operand_aliasing={{0}: (6, {}), {1}: (7, {}), {2}: (8, {})} | custom-call | tf_op jit(solution)/shard_map/expert_gradients/pallas_call | solution.py:856
  396.7 4.2 %collective-permute-start.20 = (bf16[24,1792]{1,0:T(8,128)(2,1)S(1)}, bf16[24,1792]{1,0:T(8,128)(2,1)S(1)}, u32[]{:S(2)}, u32[]{:S(2)}) collective-permute-start(bf16[24,1792]{1,0:T(8,128)(2,1)S(1)} %get-tuple-element.228), channel_id=1, source_target_pairs={{0,4},{1,5},{2,6},{3,7},{4,0},{5,1},{6,2},{7,3},{8,12},{9,13},{10,... | collective-permute-start | bytes 258056 | tf_op jit(solution)/shard_map/ppermute | solution.py:1294
  (184 shorter events, 102.5 us)
Async XLA Ops:
  8.9 9.2 %collective-permute-start = (bf16[24,1536]{1,0:T(8,128)(2,1)}, bf16[24,1536]{1,0:T(8,128)(2,1)S(1)}, u32[]{:S(2)}, u32[]{:S(2)}) collective-permute-start(bf16[24,1536]{1,0:T(8,128)(2,1)} %get-tuple-element.142), channel_id=1, source_target_pairs={{0,4},{1,5},{2,6},{3,7},{4,0},{5,1},{6,2},{7,3},{8,12},{9,13},{10,... | collective-permute-start | bytes 221192 | tf_op jit(solution)/shard_map/ppermute | solution.py:1294
  12.9 7.7 %collective-permute-start.2 = (bf16[24,1664]{1,0:T(8,128)(2,1)}, bf16[24,1664]{1,0:T(8,128)(2,1)S(1)}, u32[]{:S(2)}, u32[]{:S(2)}) collective-permute-start(bf16[24,1664]{1,0:T(8,128)(2,1)} %get-tuple-element.143), channel_id=1, source_target_pairs={{0,4},{1,5},{2,6},{3,7},{4,0},{5,1},{6,2},{7,3},{8,12},{9,13},{10,... | collective-permute-start | bytes 239624 | tf_op jit(solution)/shard_map/ppermute | solution.py:1294
  28.1 12.4 %collective-permute-start.4 = (bf16[2,2,24,1536]{3,2,0,1:T(8,128)(2,1)}, bf16[2,2,24,1536]{3,2,0,1:T(8,128)(2,1)}, u32[]{:S(2)}, u32[]{:S(2)}) collective-permute-start(bf16[2,2,24,1536]{3,2,0,1:T(8,128)(2,1)} %pad_maximum_fusion.7), channel_id=1, source_target_pairs={{0,1},{1,0},{2,3},{3,2},{4,5},{5,4},{6,7},{7,6},{8,9},{9,8},{10,11... | collective-permute-start | bytes 884744 | tf_op jit(solution)/shard_map/ppermute | solution.py:1294
  33.3 41.8 %all-to-all-start = ((bf16[8,128,768]{2,1,0:T(8,128)(2,1)}), bf16[8,128,768]{2,1,0:T(8,128)(2,1)}, u32[]{:S(2)}, u32[]{:S(2)}) async-start(bf16[8,128,768]{2,1,0:T(8,128)(2,1)} %fill_slots.4), calls=%async_computation | async-start | bytes 3145728 | tf_op jit(solution)/shard_map/all_to_all | solution.py:1373
  38.9 125.4 %all-gather.5.cloned.1.call-start = ((), (), s32[]{:S(2)}) async-start(), calls=%async_computation.9 | async-start | bytes 11919360 | tf_op jit(solution)/shard_map/all_gather | solution.py:1407
  39.0 8.0 %collective-permute-start.5 = (bf16[2,2,24,1664]{3,2,0,1:T(8,128)(2,1)S(1)}, bf16[2,2,24,1664]{3,2,0,1:T(8,128)(2,1)S(1)}, u32[]{:S(2)}, u32[]{:S(2)}) collective-permute-start(bf16[2,2,24,1664]{3,2,0,1:T(8,128)(2,1)S(1)} %pad_maximum_fusion.6), channel_id=1, source_target_pairs={{0,16},{8,24},{16,0},{24,8},{1,17},{9,25},{17,1},{25,9},{2,18},{10... | collective-permute-start | bytes 958472 | tf_op jit(solution)/shard_map/ppermute | solution.py:1294
  54.0 13.0 %collective-permute-start.6 = (bf16[2,2,2,24,1536]{4,3,0,1,2:T(8,128)(2,1)S(1)}, bf16[2,2,2,24,1536]{4,3,0,1,2:T(8,128)(2,1)S(1)}, u32[]{:S(2)}, u32[]{:S(2)}) collective-permute-start(bf16[2,2,2,24,1536]{4,3,0,1,2:T(8,128)(2,1)S(1)} %pad_maximum_fusion.5), channel_id=1, source_target_pairs={{0,16},{8,24},{16,0},{24,8},{1,17},{9,25},{17,1},{25,9},{2,18},{10... | collective-permute-start | bytes 1769480 | tf_op jit(solution)/shard_map/ppermute | solution.py:1294
  55.6 19.0 %collective-permute-start.7 = (bf16[2,2,2,24,1664]{4,3,1,2,0:T(8,128)(2,1)S(1)}, bf16[2,2,2,24,1664]{4,3,1,2,0:T(8,128)(2,1)S(1)}, u32[]{:S(2)}, u32[]{:S(2)}) collective-permute-start(bf16[2,2,2,24,1664]{4,3,1,2,0:T(8,128)(2,1)S(1)} %pad_maximum_fusion.4), channel_id=1, source_target_pairs={{0,1},{1,0},{2,3},{3,2},{4,5},{5,4},{6,7},{7,6},{8,9},{9,8},{10,11... | collective-permute-start | bytes 1916936 | tf_op jit(solution)/shard_map/ppermute | solution.py:1294
  75.2 135.4 %all-gather.7.cloned.1.call-start = ((), (), s32[]{:S(2)}) async-start(), calls=%async_computation.10 | async-start | bytes 11919360 | tf_op jit(solution)/shard_map/all_gather | solution.py:1407
  75.9 8.8 %collective-permute-start.9 = (bf16[2,192,1664]{2,1,0:T(8,128)(2,1)S(1)}, bf16[2,192,1664]{2,1,0:T(8,128)(2,1)}, u32[]{:S(2)}, u32[]{:S(2)}) collective-permute-start(bf16[2,192,1664]{2,1,0:T(8,128)(2,1)S(1)} %bitcast.88), channel_id=1, source_target_pairs={{0,8},{8,0},{16,24},{24,16},{1,9},{9,1},{17,25},{25,17},{2,10},{10... | collective-permute-start | bytes 3833864 | tf_op jit(solution)/shard_map/ppermute | solution.py:1294
  76.0 43.3 %all-to-all-start.1 = ((bf16[8,128,768]{2,1,0:T(8,128)(2,1)}), bf16[8,128,768]{2,1,0:T(8,128)(2,1)}, u32[]{:S(2)}, u32[]{:S(2)}) async-start(bf16[8,128,768]{2,1,0:T(8,128)(2,1)} %fill_slots.5), calls=%async_computation.1 | async-start | bytes 3145728 | tf_op jit(solution)/shard_map/all_to_all | solution.py:1373
  119.3 41.1 %all-to-all-start.2 = ((bf16[8,128,768]{2,1,0:T(8,128)(2,1)}), bf16[8,128,768]{2,1,0:T(8,128)(2,1)}, u32[]{:S(2)}, u32[]{:S(2)}) async-start(bf16[8,128,768]{2,1,0:T(8,128)(2,1)} %fill_slots.6), calls=%async_computation.2 | async-start | bytes 3145728 | tf_op jit(solution)/shard_map/all_to_all | solution.py:1373
  160.4 42.8 %all-to-all-start.3 = ((bf16[8,128,768]{2,1,0:T(8,128)(2,1)}), bf16[8,128,768]{2,1,0:T(8,128)(2,1)S(1)}, u32[]{:S(2)}, u32[]{:S(2)}) async-start(bf16[8,128,768]{2,1,0:T(8,128)(2,1)} %fill_slots.7), calls=%async_computation.3 | async-start | bytes 3145728 | tf_op jit(solution)/shard_map/all_to_all | solution.py:1373
  164.0 186.7 %reduce-scatter.2.cloned.1.call-start = ((), (), s32[]{:S(2)}) async-start(), calls=%async_computation.8 | async-start | bytes 11919360 | tf_op jit(solution)/shard_map/reduce_scatter | solution.py:1429
  204.4 45.1 %all-to-all-start.4 = ((bf16[8,128,768]{2,1,0:T(8,128)(2,1)}), bf16[8,128,768]{2,1,0:T(8,128)(2,1)S(1)}, u32[]{:S(2)}, u32[]{:S(2)}) async-start(bf16[8,128,768]{2,1,0:T(8,128)(2,1)} %get-tuple-element.174), calls=%async_computation.4 | async-start | bytes 3145728 | tf_op jit(solution)/shard_map/all_to_all | solution.py:1373
  249.5 15.7 %collective-permute-start.10 = (bf16[2,1552,768]{2,1,0:T(8,128)(2,1)}, bf16[2,1552,768]{2,1,0:T(8,128)(2,1)}, u32[]{:S(2)}, u32[]{:S(2)}) collective-permute-start(bf16[2,1552,768]{2,1,0:T(8,128)(2,1)} %get-tuple-element.184), channel_id=1, source_target_pairs={{0,8},{8,0},{16,24},{24,16},{1,9},{9,1},{17,25},{25,17},{2,10},{10... | collective-permute-start | bytes 14303240 | tf_op jit(solution)/shard_map/ppermute | solution.py:1294
  249.6 43.8 %all-to-all-start.5 = ((bf16[8,128,768]{2,1,0:T(8,128)(2,1)}), bf16[8,128,768]{2,1,0:T(8,128)(2,1)}, u32[]{:S(2)}, u32[]{:S(2)}) async-start(bf16[8,128,768]{2,1,0:T(8,128)(2,1)} %get-tuple-element.185), calls=%async_computation.5 | async-start | bytes 3145728 | tf_op jit(solution)/shard_map/all_to_all | solution.py:1373
  293.4 76.2 %collective-permute-start.15 = (bf16[1552,768]{1,0:T(8,128)(2,1)}, bf16[1552,768]{1,0:T(8,128)(2,1)}, u32[]{:S(2)}, u32[]{:S(2)}) collective-permute-start(bf16[1552,768]{1,0:T(8,128)(2,1)} %get-tuple-element.195), channel_id=1, source_target_pairs={{0,16},{8,24},{16,0},{24,8},{1,17},{9,25},{17,1},{25,9},{2,18},{10... | collective-permute-start | bytes 7151624 | tf_op jit(solution)/shard_map/ppermute | solution.py:1294
  294.3 82.4 %all-to-all-start.6 = ((bf16[8,256,768]{2,1,0:T(8,128)(2,1)}), bf16[8,256,768]{2,1,0:T(8,128)(2,1)}, u32[]{:S(2)}, u32[]{:S(2)}) async-start(bf16[8,256,768]{2,1,0:T(8,128)(2,1)} %get-tuple-element.205), calls=%async_computation.7 | async-start | bytes 6291456 | tf_op jit(solution)/shard_map/all_to_all | solution.py:1373
  347.6 21.9 %collective-permute-start.13 = (bf16[192,1792]{1,0:T(8,128)(2,1)}, bf16[192,1792]{1,0:T(8,128)(2,1)}, u32[]{:S(2)}, u32[]{:S(2)}) collective-permute-start(bf16[192,1792]{1,0:T(8,128)(2,1)} %get-tuple-element.193), channel_id=1, source_target_pairs={{0,16},{8,24},{16,0},{24,8},{1,17},{9,25},{17,1},{25,9},{2,18},{10... | collective-permute-start | bytes 2064392 | tf_op jit(solution)/shard_map/ppermute | solution.py:1294
  348.8 20.8 %collective-permute-start.14 = (bf16[192,1408]{1,0:T(8,128)(2,1)}, bf16[192,1408]{1,0:T(8,128)(2,1)}, u32[]{:S(2)}, u32[]{:S(2)}) collective-permute-start(bf16[192,1408]{1,0:T(8,128)(2,1)} %get-tuple-element.194), channel_id=1, source_target_pairs={{0,1},{1,0},{2,3},{3,2},{4,5},{5,4},{6,7},{7,6},{8,9},{9,8},{10,11... | collective-permute-start | bytes 1622024 | tf_op jit(solution)/shard_map/ppermute | solution.py:1294
  373.3 15.4 %collective-permute-start.16 = (bf16[96,1792]{1,0:T(8,128)(2,1)}, bf16[96,1792]{1,0:T(8,128)(2,1)S(1)}, u32[]{:S(2)}, u32[]{:S(2)}) collective-permute-start(bf16[96,1792]{1,0:T(8,128)(2,1)} %get-tuple-element.203), channel_id=1, source_target_pairs={{0,1},{1,0},{2,3},{3,2},{4,5},{5,4},{6,7},{7,6},{8,9},{9,8},{10,11... | collective-permute-start | bytes 1032200 | tf_op jit(solution)/shard_map/ppermute | solution.py:1294
  375.8 12.9 %collective-permute-start.17 = (bf16[96,1408]{1,0:T(8,128)(2,1)}, bf16[96,1408]{1,0:T(8,128)(2,1)S(1)}, u32[]{:S(2)}, u32[]{:S(2)}) collective-permute-start(bf16[96,1408]{1,0:T(8,128)(2,1)} %get-tuple-element.204), channel_id=1, source_target_pairs={{0,16},{8,24},{16,0},{24,8},{1,17},{9,25},{17,1},{25,9},{2,18},{10... | collective-permute-start | bytes 811016 | tf_op jit(solution)/shard_map/ppermute | solution.py:1294
  396.7 9.8 %collective-permute-start.20 = (bf16[24,1792]{1,0:T(8,128)(2,1)S(1)}, bf16[24,1792]{1,0:T(8,128)(2,1)S(1)}, u32[]{:S(2)}, u32[]{:S(2)}) collective-permute-start(bf16[24,1792]{1,0:T(8,128)(2,1)S(1)} %get-tuple-element.228), channel_id=1, source_target_pairs={{0,4},{1,5},{2,6},{3,7},{4,0},{5,1},{6,2},{7,3},{8,12},{9,13},{10,... | collective-permute-start | bytes 258056 | tf_op jit(solution)/shard_map/ppermute | solution.py:1294
  (48 other events, 504.3 us)
Sparse Core Ops, SparseCore 0:
  75.3 64.7 all-gather.4
  142.2 64.7 all-gather.6
  209.6 79.0 reduce-scatter.1

commit v5 on v4

--- a/solution.py
+++ b/solution.py
@@ -4,6 +4,7 @@
 import jax.numpy as jnp
 from jax import lax
 from jax.experimental import pallas as pl
+from jax.experimental.layout import Layout, with_layout_constraint
 from jax.experimental.pallas import tpu as pltpu
 from jax.sharding import PartitionSpec as P
 
@@ -77,8 +78,8 @@
     return copies
 
 
-def arrive(step, copies):
-    @pl.when(step == 0)
+def arrive(step, copies, turn=0):
+    @pl.when(step == turn)
     def _():
         for copy in copies:
             copy.wait()
@@ -1072,10 +1073,15 @@
         one_ref,
         two_ref,
         misc_ref,
+        normed_ref,
+        pair_ref,
+        first_keep_ref,
         sems,
     ) = refs[1:]
     _, length, width = tokens_ref.shape
     step = pl.program_id(0)
+    place = lax.rem(step, 2)
+    pitch = normed_ref.shape[0] // 2
     parts = ((one_own, one_other), (two_own, two_other))
     copies = load_weights(step, core_ref[0], parts, (one_ref, two_ref), sems)
     cut = one_ref.shape[-1]
@@ -1089,6 +1095,8 @@
         grad_two_ref[...] = jnp.zeros_like(grad_two_ref)
         vec_ref[...] = jnp.zeros_like(vec_ref)
         stack_ref[...] = jnp.zeros_like(stack_ref)
+        normed_ref[...] = jnp.zeros_like(normed_ref)
+        pair_ref[...] = jnp.zeros_like(pair_ref)
         load_scores(slots, score_ref)
 
     cot = cot_ref[0].astype(f32)
@@ -1155,17 +1163,28 @@
         grads[1].append(grad_k.astype(bf16))
         grads[2].append(grad_v.astype(bf16))
     grad_qkv = jnp.concatenate(grads[0] + grads[1] + grads[2], axis=1)
-    rows = tokens_ref[0].astype(f32)
-    unit, scale = norm_parts(rows)
-    normed = (unit * vec[0] + vec[1]).astype(bf16)
-    add_to(grad_one_ref, slice(None), dot_tn(normed, grad_qkv[:, 0:grad_cut]))
-    add_to(grad_two_ref, slice(0, grad_rest), dot_tn(normed, grad_qkv[:, grad_cut:]))
-    arrive(step, copies[0])
-    grad_normed = dot_nt(grad_qkv[:, 0:cut], one_ref[...].reshape(width, cut))
-    grad_normed += dot_nt(grad_qkv[:, cut:], two_ref[..., 0:rest].reshape(width, rest))
-    vec_ref[0:1, :] += jnp.sum(grad_normed * unit, axis=0, keepdims=True)
-    vec_ref[1:2, :] += jnp.sum(grad_normed, axis=0, keepdims=True)
-    grad_tokens_ref[0] = grad_first + norm_backward(grad_normed, unit, scale, vec[0])
+    pair_ref[pl.ds(pl.multiple_of(place * pitch, 16), length), :] = grad_qkv
+    first_keep_ref[place] = grad_first
+    arrive(step, copies[0], 1)
+
+    @pl.when(place == 1)
+    def _():
+        units = []
+        for k in range(2):
+            unit, scale = norm_parts(tokens_ref[k].astype(f32))
+            units.append((unit, scale))
+            normed_ref[k * pitch : k * pitch + length, :] = (unit * vec[0] + vec[1]).astype(bf16)
+        pair = pair_ref[...]
+        normed = normed_ref[...]
+        add_to(grad_one_ref, slice(None), dot_tn(normed, pair[:, 0:grad_cut]))
+        add_to(grad_two_ref, slice(0, grad_rest), dot_tn(normed, pair[:, grad_cut:]))
+        grad_both = dot_nt(pair[:, 0:cut], one_ref[...].reshape(width, cut))
+        grad_both += dot_nt(pair[:, cut:], two_ref[..., 0:rest].reshape(width, rest))
+        for k, (unit, scale) in enumerate(units):
+            grad_normed = grad_both[k * pitch : k * pitch + length]
+            vec_ref[0:1, :] += jnp.sum(grad_normed * unit, axis=0, keepdims=True)
+            vec_ref[1:2, :] += jnp.sum(grad_normed, axis=0, keepdims=True)
+            grad_tokens_ref[k] = first_keep_ref[k] + norm_backward(grad_normed, unit, scale, vec[0])
 
     @pl.when(step == pl.num_programs(0) - 1)
     def _():
@@ -1188,12 +1207,15 @@
     grad_cut = 2 * width + width // 3 // LANES * LANES
     shapes = [(*packed[0][0].shape[:2], count) for count in (grad_cut, spare - grad_cut)]
     still = lambda shape: pl.BlockSpec(shape, lambda i: (0, 0, 0))
+    assert images % 2 == 0
+    both = pl.BlockSpec((2, length, width), lambda i: (i // 2, 0, 0))
+    pitch = -(-length // 16) * 16
     return pl.pallas_call(
         functools.partial(backward_kernel, labels, local, cap),
         grid=(images,),
         in_specs=[
             pl.BlockSpec(memory_space=pltpu.SMEM),
-            whole(length, width),
+            both,
             whole(length, width),
             whole(length, 8),
             whole(length, 3 * width),
@@ -1206,7 +1228,7 @@
             pl.BlockSpec((owners, capp, width), lambda i: (0, 0, 0)),
         ],
         out_specs=[
-            whole(length, width),
+            both,
             *[still(shape) for shape in shapes for _ in range(2)],
         ],
         out_shape=[
@@ -1220,9 +1242,12 @@
             pltpu.VMEM((16, owners * capp), bf16),
             *weight_scratch(packed),
             pltpu.VMEM((LANES, width), bf16),
+            pltpu.VMEM((2 * pitch, width), bf16),
+            pltpu.VMEM((2 * pitch, 3 * width), bf16),
+            pltpu.VMEM((2, length, width), f32),
             pltpu.SemaphoreType.DMA((4,)),
         ],
-        compiler_params=params(58),
+        compiler_params=params(60),
         cost_estimate=pl.CostEstimate(
             flops=40_000_000_000, bytes_accessed=40_000_000, transcendentals=2_000_000
         ),
@@ -1473,25 +1498,21 @@
         for have, hop in zip(left, hops):
             have.remove(hop)
         if turn == 0:
-            share = share_out(shares[0], None, 0, local, depth)
-            beside = [shares[-1][1], *share]
+            for l in range(local):
+                share = share_out(shares[l], share, l, local, depth)
+            grad_tokens = with_layout_constraint(grad_tokens, Layout(major_to_minor=(1, 0, 2)))
+            beside = [grad_tokens, *share]
         elif turn == 1:
             output = combine(first, cols, gates, joined, local)
             beside = [output]
-        elif turn == 2:
-            for l in range(1, local):
-                share = share_out(shares[l], share, l, local, depth)
-            beside = [*share, grad_tokens]
         else:
             continue
         one, two, *beside = lax.optimization_barrier((sums[0][1], sums[1][1], *beside))
         sums = [(sums[0][0], one), (sums[1][0], two)]
         if turn == 0:
-            shares[-1][1], *share = beside
-        elif turn == 1:
+            grad_tokens, *share = beside
+        else:
             output = beside[0]
-        else:
-            *share, grad_tokens = beside
     one, two = sums
     share_back, share_in, share_bias = share
     grad_qkv, grad_out, grad_router, *small = dense_out(one, two, labels, owners)

time: 424 us -> 422 us (level)
    unnamed x86 -> x83, local copies, waits for them, and re-layouts: 29.1 us -> 25 us
  transfers between devices with their start and end apart: 32 -> 32, of which waited for: 15 -> 15; matrix products, arithmetic and copies ran while one was open for 6% -> 7% of each run, Pallas kernels for 42% -> 42%
where the time goes in v5:
time: 422 us; the launch traced here: 413 us
  Pallas kernels  177 us (42%)
  waiting for transfers between devices  109 us (26%)
  starting transfers between devices  63.4 us (15%)
  local copies, waits for them, and re-layouts  31.6 us (7%)
  other arithmetic  17.5 us (4%)
  between operations  14.9 us (4%)
    all_to_all x7, waiting for transfers between devices, per_device(): exchange = lambda block: lax.all_to_all(block, 'expert', 0, 0, tiled=True)  62.7 us
    ppermute x22, waiting for transfers between devices, swap(): lax.ppermute(block, axis, [(d, d ^ 1 << bit) for d in range(sizes[axis])])  45 us
    pallas_call x1, Pallas kernels, parted_expert(): pl.pallas_call(functools.partial(parted_kernel, cap), grid=(groups,), in_...  38.9 us
    pallas_call x1, Pallas kernels, expert(): pl.pallas_call(functools.partial(expert_kernel, cap), grid=(groups,), in_...  38.9 us
    pallas_call x1, Pallas kernels, backward(): pl.pallas_call(functools.partial(backward_kernel, labels, local, cap), gr...  36.7 us
    all_to_all x7, starting transfers between devices, per_device(): exchange = lambda block: lax.all_to_all(block, 'expert', 0, 0, tiled=True)  35.7 us
    ppermute x22, starting transfers between devices, swap(): lax.ppermute(block, axis, [(d, d ^ 1 << bit) for d in range(sizes[axis])])  27.2 us
    unnamed x83, local copies, waits for them, and re-layouts  25 us
  transfers between devices with their start and end apart: 32, of which 15 were waited for; matrix products, arithmetic and copies ran while one was open for 7% of the time, Pallas kernels for 42%

profile of v5, /device:TPU:0, one launch (start us, length us, event | category | flops | bytes accessed | tf_op | source)
XLA Modules:
  0.0 413.1 jit_solution(12606263933952061224)
XLA Ops:
  33.3 5.6 %all-to-all-start = ((bf16[8,128,768]{2,1,0:T(8,128)(2,1)}), bf16[8,128,768]{2,1,0:T(8,128)(2,1)}, u32[]{:S(2)}, u32[]{:S(2)}) async-start(bf16[8,128,768]{2,1,0:T(8,128)(2,1)} %fill_slots.4), calls=%async_computation | async-start | bytes 3145728 | tf_op jit(solution)/shard_map/all_to_all | solution.py:1398
  41.7 5.3 %collective-permute-done.5 = bf16[2,2,24,1664]{3,2,0,1:T(8,128)(2,1)S(1)} collective-permute-done((bf16[2,2,24,1664]{3,2,0,1:T(8,128)(2,1)S(1)}, bf16[2,2,24,1664]{3,2,0,1:T(8,128)(2,1)S(1)}, u32[]{:S(2)}, u32[]{:S(2)}) %collective-permute-start.5) | collective-permute-done | bytes 319520 | tf_op jit(solution)/shard_map/ppermute | solution.py:1319
  60.0 7.0 %collective-permute-done.6 = bf16[2,2,2,24,1536]{4,3,0,1,2:T(8,128)(2,1)S(1)} collective-permute-done((bf16[2,2,2,24,1536]{4,3,0,1,2:T(8,128)(2,1)S(1)}, bf16[2,2,2,24,1536]{4,3,0,1,2:T(8,128)(2,1)S(1)}, u32[]{:S(2)}, u32[]{:S(2)}) %collective-permute-start.6) | collective-permute-done | bytes 589856 | tf_op jit(solution)/shard_map/ppermute | solution.py:1319
  67.3 7.3 %collective-permute-done.7 = bf16[2,2,2,24,1664]{4,3,1,2,0:T(8,128)(2,1)S(1)} collective-permute-done((bf16[2,2,2,24,1664]{4,3,1,2,0:T(8,128)(2,1)S(1)}, bf16[2,2,2,24,1664]{4,3,1,2,0:T(8,128)(2,1)S(1)}, u32[]{:S(2)}, u32[]{:S(2)}) %collective-permute-start.7) | collective-permute-done | bytes 639008 | tf_op jit(solution)/shard_map/ppermute | solution.py:1319
  76.0 5.4 %all-to-all-start.1 = ((bf16[8,128,768]{2,1,0:T(8,128)(2,1)}), bf16[8,128,768]{2,1,0:T(8,128)(2,1)}, u32[]{:S(2)}, u32[]{:S(2)}) async-start(bf16[8,128,768]{2,1,0:T(8,128)(2,1)} %fill_slots.5), calls=%async_computation.1 | async-start | bytes 3145728 | tf_op jit(solution)/shard_map/all_to_all | solution.py:1398
  84.4 16.8 %attention_forward.1 = (bf16[4,197,2304]{2,1,0:T(8,128)(2,1)}, bf16[4,197,768]{2,1,0:T(8,128)(2,1)S(1)}, f32[4,16,256]{2,1,0:T(8,128)S(1)}, f32[4,197,768]{2,1,0...) custom-call(s32[1]{0:T(128)} %bitcast.2.core_ref, ...), custom_call_target="tpu_custom_call" | custom-call | flops 16000000000 | bytes 20000000 | tf_op jit(solution)/shard_map/attention_forward/pallas_call | solution.py:386
  104.5 4.4 %fill_slots.6 = bf16[8,128,768]{2,1,0:T(8,128)(2,1)} custom-call(s32[4,8,197]{2,1,0:T(8,128)S(1)} %get-tuple-element.141.rows_ref, bf16[4,197,768]{2,1,0:T(8,128)(2,1)S(1)} %get-tuple-element.152.value_ref.routed_ref, bf16[4,16,197]{2,1,0:T(8,128)(2,1)S(1)} %get-tuple-element.153.refs_0_), custom_call_target="tpu_custom_call" | custom-call | tf_op jit(solution)/shard_map/fill_slots/pallas_call | solution.py:273
  108.9 10.1 %all-to-all-done.1.cot_ref = bf16[8,128,768]{2,1,0:T(8,128)(2,1)} async-done(((bf16[8,128,768]{2,1,0:T(8,128)(2,1)}), bf16[8,128,768]{2,1,0:T(8,128)(2,1)}, u32[]{:S(2)}, u32[]{:S(2)}) %all-to-all-start.1) | async-done | bytes 1572896 | tf_op jit(solution)/shard_map/all_to_all | solution.py:1398
  119.1 4.3 %all-to-all-start.2 = ((bf16[8,128,768]{2,1,0:T(8,128)(2,1)}), bf16[8,128,768]{2,1,0:T(8,128)(2,1)}, u32[]{:S(2)}, u32[]{:S(2)}) async-start(bf16[8,128,768]{2,1,0:T(8,128)(2,1)} %fill_slots.6), calls=%async_computation.2 | async-start | bytes 3145728 | tf_op jit(solution)/shard_map/all_to_all | solution.py:1398
  127.4 32.8 %all-to-all-done.2.rows_ref = bf16[8,128,768]{2,1,0:T(8,128)(2,1)} async-done(((bf16[8,128,768]{2,1,0:T(8,128)(2,1)}), bf16[8,128,768]{2,1,0:T(8,128)(2,1)}, u32[]{:S(2)}, u32[]{:S(2)}) %all-to-all-start.2) | async-done | bytes 1572896 | tf_op jit(solution)/shard_map/all_to_all | solution.py:1398
  164.3 38.9 %expert_rows.1 = (bf16[8,256,768]{2,1,0:T(8,128)(2,1)}, bf16[8,128,768]{2,1,0:T(8,128)(2,1)}, bf16[4,1552,768]{2,1,0:T(8,128)(2,1)}) custom-call(bf16[8,128,768]{2,1,0:T(8,128)(2,1)} %all-to-all-done.2.rows_ref, bf16[8,128,768]{2,1,0:T(8,128)(2,1)} %all-to-all-done.cot_ref, bf16[4,1552,768]{2,1,0:T(8,128)(2,1)} %bitcast.114, ...), custom_call_target="tpu_custom_call" | custom-call | flops 28991029248 | bytes 30000000 | tf_op jit(solution)/shard_map/expert_rows/pallas_call | solution.py:572
  204.3 6.2 %all-to-all-start.4 = ((bf16[8,128,768]{2,1,0:T(8,128)(2,1)}), bf16[8,128,768]{2,1,0:T(8,128)(2,1)S(1)}, u32[]{:S(2)}, u32[]{:S(2)}) async-start(bf16[8,128,768]{2,1,0:T(8,128)(2,1)} %get-tuple-element.168), calls=%async_computation.4 | async-start | bytes 3145728 | tf_op jit(solution)/shard_map/all_to_all | solution.py:1398
  210.5 38.9 %expert_rows_parted.1 = (bf16[8,256,768]{2,1,0:T(8,128)(2,1)}, bf16[8,128,768]{2,1,0:T(8,128)(2,1)}, bf16[2,1552,768]{2,1,0:T(8,128)(2,1)}, bf16[2,1552,768]{2,1,0:T(8,128)(2,1)}) custom-call(s32[1]{0:T(128)} %bitcast.2.core_ref, bf16[8,128,768]{2,1,0:T(8,128)(2,1)} %copy-done.31, ...), custom_call_target="tpu_custom_call", output_to_operand_aliasing={{0}: (6, {})} | custom-call | flops 28991029248 | bytes 30000000 | tf_op jit(solution)/shard_map/expert_rows_parted/pallas_call | solution.py:791
  249.5 6.0 %all-to-all-start.5 = ((bf16[8,128,768]{2,1,0:T(8,128)(2,1)}), bf16[8,128,768]{2,1,0:T(8,128)(2,1)}, u32[]{:S(2)}, u32[]{:S(2)}) async-start(bf16[8,128,768]{2,1,0:T(8,128)(2,1)} %get-tuple-element.179), calls=%async_computation.5 | async-start | bytes 3145728 | tf_op jit(solution)/shard_map/all_to_all | solution.py:1398
  257.8 5.0 %attention_again.1 = (f32[4,197,768]{2,1,0:T(8,128)S(1)}, f32[4,197,8]{2,1,0:T(8,128)S(1)}, bf16[4,12,197,197]{3,2,1,0:T(8,128)(2,1)S(1)}) custom-call(s32[4,197,8]{2,1,0:T(8,128)S(1)} %get-tuple-element.134.cols_ref, bf16[4,197,2304]{2,1,0:T(8,128)(2,1)S(1)} %copy-done.26, f32[4,16,256]{2,1,0:T(8,128)S(1)} %get-tuple-element.150.lse_ref, ...), custom_call_target="tpu_custom_call" | custom-call | flops 10000000000 | bytes 20000000 | tf_op jit(solution)/shard_map/attention_again/pallas_call | solution.py:1015
  265.0 6.9 %convert_add_fusion = bf16[2,1552,768]{2,1,0:T(8,128)(2,1)S(1)} fusion(bf16[2,1552,768]{2,1,0:T(8,128)(2,1)} %collective-permute-done.10, bf16[2,1552,768]{2,1,0:T(8,128)(2,1)} %get-tuple-element.177), kind=kLoop, calls=%fused_computation | loop fusion | flops 9535488 | bytes 14303232 | tf_op jit(solution)/shard_map/add | solution.py:1458
  273.7 19.6 %all-to-all-done.5.refs_0_ = bf16[8,128,768]{2,1,0:T(8,128)(2,1)} async-done(((bf16[8,128,768]{2,1,0:T(8,128)(2,1)}), bf16[8,128,768]{2,1,0:T(8,128)(2,1)}, u32[]{:S(2)}, u32[]{:S(2)}) %all-to-all-start.5) | async-done | bytes 1572896 | tf_op jit(solution)/shard_map/all_to_all | solution.py:1398
  294.2 4.7 %all-to-all-start.6 = ((bf16[8,256,768]{2,1,0:T(8,128)(2,1)}), bf16[8,256,768]{2,1,0:T(8,128)(2,1)}, u32[]{:S(2)}, u32[]{:S(2)}) async-start(bf16[8,256,768]{2,1,0:T(8,128)(2,1)} %get-tuple-element.204), calls=%async_computation.7 | async-start | bytes 6291456 | tf_op jit(solution)/shard_map/all_to_all | solution.py:1398
  298.8 36.7 %attention_backward.1 = (f32[4,197,768]{2,1,0:T(8,128)}, bf16[2,192,1792]{2,1,0:T(8,128)(2,1)}, bf16[2,192,1792]{2,1,0:T(8,128)(2,1)}, bf16[2,192,1408]{2,1,0:T(8,128)(2,1)}, bf16[2,192,1408]{2,1,0:T(8,128)(2,1)}) custom-call(s32[1]{0:T(128)} %bitcast.2.core_ref, bf16[4,197,768]{2,1,0:T(8,128)(2,1)} %copy-done.9, bf16[4,197,768]{2,1,0:T(8,128)(2,1)} %copy-done.1, ...), custom_call_target="tpu_custom_call" | custom-call | flops 40000000000 | bytes 40000000 | tf_op jit(solution)/shard_map/attention_backward/pallas_call | solution.py:1213
  336.1 4.4 %collective-permute-done.12 = bf16[2,192,1408]{2,1,0:T(8,128)(2,1)S(1)} collective-permute-done((bf16[2,192,1408]{2,1,0:T(8,128)(2,1)}, bf16[2,192,1408]{2,1,0:T(8,128)(2,1)S(1)}, u32[]{:S(2)}, u32[]{:S(2)}) %collective-permute-start.12) | collective-permute-done | bytes 1081376 | tf_op jit(solution)/shard_map/ppermute | solution.py:1319
  355.8 4.4 %expert_gradients.3 = (f32[2,768,768]{2,1,0:T(8,128)}, f32[2,192,3072]{2,1,0:T(8,128)}, f32[2,16,768]{2,1,0:T(8,128)S(1)}) custom-call(bf16[1552,768]{1,0:T(8,128)(2,1)S(1)} %get-tuple-element.190.refs_0_.refs_1_.refs_2_, ...), custom_call_target="tpu_custom_call", output_to_operand_aliasing={{0}: (6, {}), {1}: (7, {}), {2}: (8, {})} | custom-call | tf_op jit(solution)/shard_map/expert_gradients/pallas_call | solution.py:857
  360.9 7.2 %collective-permute-done.14 = bf16[192,1408]{1,0:T(8,128)(2,1)} collective-permute-done((bf16[192,1408]{1,0:T(8,128)(2,1)}, bf16[192,1408]{1,0:T(8,128)(2,1)}, u32[]{:S(2)}, u32[]{:S(2)}) %collective-permute-start.14) | collective-permute-done | bytes 540704 | tf_op jit(solution)/shard_map/ppermute | solution.py:1319
  377.5 8.2 %combine_outputs.1 = bf16[4,197,768]{2,1,0:T(8,128)(2,1)S(1)} custom-call(f32[4,197,768]{2,1,0:T(8,128)S(1)} %copy-done.4, s32[4,197,8]{2,1,0:T(8,128)S(1)} %copy-done.18, f32[4,197,16]{2,1,0:T(8,128)S(1)} %copy-done.20, bf16[8,256,768]{2,1,0:T(8,128)(2,1)} %all-to-all-done.6.slots_ref), custom_call_target="tpu_custom_call" | custom-call | tf_op jit(solution)/shard_map/combine_outputs/pallas_call | solution.py:1295
  389.0 5.6 %collective-permute-done.19.refs_5_ = bf16[48,1408]{1,0:T(8,128)(2,1)S(1)} collective-permute-done((bf16[48,1408]{1,0:T(8,128)(2,1)S(1)}, bf16[48,1408]{1,0:T(8,128)(2,1)S(1)}, u32[]{:S(2)}, u32[]{:S(2)}) %collective-permute-start.19) | collective-permute-done | bytes 135200 | tf_op jit(solution)/shard_map/ppermute | solution.py:1319
  (182 shorter events, 106.7 us)
Async XLA Ops:
  8.9 9.2 %collective-permute-start = (bf16[24,1536]{1,0:T(8,128)(2,1)}, bf16[24,1536]{1,0:T(8,128)(2,1)S(1)}, u32[]{:S(2)}, u32[]{:S(2)}) collective-permute-start(bf16[24,1536]{1,0:T(8,128)(2,1)} %get-tuple-element.136), channel_id=1, source_target_pairs={{0,4},{1,5},{2,6},{3,7},{4,0},{5,1},{6,2},{7,3},{8,12},{9,13},{10,... | collective-permute-start | bytes 221192 | tf_op jit(solution)/shard_map/ppermute | solution.py:1319
  12.9 7.7 %collective-permute-start.2 = (bf16[24,1664]{1,0:T(8,128)(2,1)}, bf16[24,1664]{1,0:T(8,128)(2,1)S(1)}, u32[]{:S(2)}, u32[]{:S(2)}) collective-permute-start(bf16[24,1664]{1,0:T(8,128)(2,1)} %get-tuple-element.137), channel_id=1, source_target_pairs={{0,4},{1,5},{2,6},{3,7},{4,0},{5,1},{6,2},{7,3},{8,12},{9,13},{10,... | collective-permute-start | bytes 239624 | tf_op jit(solution)/shard_map/ppermute | solution.py:1319
  28.1 12.4 %collective-permute-start.4 = (bf16[2,2,24,1536]{3,2,0,1:T(8,128)(2,1)}, bf16[2,2,24,1536]{3,2,0,1:T(8,128)(2,1)}, u32[]{:S(2)}, u32[]{:S(2)}) collective-permute-start(bf16[2,2,24,1536]{3,2,0,1:T(8,128)(2,1)} %pad_maximum_fusion.7), channel_id=1, source_target_pairs={{0,1},{1,0},{2,3},{3,2},{4,5},{5,4},{6,7},{7,6},{8,9},{9,8},{10,11... | collective-permute-start | bytes 884744 | tf_op jit(solution)/shard_map/ppermute | solution.py:1319
  33.3 41.8 %all-to-all-start = ((bf16[8,128,768]{2,1,0:T(8,128)(2,1)}), bf16[8,128,768]{2,1,0:T(8,128)(2,1)}, u32[]{:S(2)}, u32[]{:S(2)}) async-start(bf16[8,128,768]{2,1,0:T(8,128)(2,1)} %fill_slots.4), calls=%async_computation | async-start | bytes 3145728 | tf_op jit(solution)/shard_map/all_to_all | solution.py:1398
  38.9 125.4 %all-gather.5.cloned.1.call-start = ((), (), s32[]{:S(2)}) async-start(), calls=%async_computation.9 | async-start | bytes 11919360 | tf_op jit(solution)/shard_map/all_gather | solution.py:1432
  39.0 8.0 %collective-permute-start.5 = (bf16[2,2,24,1664]{3,2,0,1:T(8,128)(2,1)S(1)}, bf16[2,2,24,1664]{3,2,0,1:T(8,128)(2,1)S(1)}, u32[]{:S(2)}, u32[]{:S(2)}) collective-permute-start(bf16[2,2,24,1664]{3,2,0,1:T(8,128)(2,1)S(1)} %pad_maximum_fusion.6), channel_id=1, source_target_pairs={{0,16},{8,24},{16,0},{24,8},{1,17},{9,25},{17,1},{25,9},{2,18},{10... | collective-permute-start | bytes 958472 | tf_op jit(solution)/shard_map/ppermute | solution.py:1319
  54.0 13.0 %collective-permute-start.6 = (bf16[2,2,2,24,1536]{4,3,0,1,2:T(8,128)(2,1)S(1)}, bf16[2,2,2,24,1536]{4,3,0,1,2:T(8,128)(2,1)S(1)}, u32[]{:S(2)}, u32[]{:S(2)}) collective-permute-start(bf16[2,2,2,24,1536]{4,3,0,1,2:T(8,128)(2,1)S(1)} %pad_maximum_fusion.5), channel_id=1, source_target_pairs={{0,16},{8,24},{16,0},{24,8},{1,17},{9,25},{17,1},{25,9},{2,18},{10... | collective-permute-start | bytes 1769480 | tf_op jit(solution)/shard_map/ppermute | solution.py:1319
  55.6 19.0 %collective-permute-start.7 = (bf16[2,2,2,24,1664]{4,3,1,2,0:T(8,128)(2,1)S(1)}, bf16[2,2,2,24,1664]{4,3,1,2,0:T(8,128)(2,1)S(1)}, u32[]{:S(2)}, u32[]{:S(2)}) collective-permute-start(bf16[2,2,2,24,1664]{4,3,1,2,0:T(8,128)(2,1)S(1)} %pad_maximum_fusion.4), channel_id=1, source_target_pairs={{0,1},{1,0},{2,3},{3,2},{4,5},{5,4},{6,7},{7,6},{8,9},{9,8},{10,11... | collective-permute-start | bytes 1916936 | tf_op jit(solution)/shard_map/ppermute | solution.py:1319
  75.2 135.3 %all-gather.7.cloned.1.call-start = ((), (), s32[]{:S(2)}) async-start(), calls=%async_computation.10 | async-start | bytes 11919360 | tf_op jit(solution)/shard_map/all_gather | solution.py:1432
  75.9 8.5 %collective-permute-start.9 = (bf16[2,192,1664]{2,1,0:T(8,128)(2,1)S(1)}, bf16[2,192,1664]{2,1,0:T(8,128)(2,1)}, u32[]{:S(2)}, u32[]{:S(2)}) collective-permute-start(bf16[2,192,1664]{2,1,0:T(8,128)(2,1)S(1)} %bitcast.88), channel_id=1, source_target_pairs={{0,8},{8,0},{16,24},{24,16},{1,9},{9,1},{17,25},{25,17},{2,10},{10... | collective-permute-start | bytes 3833864 | tf_op jit(solution)/shard_map/ppermute | solution.py:1319
  76.0 43.1 %all-to-all-start.1 = ((bf16[8,128,768]{2,1,0:T(8,128)(2,1)}), bf16[8,128,768]{2,1,0:T(8,128)(2,1)}, u32[]{:S(2)}, u32[]{:S(2)}) async-start(bf16[8,128,768]{2,1,0:T(8,128)(2,1)} %fill_slots.5), calls=%async_computation.1 | async-start | bytes 3145728 | tf_op jit(solution)/shard_map/all_to_all | solution.py:1398
  119.1 41.1 %all-to-all-start.2 = ((bf16[8,128,768]{2,1,0:T(8,128)(2,1)}), bf16[8,128,768]{2,1,0:T(8,128)(2,1)}, u32[]{:S(2)}, u32[]{:S(2)}) async-start(bf16[8,128,768]{2,1,0:T(8,128)(2,1)} %fill_slots.6), calls=%async_computation.2 | async-start | bytes 3145728 | tf_op jit(solution)/shard_map/all_to_all | solution.py:1398
  160.2 43.0 %all-to-all-start.3 = ((bf16[8,128,768]{2,1,0:T(8,128)(2,1)}), bf16[8,128,768]{2,1,0:T(8,128)(2,1)S(1)}, u32[]{:S(2)}, u32[]{:S(2)}) async-start(bf16[8,128,768]{2,1,0:T(8,128)(2,1)} %fill_slots.7), calls=%async_computation.3 | async-start | bytes 3145728 | tf_op jit(solution)/shard_map/all_to_all | solution.py:1398
  163.8 187.8 %reduce-scatter.2.cloned.1.call-start = ((), (), s32[]{:S(2)}) async-start(), calls=%async_computation.8 | async-start | bytes 11919360 | tf_op jit(solution)/shard_map/reduce_scatter | solution.py:1454
  204.3 45.1 %all-to-all-start.4 = ((bf16[8,128,768]{2,1,0:T(8,128)(2,1)}), bf16[8,128,768]{2,1,0:T(8,128)(2,1)S(1)}, u32[]{:S(2)}, u32[]{:S(2)}) async-start(bf16[8,128,768]{2,1,0:T(8,128)(2,1)} %get-tuple-element.168), calls=%async_computation.4 | async-start | bytes 3145728 | tf_op jit(solution)/shard_map/all_to_all | solution.py:1398
  249.4 15.6 %collective-permute-start.10 = (bf16[2,1552,768]{2,1,0:T(8,128)(2,1)}, bf16[2,1552,768]{2,1,0:T(8,128)(2,1)}, u32[]{:S(2)}, u32[]{:S(2)}) collective-permute-start(bf16[2,1552,768]{2,1,0:T(8,128)(2,1)} %get-tuple-element.178), channel_id=1, source_target_pairs={{0,8},{8,0},{16,24},{24,16},{1,9},{9,1},{17,25},{25,17},{2,10},{10... | collective-permute-start | bytes 14303240 | tf_op jit(solution)/shard_map/ppermute | solution.py:1319
  249.5 43.8 %all-to-all-start.5 = ((bf16[8,128,768]{2,1,0:T(8,128)(2,1)}), bf16[8,128,768]{2,1,0:T(8,128)(2,1)}, u32[]{:S(2)}, u32[]{:S(2)}) async-start(bf16[8,128,768]{2,1,0:T(8,128)(2,1)} %get-tuple-element.179), calls=%async_computation.5 | async-start | bytes 3145728 | tf_op jit(solution)/shard_map/all_to_all | solution.py:1398
  293.3 62.5 %collective-permute-start.15 = (bf16[1552,768]{1,0:T(8,128)(2,1)}, bf16[1552,768]{1,0:T(8,128)(2,1)}, u32[]{:S(2)}, u32[]{:S(2)}) collective-permute-start(bf16[1552,768]{1,0:T(8,128)(2,1)} %get-tuple-element.191), channel_id=1, source_target_pairs={{0,16},{8,24},{16,0},{24,8},{1,17},{9,25},{17,1},{25,9},{2,18},{10... | collective-permute-start | bytes 7151624 | tf_op jit(solution)/shard_map/ppermute | solution.py:1319
  294.2 81.3 %all-to-all-start.6 = ((bf16[8,256,768]{2,1,0:T(8,128)(2,1)}), bf16[8,256,768]{2,1,0:T(8,128)(2,1)}, u32[]{:S(2)}, u32[]{:S(2)}) async-start(bf16[8,256,768]{2,1,0:T(8,128)(2,1)} %get-tuple-element.204), calls=%async_computation.7 | async-start | bytes 6291456 | tf_op jit(solution)/shard_map/all_to_all | solution.py:1398
  346.2 21.9 %collective-permute-start.13 = (bf16[192,1792]{1,0:T(8,128)(2,1)}, bf16[192,1792]{1,0:T(8,128)(2,1)}, u32[]{:S(2)}, u32[]{:S(2)}) collective-permute-start(bf16[192,1792]{1,0:T(8,128)(2,1)} %get-tuple-element.187), channel_id=1, source_target_pairs={{0,16},{8,24},{16,0},{24,8},{1,17},{9,25},{17,1},{25,9},{2,18},{10... | collective-permute-start | bytes 2064392 | tf_op jit(solution)/shard_map/ppermute | solution.py:1319
  347.3 20.8 %collective-permute-start.14 = (bf16[192,1408]{1,0:T(8,128)(2,1)}, bf16[192,1408]{1,0:T(8,128)(2,1)}, u32[]{:S(2)}, u32[]{:S(2)}) collective-permute-start(bf16[192,1408]{1,0:T(8,128)(2,1)} %get-tuple-element.188), channel_id=1, source_target_pairs={{0,1},{1,0},{2,3},{3,2},{4,5},{5,4},{6,7},{7,6},{8,9},{9,8},{10,11... | collective-permute-start | bytes 1622024 | tf_op jit(solution)/shard_map/ppermute | solution.py:1319
  372.1 13.7 %collective-permute-start.16 = (bf16[96,1792]{1,0:T(8,128)(2,1)}, bf16[96,1792]{1,0:T(8,128)(2,1)S(1)}, u32[]{:S(2)}, u32[]{:S(2)}) collective-permute-start(bf16[96,1792]{1,0:T(8,128)(2,1)} %get-tuple-element.202), channel_id=1, source_target_pairs={{0,1},{1,0},{2,3},{3,2},{4,5},{5,4},{6,7},{7,6},{8,9},{9,8},{10,11... | collective-permute-start | bytes 1032200 | tf_op jit(solution)/shard_map/ppermute | solution.py:1319
  374.6 11.2 %collective-permute-start.17 = (bf16[96,1408]{1,0:T(8,128)(2,1)}, bf16[96,1408]{1,0:T(8,128)(2,1)}, u32[]{:S(2)}, u32[]{:S(2)}) collective-permute-start(bf16[96,1408]{1,0:T(8,128)(2,1)} %get-tuple-element.203), channel_id=1, source_target_pairs={{0,16},{8,24},{16,0},{24,8},{1,17},{9,25},{17,1},{25,9},{2,18},{10... | collective-permute-start | bytes 811016 | tf_op jit(solution)/shard_map/ppermute | solution.py:1319
  394.7 9.0 %collective-permute-start.20 = (bf16[24,1792]{1,0:T(8,128)(2,1)S(1)}, bf16[24,1792]{1,0:T(8,128)(2,1)S(1)}, u32[]{:S(2)}, u32[]{:S(2)}) collective-permute-start(bf16[24,1792]{1,0:T(8,128)(2,1)S(1)} %get-tuple-element.216), channel_id=1, source_target_pairs={{0,4},{1,5},{2,6},{3,7},{4,0},{5,1},{6,2},{7,3},{8,12},{9,13},{10,... | collective-permute-start | bytes 258056 | tf_op jit(solution)/shard_map/ppermute | solution.py:1319
  (47 other events, 503.3 us)
Sparse Core Ops, SparseCore 0:
  75.3 64.7 all-gather.4
  142.2 64.7 all-gather.6
  209.6 79.0 reduce-scatter.1

commit v6 on v5

--- a/solution.py
+++ b/solution.py
@@ -1397,10 +1397,14 @@
     rows, cols = route(marks, order, labels, cap, capp)
     exchange = lambda block: lax.all_to_all(block, "expert", 0, 0, tiled=True)
     slices = [spread(block, [], near[:1], order_of_hops, sizes)[0] for block in slices]
+    rows, *slices = lax.optimization_barrier((rows, *slices))
+    filled = dispatch(rows, cotangent, None, cap, capp, owners, [0])
     slices = [spread(block, near[:1], near[1:], order_of_hops, sizes) for block in slices]
     haves = [have for _, have in slices]
-    rows, *slices = lax.optimization_barrier((rows, *[block for block, _ in slices]))
-    cots = [exchange(dispatch(rows, cotangent, None, cap, capp, owners, [0]))]
+    rows, filled, *slices = lax.optimization_barrier(
+        (rows, filled, *[block for block, _ in slices])
+    )
+    cots = [exchange(filled)]
     columns = [block.shape[-1] for block in slices]
     halves = []
     for turn in range(len(outer) + 1):
@@ -1426,7 +1430,8 @@
         jnp.concatenate([w_back[l], wide[l], biases[l]], axis=0).astype(bf16)
         for l in range(local)
     ]
-    cots[0], cots[-1], *moved = lax.optimization_barrier((cots[0], cots[-1], *experts, *halves))
+    cots[0], cots[-1] = lax.optimization_barrier((cots[0], cots[-1]))
+    cots[0], *moved = lax.optimization_barrier((cots[0], *experts, *halves))
     experts, halves = moved[:local], moved[local:]
     cots[1:] = [exchange(block) for block in cots[1:]]
     experts = [lax.all_gather(block, "group") for block in experts]

time: 422 us -> 420 us (level)
    unnamed x83 -> x81, local copies, waits for them, and re-layouts: 25 us -> 26.2 us
  transfers between devices with their start and end apart: 32 -> 32, of which waited for: 15 -> 16; matrix products, arithmetic and copies ran while one was open for 7% -> 7% of each run, Pallas kernels for 42% -> 42%
where the time goes in v6:
time: 420 us; the launch traced here: 412 us
  Pallas kernels  177 us (42%)
  waiting for transfers between devices  109 us (26%)
  starting transfers between devices  62.7 us (15%)
  local copies, waits for them, and re-layouts  32.8 us (8%)
  other arithmetic  15.8 us (4%)
  between operations  14.9 us (4%)
    all_to_all x7, waiting for transfers between devices, per_device(): exchange = lambda block: lax.all_to_all(block, 'expert', 0, 0, tiled=True)  62.6 us
    ppermute x22, waiting for transfers between devices, swap(): lax.ppermute(block, axis, [(d, d ^ 1 << bit) for d in range(sizes[axis])])  45.3 us
    pallas_call x1, Pallas kernels, parted_expert(): pl.pallas_call(functools.partial(parted_kernel, cap), grid=(groups,), in_...  38.9 us
    pallas_call x1, Pallas kernels, expert(): pl.pallas_call(functools.partial(expert_kernel, cap), grid=(groups,), in_...  38.9 us
    pallas_call x1, Pallas kernels, backward(): pl.pallas_call(functools.partial(backward_kernel, labels, local, cap), gr...  36.7 us
    all_to_all x7, starting transfers between devices, per_device(): exchange = lambda block: lax.all_to_all(block, 'expert', 0, 0, tiled=True)  35.2 us
    ppermute x22, starting transfers between devices, swap(): lax.ppermute(block, axis, [(d, d ^ 1 << bit) for d in range(sizes[axis])])  26.9 us
    unnamed x81, local copies, waits for them, and re-layouts  26.2 us
  transfers between devices with their start and end apart: 32, of which 16 were waited for; matrix products, arithmetic and copies ran while one was open for 7% of the time, Pallas kernels for 42%

profile of v6, /device:TPU:0, one launch (start us, length us, event | category | flops | bytes accessed | tf_op | source)
XLA Modules:
  0.0 412.0 jit_solution(13608718622516059597)
XLA Ops:
  32.5 4.9 %all-to-all-start = ((bf16[8,128,768]{2,1,0:T(8,128)(2,1)}), bf16[8,128,768]{2,1,0:T(8,128)(2,1)}, u32[]{:S(2)}, u32[]{:S(2)}) async-start(bf16[8,128,768]{2,1,0:T(8,128)(2,1)} %fill_slots.4), calls=%async_computation | async-start | bytes 3145728 | tf_op jit(solution)/shard_map/all_to_all | solution.py:1398
  41.0 4.6 %collective-permute-done.5 = bf16[2,2,24,1664]{3,2,0,1:T(8,128)(2,1)S(1)} collective-permute-done((bf16[2,2,24,1664]{3,2,0,1:T(8,128)(2,1)S(1)}, bf16[2,2,24,1664]{3,2,0,1:T(8,128)(2,1)S(1)}, u32[]{:S(2)}, u32[]{:S(2)}) %collective-permute-start.5) | collective-permute-done | bytes 319520 | tf_op jit(solution)/shard_map/ppermute | solution.py:1319
  58.6 7.1 %collective-permute-done.6 = bf16[2,2,2,24,1536]{4,3,0,1,2:T(8,128)(2,1)S(1)} collective-permute-done((bf16[2,2,2,24,1536]{4,3,0,1,2:T(8,128)(2,1)S(1)}, bf16[2,2,2,24,1536]{4,3,0,1,2:T(8,128)(2,1)S(1)}, u32[]{:S(2)}, u32[]{:S(2)}) %collective-permute-start.6) | collective-permute-done | bytes 589856 | tf_op jit(solution)/shard_map/ppermute | solution.py:1319
  66.1 7.3 %collective-permute-done.7 = bf16[2,2,2,24,1664]{4,3,1,2,0:T(8,128)(2,1)S(1)} collective-permute-done((bf16[2,2,2,24,1664]{4,3,1,2,0:T(8,128)(2,1)S(1)}, bf16[2,2,2,24,1664]{4,3,1,2,0:T(8,128)(2,1)S(1)}, u32[]{:S(2)}, u32[]{:S(2)}) %collective-permute-start.7) | collective-permute-done | bytes 639008 | tf_op jit(solution)/shard_map/ppermute | solution.py:1319
  74.6 5.6 %all-to-all-start.1 = ((bf16[8,128,768]{2,1,0:T(8,128)(2,1)}), bf16[8,128,768]{2,1,0:T(8,128)(2,1)}, u32[]{:S(2)}, u32[]{:S(2)}) async-start(bf16[8,128,768]{2,1,0:T(8,128)(2,1)} %fill_slots.5), calls=%async_computation.1 | async-start | bytes 3145728 | tf_op jit(solution)/shard_map/all_to_all | solution.py:1398
  83.2 16.8 %attention_forward.1 = (bf16[4,197,2304]{2,1,0:T(8,128)(2,1)}, bf16[4,197,768]{2,1,0:T(8,128)(2,1)S(1)}, f32[4,16,256]{2,1,0:T(8,128)S(1)}, f32[4,197,768]{2,1,0...) custom-call(s32[1]{0:T(128)} %bitcast.2.core_ref, ...), custom_call_target="tpu_custom_call" | custom-call | flops 16000000000 | bytes 20000000 | tf_op jit(solution)/shard_map/attention_forward/pallas_call | solution.py:386
  103.3 4.4 %fill_slots.6 = bf16[8,128,768]{2,1,0:T(8,128)(2,1)} custom-call(s32[4,8,197]{2,1,0:T(8,128)S(1)} %get-tuple-element.150.rows_ref, bf16[4,197,768]{2,1,0:T(8,128)(2,1)S(1)} %get-tuple-element.162.value_ref.routed_ref, bf16[4,16,197]{2,1,0:T(8,128)(2,1)S(1)} %get-tuple-element.163.refs_0_), custom_call_target="tpu_custom_call" | custom-call | tf_op jit(solution)/shard_map/fill_slots/pallas_call | solution.py:273
  107.7 10.1 %all-to-all-done.1.cot_ref = bf16[8,128,768]{2,1,0:T(8,128)(2,1)} async-done(((bf16[8,128,768]{2,1,0:T(8,128)(2,1)}), bf16[8,128,768]{2,1,0:T(8,128)(2,1)}, u32[]{:S(2)}, u32[]{:S(2)}) %all-to-all-start.1) | async-done | bytes 1572896 | tf_op jit(solution)/shard_map/all_to_all | solution.py:1398
  117.9 4.3 %all-to-all-start.2 = ((bf16[8,128,768]{2,1,0:T(8,128)(2,1)}), bf16[8,128,768]{2,1,0:T(8,128)(2,1)}, u32[]{:S(2)}, u32[]{:S(2)}) async-start(bf16[8,128,768]{2,1,0:T(8,128)(2,1)} %fill_slots.6), calls=%async_computation.2 | async-start | bytes 3145728 | tf_op jit(solution)/shard_map/all_to_all | solution.py:1398
  126.2 32.8 %all-to-all-done.2.rows_ref = bf16[8,128,768]{2,1,0:T(8,128)(2,1)} async-done(((bf16[8,128,768]{2,1,0:T(8,128)(2,1)}), bf16[8,128,768]{2,1,0:T(8,128)(2,1)}, u32[]{:S(2)}, u32[]{:S(2)}) %all-to-all-start.2) | async-done | bytes 1572896 | tf_op jit(solution)/shard_map/all_to_all | solution.py:1398
  163.1 38.9 %expert_rows.1 = (bf16[8,256,768]{2,1,0:T(8,128)(2,1)}, bf16[8,128,768]{2,1,0:T(8,128)(2,1)}, bf16[4,1552,768]{2,1,0:T(8,128)(2,1)}) custom-call(bf16[8,128,768]{2,1,0:T(8,128)(2,1)} %all-to-all-done.2.rows_ref, bf16[8,128,768]{2,1,0:T(8,128)(2,1)} %all-to-all-done.cot_ref, bf16[4,1552,768]{2,1,0:T(8,128)(2,1)} %bitcast.114, ...), custom_call_target="tpu_custom_call" | custom-call | flops 28991029248 | bytes 30000000 | tf_op jit(solution)/shard_map/expert_rows/pallas_call | solution.py:572
  203.1 6.2 %all-to-all-start.4 = ((bf16[8,128,768]{2,1,0:T(8,128)(2,1)}), bf16[8,128,768]{2,1,0:T(8,128)(2,1)S(1)}, u32[]{:S(2)}, u32[]{:S(2)}) async-start(bf16[8,128,768]{2,1,0:T(8,128)(2,1)} %get-tuple-element.178), calls=%async_computation.4 | async-start | bytes 3145728 | tf_op jit(solution)/shard_map/all_to_all | solution.py:1398
  209.3 38.9 %expert_rows_parted.1 = (bf16[8,256,768]{2,1,0:T(8,128)(2,1)}, bf16[8,128,768]{2,1,0:T(8,128)(2,1)}, bf16[2,1552,768]{2,1,0:T(8,128)(2,1)}, bf16[2,1552,768]{2,1,0:T(8,128)(2,1)}) custom-call(s32[1]{0:T(128)} %bitcast.2.core_ref, bf16[8,128,768]{2,1,0:T(8,128)(2,1)} %copy-done.31, ...), custom_call_target="tpu_custom_call", output_to_operand_aliasing={{0}: (6, {})} | custom-call | flops 28991029248 | bytes 30000000 | tf_op jit(solution)/shard_map/expert_rows_parted/pallas_call | solution.py:791
  248.3 6.0 %all-to-all-start.5 = ((bf16[8,128,768]{2,1,0:T(8,128)(2,1)}), bf16[8,128,768]{2,1,0:T(8,128)(2,1)}, u32[]{:S(2)}, u32[]{:S(2)}) async-start(bf16[8,128,768]{2,1,0:T(8,128)(2,1)} %get-tuple-element.189), calls=%async_computation.5 | async-start | bytes 3145728 | tf_op jit(solution)/shard_map/all_to_all | solution.py:1398
  256.6 5.0 %attention_again.1 = (f32[4,197,768]{2,1,0:T(8,128)S(1)}, f32[4,197,8]{2,1,0:T(8,128)S(1)}, bf16[4,12,197,197]{3,2,1,0:T(8,128)(2,1)S(1)}) custom-call(s32[4,197,8]{2,1,0:T(8,128)S(1)} %get-tuple-element.139.cols_ref, bf16[4,197,2304]{2,1,0:T(8,128)(2,1)S(1)} %copy-done.26, f32[4,16,256]{2,1,0:T(8,128)S(1)} %get-tuple-element.160.lse_ref, ...), custom_call_target="tpu_custom_call" | custom-call | flops 10000000000 | bytes 20000000 | tf_op jit(solution)/shard_map/attention_again/pallas_call | solution.py:1015
  263.8 6.9 %convert_add_fusion = bf16[2,1552,768]{2,1,0:T(8,128)(2,1)S(1)} fusion(bf16[2,1552,768]{2,1,0:T(8,128)(2,1)} %collective-permute-done.10, bf16[2,1552,768]{2,1,0:T(8,128)(2,1)} %get-tuple-element.187), kind=kLoop, calls=%fused_computation | loop fusion | flops 9535488 | bytes 14303232 | tf_op jit(solution)/shard_map/add | solution.py:1463
  272.5 19.6 %all-to-all-done.5.refs_0_ = bf16[8,128,768]{2,1,0:T(8,128)(2,1)} async-done(((bf16[8,128,768]{2,1,0:T(8,128)(2,1)}), bf16[8,128,768]{2,1,0:T(8,128)(2,1)}, u32[]{:S(2)}, u32[]{:S(2)}) %all-to-all-start.5) | async-done | bytes 1572896 | tf_op jit(solution)/shard_map/all_to_all | solution.py:1398
  293.0 4.7 %all-to-all-start.6 = ((bf16[8,256,768]{2,1,0:T(8,128)(2,1)}), bf16[8,256,768]{2,1,0:T(8,128)(2,1)}, u32[]{:S(2)}, u32[]{:S(2)}) async-start(bf16[8,256,768]{2,1,0:T(8,128)(2,1)} %get-tuple-element.214), calls=%async_computation.7 | async-start | bytes 6291456 | tf_op jit(solution)/shard_map/all_to_all | solution.py:1398
  297.7 36.7 %attention_backward.1 = (f32[4,197,768]{2,1,0:T(8,128)}, bf16[2,192,1792]{2,1,0:T(8,128)(2,1)}, bf16[2,192,1792]{2,1,0:T(8,128)(2,1)}, bf16[2,192,1408]{2,1,0:T(8,128)(2,1)}, bf16[2,192,1408]{2,1,0:T(8,128)(2,1)}) custom-call(s32[1]{0:T(128)} %bitcast.2.core_ref, bf16[4,197,768]{2,1,0:T(8,128)(2,1)} %copy-done.9, bf16[4,197,768]{2,1,0:T(8,128)(2,1)} %copy-done.1, ...), custom_call_target="tpu_custom_call" | custom-call | flops 40000000000 | bytes 40000000 | tf_op jit(solution)/shard_map/attention_backward/pallas_call | solution.py:1213
  334.9 4.4 %collective-permute-done.12 = bf16[2,192,1408]{2,1,0:T(8,128)(2,1)S(1)} collective-permute-done((bf16[2,192,1408]{2,1,0:T(8,128)(2,1)}, bf16[2,192,1408]{2,1,0:T(8,128)(2,1)S(1)}, u32[]{:S(2)}, u32[]{:S(2)}) %collective-permute-start.12) | collective-permute-done | bytes 1081376 | tf_op jit(solution)/shard_map/ppermute | solution.py:1319
  354.6 4.4 %expert_gradients.3 = (f32[2,768,768]{2,1,0:T(8,128)}, f32[2,192,3072]{2,1,0:T(8,128)}, f32[2,16,768]{2,1,0:T(8,128)S(1)}) custom-call(bf16[1552,768]{1,0:T(8,128)(2,1)S(1)} %get-tuple-element.200.refs_0_.refs_1_.refs_2_, ...), custom_call_target="tpu_custom_call", output_to_operand_aliasing={{0}: (6, {}), {1}: (7, {}), {2}: (8, {})} | custom-call | tf_op jit(solution)/shard_map/expert_gradients/pallas_call | solution.py:857
  359.7 7.2 %collective-permute-done.14 = bf16[192,1408]{1,0:T(8,128)(2,1)} collective-permute-done((bf16[192,1408]{1,0:T(8,128)(2,1)}, bf16[192,1408]{1,0:T(8,128)(2,1)}, u32[]{:S(2)}, u32[]{:S(2)}) %collective-permute-start.14) | collective-permute-done | bytes 540704 | tf_op jit(solution)/shard_map/ppermute | solution.py:1319
  376.3 8.3 %combine_outputs.1 = bf16[4,197,768]{2,1,0:T(8,128)(2,1)S(1)} custom-call(f32[4,197,768]{2,1,0:T(8,128)S(1)} %copy-done.4, s32[4,197,8]{2,1,0:T(8,128)S(1)} %copy-done.18, f32[4,197,16]{2,1,0:T(8,128)S(1)} %copy-done.20, bf16[8,256,768]{2,1,0:T(8,128)(2,1)} %all-to-all-done.6.slots_ref), custom_call_target="tpu_custom_call" | custom-call | tf_op jit(solution)/shard_map/combine_outputs/pallas_call | solution.py:1295
  387.8 5.6 %collective-permute-done.19.refs_5_ = bf16[48,1408]{1,0:T(8,128)(2,1)S(1)} collective-permute-done((bf16[48,1408]{1,0:T(8,128)(2,1)S(1)}, bf16[48,1408]{1,0:T(8,128)(2,1)S(1)}, u32[]{:S(2)}, u32[]{:S(2)}) %collective-permute-start.19) | collective-permute-done | bytes 135200 | tf_op jit(solution)/shard_map/ppermute | solution.py:1319
  (180 shorter events, 106.6 us)
Async XLA Ops:
  8.9 9.2 %collective-permute-start = (bf16[24,1536]{1,0:T(8,128)(2,1)}, bf16[24,1536]{1,0:T(8,128)(2,1)S(1)}, u32[]{:S(2)}, u32[]{:S(2)}) collective-permute-start(bf16[24,1536]{1,0:T(8,128)(2,1)} %get-tuple-element.141), channel_id=1, source_target_pairs={{0,4},{1,5},{2,6},{3,7},{4,0},{5,1},{6,2},{7,3},{8,12},{9,13},{10,... | collective-permute-start | bytes 221192 | tf_op jit(solution)/shard_map/ppermute | solution.py:1319
  30.7 10.2 %collective-permute-start.4 = (bf16[2,2,24,1536]{3,2,0,1:T(8,128)(2,1)S(1)}, bf16[2,2,24,1536]{3,2,0,1:T(8,128)(2,1)S(1)}, u32[]{:S(2)}, u32[]{:S(2)}) collective-permute-start(bf16[2,2,24,1536]{3,2,0,1:T(8,128)(2,1)S(1)} %pad_maximum_fusion.7), channel_id=1, source_target_pairs={{0,1},{1,0},{2,3},{3,2},{4,5},{5,4},{6,7},{7,6},{8,9},{9,8},{10,11... | collective-permute-start | bytes 884744 | tf_op jit(solution)/shard_map/ppermute | solution.py:1319
  32.5 41.2 %all-to-all-start = ((bf16[8,128,768]{2,1,0:T(8,128)(2,1)}), bf16[8,128,768]{2,1,0:T(8,128)(2,1)}, u32[]{:S(2)}, u32[]{:S(2)}) async-start(bf16[8,128,768]{2,1,0:T(8,128)(2,1)} %fill_slots.4), calls=%async_computation | async-start | bytes 3145728 | tf_op jit(solution)/shard_map/all_to_all | solution.py:1398
  37.5 125.6 %all-gather.5.cloned.1.call-start = ((), (), s32[]{:S(2)}) async-start(), calls=%async_computation.9 | async-start | bytes 11919360 | tf_op jit(solution)/shard_map/all_gather | solution.py:1437
  37.5 8.1 %collective-permute-start.5 = (bf16[2,2,24,1664]{3,2,0,1:T(8,128)(2,1)S(1)}, bf16[2,2,24,1664]{3,2,0,1:T(8,128)(2,1)S(1)}, u32[]{:S(2)}, u32[]{:S(2)}) collective-permute-start(bf16[2,2,24,1664]{3,2,0,1:T(8,128)(2,1)S(1)} %pad_maximum_fusion.6), channel_id=1, source_target_pairs={{0,16},{8,24},{16,0},{24,8},{1,17},{9,25},{17,1},{25,9},{2,18},{10... | collective-permute-start | bytes 958472 | tf_op jit(solution)/shard_map/ppermute | solution.py:1319
  52.7 13.1 %collective-permute-start.6 = (bf16[2,2,2,24,1536]{4,3,0,1,2:T(8,128)(2,1)S(1)}, bf16[2,2,2,24,1536]{4,3,0,1,2:T(8,128)(2,1)S(1)}, u32[]{:S(2)}, u32[]{:S(2)}) collective-permute-start(bf16[2,2,2,24,1536]{4,3,0,1,2:T(8,128)(2,1)S(1)} %pad_maximum_fusion.5), channel_id=1, source_target_pairs={{0,16},{8,24},{16,0},{24,8},{1,17},{9,25},{17,1},{25,9},{2,18},{10... | collective-permute-start | bytes 1769480 | tf_op jit(solution)/shard_map/ppermute | solution.py:1319
  54.2 19.2 %collective-permute-start.7 = (bf16[2,2,2,24,1664]{4,3,1,2,0:T(8,128)(2,1)S(1)}, bf16[2,2,2,24,1664]{4,3,1,2,0:T(8,128)(2,1)S(1)}, u32[]{:S(2)}, u32[]{:S(2)}) collective-permute-start(bf16[2,2,2,24,1664]{4,3,1,2,0:T(8,128)(2,1)S(1)} %pad_maximum_fusion.4), channel_id=1, source_target_pairs={{0,1},{1,0},{2,3},{3,2},{4,5},{5,4},{6,7},{7,6},{8,9},{9,8},{10,11... | collective-permute-start | bytes 1916936 | tf_op jit(solution)/shard_map/ppermute | solution.py:1319
  73.8 135.5 %all-gather.7.cloned.1.call-start = ((), (), s32[]{:S(2)}) async-start(), calls=%async_computation.10 | async-start | bytes 11919360 | tf_op jit(solution)/shard_map/all_gather | solution.py:1437
  74.5 8.7 %collective-permute-start.9 = (bf16[2,192,1664]{2,1,0:T(8,128)(2,1)S(1)}, bf16[2,192,1664]{2,1,0:T(8,128)(2,1)}, u32[]{:S(2)}, u32[]{:S(2)}) collective-permute-start(bf16[2,192,1664]{2,1,0:T(8,128)(2,1)S(1)} %bitcast.88), channel_id=1, source_target_pairs={{0,8},{8,0},{16,24},{24,16},{1,9},{9,1},{17,25},{25,17},{2,10},{10... | collective-permute-start | bytes 3833864 | tf_op jit(solution)/shard_map/ppermute | solution.py:1319
  74.6 43.2 %all-to-all-start.1 = ((bf16[8,128,768]{2,1,0:T(8,128)(2,1)}), bf16[8,128,768]{2,1,0:T(8,128)(2,1)}, u32[]{:S(2)}, u32[]{:S(2)}) async-start(bf16[8,128,768]{2,1,0:T(8,128)(2,1)} %fill_slots.5), calls=%async_computation.1 | async-start | bytes 3145728 | tf_op jit(solution)/shard_map/all_to_all | solution.py:1398
  117.9 41.2 %all-to-all-start.2 = ((bf16[8,128,768]{2,1,0:T(8,128)(2,1)}), bf16[8,128,768]{2,1,0:T(8,128)(2,1)}, u32[]{:S(2)}, u32[]{:S(2)}) async-start(bf16[8,128,768]{2,1,0:T(8,128)(2,1)} %fill_slots.6), calls=%async_computation.2 | async-start | bytes 3145728 | tf_op jit(solution)/shard_map/all_to_all | solution.py:1398
  159.0 43.0 %all-to-all-start.3 = ((bf16[8,128,768]{2,1,0:T(8,128)(2,1)}), bf16[8,128,768]{2,1,0:T(8,128)(2,1)S(1)}, u32[]{:S(2)}, u32[]{:S(2)}) async-start(bf16[8,128,768]{2,1,0:T(8,128)(2,1)} %fill_slots.7), calls=%async_computation.3 | async-start | bytes 3145728 | tf_op jit(solution)/shard_map/all_to_all | solution.py:1398
  162.6 187.8 %reduce-scatter.2.cloned.1.call-start = ((), (), s32[]{:S(2)}) async-start(), calls=%async_computation.8 | async-start | bytes 11919360 | tf_op jit(solution)/shard_map/reduce_scatter | solution.py:1459
  203.1 45.1 %all-to-all-start.4 = ((bf16[8,128,768]{2,1,0:T(8,128)(2,1)}), bf16[8,128,768]{2,1,0:T(8,128)(2,1)S(1)}, u32[]{:S(2)}, u32[]{:S(2)}) async-start(bf16[8,128,768]{2,1,0:T(8,128)(2,1)} %get-tuple-element.178), calls=%async_computation.4 | async-start | bytes 3145728 | tf_op jit(solution)/shard_map/all_to_all | solution.py:1398
  248.2 15.6 %collective-permute-start.10 = (bf16[2,1552,768]{2,1,0:T(8,128)(2,1)}, bf16[2,1552,768]{2,1,0:T(8,128)(2,1)}, u32[]{:S(2)}, u32[]{:S(2)}) collective-permute-start(bf16[2,1552,768]{2,1,0:T(8,128)(2,1)} %get-tuple-element.188), channel_id=1, source_target_pairs={{0,8},{8,0},{16,24},{24,16},{1,9},{9,1},{17,25},{25,17},{2,10},{10... | collective-permute-start | bytes 14303240 | tf_op jit(solution)/shard_map/ppermute | solution.py:1319
  248.3 43.8 %all-to-all-start.5 = ((bf16[8,128,768]{2,1,0:T(8,128)(2,1)}), bf16[8,128,768]{2,1,0:T(8,128)(2,1)}, u32[]{:S(2)}, u32[]{:S(2)}) async-start(bf16[8,128,768]{2,1,0:T(8,128)(2,1)} %get-tuple-element.189), calls=%async_computation.5 | async-start | bytes 3145728 | tf_op jit(solution)/shard_map/all_to_all | solution.py:1398
  292.1 62.5 %collective-permute-start.15 = (bf16[1552,768]{1,0:T(8,128)(2,1)}, bf16[1552,768]{1,0:T(8,128)(2,1)}, u32[]{:S(2)}, u32[]{:S(2)}) collective-permute-start(bf16[1552,768]{1,0:T(8,128)(2,1)} %get-tuple-element.201), channel_id=1, source_target_pairs={{0,16},{8,24},{16,0},{24,8},{1,17},{9,25},{17,1},{25,9},{2,18},{10... | collective-permute-start | bytes 7151624 | tf_op jit(solution)/shard_map/ppermute | solution.py:1319
  293.0 81.3 %all-to-all-start.6 = ((bf16[8,256,768]{2,1,0:T(8,128)(2,1)}), bf16[8,256,768]{2,1,0:T(8,128)(2,1)}, u32[]{:S(2)}, u32[]{:S(2)}) async-start(bf16[8,256,768]{2,1,0:T(8,128)(2,1)} %get-tuple-element.214), calls=%async_computation.7 | async-start | bytes 6291456 | tf_op jit(solution)/shard_map/all_to_all | solution.py:1398
  345.0 21.9 %collective-permute-start.13 = (bf16[192,1792]{1,0:T(8,128)(2,1)}, bf16[192,1792]{1,0:T(8,128)(2,1)}, u32[]{:S(2)}, u32[]{:S(2)}) collective-permute-start(bf16[192,1792]{1,0:T(8,128)(2,1)} %get-tuple-element.197), channel_id=1, source_target_pairs={{0,16},{8,24},{16,0},{24,8},{1,17},{9,25},{17,1},{25,9},{2,18},{10... | collective-permute-start | bytes 2064392 | tf_op jit(solution)/shard_map/ppermute | solution.py:1319
  346.1 20.8 %collective-permute-start.14 = (bf16[192,1408]{1,0:T(8,128)(2,1)}, bf16[192,1408]{1,0:T(8,128)(2,1)}, u32[]{:S(2)}, u32[]{:S(2)}) collective-permute-start(bf16[192,1408]{1,0:T(8,128)(2,1)} %get-tuple-element.198), channel_id=1, source_target_pairs={{0,1},{1,0},{2,3},{3,2},{4,5},{5,4},{6,7},{7,6},{8,9},{9,8},{10,11... | collective-permute-start | bytes 1622024 | tf_op jit(solution)/shard_map/ppermute | solution.py:1319
  370.9 13.7 %collective-permute-start.16 = (bf16[96,1792]{1,0:T(8,128)(2,1)}, bf16[96,1792]{1,0:T(8,128)(2,1)S(1)}, u32[]{:S(2)}, u32[]{:S(2)}) collective-permute-start(bf16[96,1792]{1,0:T(8,128)(2,1)} %get-tuple-element.212), channel_id=1, source_target_pairs={{0,1},{1,0},{2,3},{3,2},{4,5},{5,4},{6,7},{7,6},{8,9},{9,8},{10,11... | collective-permute-start | bytes 1032200 | tf_op jit(solution)/shard_map/ppermute | solution.py:1319
  373.3 11.2 %collective-permute-start.17 = (bf16[96,1408]{1,0:T(8,128)(2,1)}, bf16[96,1408]{1,0:T(8,128)(2,1)}, u32[]{:S(2)}, u32[]{:S(2)}) collective-permute-start(bf16[96,1408]{1,0:T(8,128)(2,1)} %get-tuple-element.213), channel_id=1, source_target_pairs={{0,16},{8,24},{16,0},{24,8},{1,17},{9,25},{17,1},{25,9},{2,18},{10... | collective-permute-start | bytes 811016 | tf_op jit(solution)/shard_map/ppermute | solution.py:1319
  385.7 7.7 %collective-permute-start.18 = (bf16[48,1792]{1,0:T(8,128)(2,1)S(1)}, bf16[48,1792]{1,0:T(8,128)(2,1)S(1)}, u32[]{:S(2)}, u32[]{:S(2)}) collective-permute-start(bf16[48,1792]{1,0:T(8,128)(2,1)S(1)} %get-tuple-element.222), channel_id=1, source_target_pairs={{0,2},{1,3},{2,0},{3,1},{4,6},{5,7},{6,4},{7,5},{8,10},{9,11},{10,... | collective-permute-start | bytes 516104 | tf_op jit(solution)/shard_map/ppermute | solution.py:1319
  393.5 9.1 %collective-permute-start.20 = (bf16[24,1792]{1,0:T(8,128)(2,1)S(1)}, bf16[24,1792]{1,0:T(8,128)(2,1)S(1)}, u32[]{:S(2)}, u32[]{:S(2)}) collective-permute-start(bf16[24,1792]{1,0:T(8,128)(2,1)S(1)} %get-tuple-element.226), channel_id=1, source_target_pairs={{0,4},{1,5},{2,6},{3,7},{4,0},{5,1},{6,2},{7,3},{8,12},{9,13},{10,... | collective-permute-start | bytes 258056 | tf_op jit(solution)/shard_map/ppermute | solution.py:1319
  (46 other events, 493.3 us)
Sparse Core Ops, SparseCore 0:
  73.9 64.9 all-gather.4
  141.0 64.7 all-gather.6
  208.5 79.0 reduce-scatter.1

commit v7 on v6

--- a/solution.py
+++ b/solution.py
@@ -1247,7 +1247,7 @@
             pltpu.VMEM((2, length, width), f32),
             pltpu.SemaphoreType.DMA((4,)),
         ],
-        compiler_params=params(60),
+        compiler_params=params(50),
         cost_estimate=pl.CostEstimate(
             flops=40_000_000_000, bytes_accessed=40_000_000, transcendentals=2_000_000
         ),

time: 420 us -> 419 us (level)
  no operation moved by 1% of the time
where the time goes in v7:
time: 419 us; the launch traced here: 410 us
  Pallas kernels  176 us (42%)
  waiting for transfers between devices  109 us (26%)
  starting transfers between devices  62.5 us (15%)
  local copies, waits for them, and re-layouts  31.8 us (8%)
  other arithmetic  15.8 us (4%)
  between operations  14.9 us (4%)
    all_to_all x7, waiting for transfers between devices, per_device(): exchange = lambda block: lax.all_to_all(block, 'expert', 0, 0, tiled=True)  63.4 us
    ppermute x22, waiting for transfers between devices, swap(): lax.ppermute(block, axis, [(d, d ^ 1 << bit) for d in range(sizes[axis])])  45.1 us
    pallas_call x1, Pallas kernels, parted_expert(): pl.pallas_call(functools.partial(parted_kernel, cap), grid=(groups,), in_...  38.9 us
    pallas_call x1, Pallas kernels, expert(): pl.pallas_call(functools.partial(expert_kernel, cap), grid=(groups,), in_...  38.9 us
    pallas_call x1, Pallas kernels, backward(): pl.pallas_call(functools.partial(backward_kernel, labels, local, cap), gr...  35.5 us
    all_to_all x7, starting transfers between devices, per_device(): exchange = lambda block: lax.all_to_all(block, 'expert', 0, 0, tiled=True)  35.2 us
    ppermute x22, starting transfers between devices, swap(): lax.ppermute(block, axis, [(d, d ^ 1 << bit) for d in range(sizes[axis])])  26.7 us
    unnamed x81, local copies, waits for them, and re-layouts  25.2 us
  transfers between devices with their start and end apart: 32, of which 16 were waited for; matrix products, arithmetic and copies ran while one was open for 7% of the time, Pallas kernels for 42%

profile of v7, /device:TPU:0, one launch (start us, length us, event | category | flops | bytes accessed | tf_op | source)
XLA Modules:
  0.0 410.2 jit_solution(9785176887311334791)
XLA Ops:
  32.5 4.9 %all-to-all-start = ((bf16[8,128,768]{2,1,0:T(8,128)(2,1)}), bf16[8,128,768]{2,1,0:T(8,128)(2,1)}, u32[]{:S(2)}, u32[]{:S(2)}) async-start(bf16[8,128,768]{2,1,0:T(8,128)(2,1)} %fill_slots.4), calls=%async_computation | async-start | bytes 3145728 | tf_op jit(solution)/shard_map/all_to_all | solution.py:1398
  41.0 4.6 %collective-permute-done.5 = bf16[2,2,24,1664]{3,2,0,1:T(8,128)(2,1)S(1)} collective-permute-done((bf16[2,2,24,1664]{3,2,0,1:T(8,128)(2,1)S(1)}, bf16[2,2,24,1664]{3,2,0,1:T(8,128)(2,1)S(1)}, u32[]{:S(2)}, u32[]{:S(2)}) %collective-permute-start.5) | collective-permute-done | bytes 319520 | tf_op jit(solution)/shard_map/ppermute | solution.py:1319
  58.6 7.1 %collective-permute-done.6 = bf16[2,2,2,24,1536]{4,3,0,1,2:T(8,128)(2,1)S(1)} collective-permute-done((bf16[2,2,2,24,1536]{4,3,0,1,2:T(8,128)(2,1)S(1)}, bf16[2,2,2,24,1536]{4,3,0,1,2:T(8,128)(2,1)S(1)}, u32[]{:S(2)}, u32[]{:S(2)}) %collective-permute-start.6) | collective-permute-done | bytes 589856 | tf_op jit(solution)/shard_map/ppermute | solution.py:1319
  66.1 7.3 %collective-permute-done.7 = bf16[2,2,2,24,1664]{4,3,1,2,0:T(8,128)(2,1)S(1)} collective-permute-done((bf16[2,2,2,24,1664]{4,3,1,2,0:T(8,128)(2,1)S(1)}, bf16[2,2,2,24,1664]{4,3,1,2,0:T(8,128)(2,1)S(1)}, u32[]{:S(2)}, u32[]{:S(2)}) %collective-permute-start.7) | collective-permute-done | bytes 639008 | tf_op jit(solution)/shard_map/ppermute | solution.py:1319
  74.6 5.6 %all-to-all-start.1 = ((bf16[8,128,768]{2,1,0:T(8,128)(2,1)}), bf16[8,128,768]{2,1,0:T(8,128)(2,1)}, u32[]{:S(2)}, u32[]{:S(2)}) async-start(bf16[8,128,768]{2,1,0:T(8,128)(2,1)} %fill_slots.5), calls=%async_computation.1 | async-start | bytes 3145728 | tf_op jit(solution)/shard_map/all_to_all | solution.py:1398
  83.2 16.8 %attention_forward.1 = (bf16[4,197,2304]{2,1,0:T(8,128)(2,1)}, bf16[4,197,768]{2,1,0:T(8,128)(2,1)S(1)}, f32[4,16,256]{2,1,0:T(8,128)S(1)}, f32[4,197,768]{2,1,0...) custom-call(s32[1]{0:T(128)} %bitcast.2.core_ref, ...), custom_call_target="tpu_custom_call" | custom-call | flops 16000000000 | bytes 20000000 | tf_op jit(solution)/shard_map/attention_forward/pallas_call | solution.py:386
  102.6 4.4 %fill_slots.6 = bf16[8,128,768]{2,1,0:T(8,128)(2,1)} custom-call(s32[4,8,197]{2,1,0:T(8,128)S(1)} %get-tuple-element.150.rows_ref, bf16[4,197,768]{2,1,0:T(8,128)(2,1)S(1)} %get-tuple-element.162.value_ref.routed_ref, bf16[4,16,197]{2,1,0:T(8,128)(2,1)S(1)} %get-tuple-element.163.refs_0_), custom_call_target="tpu_custom_call" | custom-call | tf_op jit(solution)/shard_map/fill_slots/pallas_call | solution.py:273
  106.9 10.9 %all-to-all-done.1.cot_ref = bf16[8,128,768]{2,1,0:T(8,128)(2,1)} async-done(((bf16[8,128,768]{2,1,0:T(8,128)(2,1)}), bf16[8,128,768]{2,1,0:T(8,128)(2,1)}, u32[]{:S(2)}, u32[]{:S(2)}) %all-to-all-start.1) | async-done | bytes 1572896 | tf_op jit(solution)/shard_map/all_to_all | solution.py:1398
  117.9 4.3 %all-to-all-start.2 = ((bf16[8,128,768]{2,1,0:T(8,128)(2,1)}), bf16[8,128,768]{2,1,0:T(8,128)(2,1)}, u32[]{:S(2)}, u32[]{:S(2)}) async-start(bf16[8,128,768]{2,1,0:T(8,128)(2,1)} %fill_slots.6), calls=%async_computation.2 | async-start | bytes 3145728 | tf_op jit(solution)/shard_map/all_to_all | solution.py:1398
  126.2 32.8 %all-to-all-done.2.rows_ref = bf16[8,128,768]{2,1,0:T(8,128)(2,1)} async-done(((bf16[8,128,768]{2,1,0:T(8,128)(2,1)}), bf16[8,128,768]{2,1,0:T(8,128)(2,1)}, u32[]{:S(2)}, u32[]{:S(2)}) %all-to-all-start.2) | async-done | bytes 1572896 | tf_op jit(solution)/shard_map/all_to_all | solution.py:1398
  163.1 38.9 %expert_rows.1 = (bf16[8,256,768]{2,1,0:T(8,128)(2,1)}, bf16[8,128,768]{2,1,0:T(8,128)(2,1)}, bf16[4,1552,768]{2,1,0:T(8,128)(2,1)}) custom-call(bf16[8,128,768]{2,1,0:T(8,128)(2,1)} %all-to-all-done.2.rows_ref, bf16[8,128,768]{2,1,0:T(8,128)(2,1)} %all-to-all-done.cot_ref, bf16[4,1552,768]{2,1,0:T(8,128)(2,1)} %bitcast.114, ...), custom_call_target="tpu_custom_call" | custom-call | flops 28991029248 | bytes 30000000 | tf_op jit(solution)/shard_map/expert_rows/pallas_call | solution.py:572
  203.1 6.2 %all-to-all-start.4 = ((bf16[8,128,768]{2,1,0:T(8,128)(2,1)}), bf16[8,128,768]{2,1,0:T(8,128)(2,1)S(1)}, u32[]{:S(2)}, u32[]{:S(2)}) async-start(bf16[8,128,768]{2,1,0:T(8,128)(2,1)} %get-tuple-element.178), calls=%async_computation.4 | async-start | bytes 3145728 | tf_op jit(solution)/shard_map/all_to_all | solution.py:1398
  209.3 38.9 %expert_rows_parted.1 = (bf16[8,256,768]{2,1,0:T(8,128)(2,1)}, bf16[8,128,768]{2,1,0:T(8,128)(2,1)}, bf16[2,1552,768]{2,1,0:T(8,128)(2,1)}, bf16[2,1552,768]{2,1,0:T(8,128)(2,1)}) custom-call(s32[1]{0:T(128)} %bitcast.2.core_ref, bf16[8,128,768]{2,1,0:T(8,128)(2,1)} %copy-done.31, ...), custom_call_target="tpu_custom_call", output_to_operand_aliasing={{0}: (6, {})} | custom-call | flops 28991029248 | bytes 30000000 | tf_op jit(solution)/shard_map/expert_rows_parted/pallas_call | solution.py:791
  248.3 6.0 %all-to-all-start.5 = ((bf16[8,128,768]{2,1,0:T(8,128)(2,1)}), bf16[8,128,768]{2,1,0:T(8,128)(2,1)}, u32[]{:S(2)}, u32[]{:S(2)}) async-start(bf16[8,128,768]{2,1,0:T(8,128)(2,1)} %get-tuple-element.189), calls=%async_computation.5 | async-start | bytes 3145728 | tf_op jit(solution)/shard_map/all_to_all | solution.py:1398
  256.6 5.1 %attention_again.1 = (f32[4,197,768]{2,1,0:T(8,128)S(1)}, f32[4,197,8]{2,1,0:T(8,128)S(1)}, bf16[4,12,197,197]{3,2,1,0:T(8,128)(2,1)S(1)}) custom-call(s32[4,197,8]{2,1,0:T(8,128)S(1)} %get-tuple-element.139.cols_ref, bf16[4,197,2304]{2,1,0:T(8,128)(2,1)S(1)} %copy-done.25, f32[4,16,256]{2,1,0:T(8,128)S(1)} %get-tuple-element.160.lse_ref, ...), custom_call_target="tpu_custom_call" | custom-call | flops 10000000000 | bytes 20000000 | tf_op jit(solution)/shard_map/attention_again/pallas_call | solution.py:1015
  263.8 6.9 %convert_add_fusion = bf16[2,1552,768]{2,1,0:T(8,128)(2,1)S(1)} fusion(bf16[2,1552,768]{2,1,0:T(8,128)(2,1)} %collective-permute-done.10, bf16[2,1552,768]{2,1,0:T(8,128)(2,1)} %get-tuple-element.187), kind=kLoop, calls=%fused_computation | loop fusion | flops 9535488 | bytes 14303232 | tf_op jit(solution)/shard_map/add | solution.py:1463
  272.5 19.6 %all-to-all-done.5.refs_0_ = bf16[8,128,768]{2,1,0:T(8,128)(2,1)} async-done(((bf16[8,128,768]{2,1,0:T(8,128)(2,1)}), bf16[8,128,768]{2,1,0:T(8,128)(2,1)}, u32[]{:S(2)}, u32[]{:S(2)}) %all-to-all-start.5) | async-done | bytes 1572896 | tf_op jit(solution)/shard_map/all_to_all | solution.py:1398
  293.0 4.7 %all-to-all-start.6 = ((bf16[8,256,768]{2,1,0:T(8,128)(2,1)}), bf16[8,256,768]{2,1,0:T(8,128)(2,1)}, u32[]{:S(2)}, u32[]{:S(2)}) async-start(bf16[8,256,768]{2,1,0:T(8,128)(2,1)} %get-tuple-element.214), calls=%async_computation.7 | async-start | bytes 6291456 | tf_op jit(solution)/shard_map/all_to_all | solution.py:1398
  298.7 35.5 %attention_backward.1 = (f32[4,197,768]{2,1,0:T(8,128)}, bf16[2,192,1792]{2,1,0:T(8,128)(2,1)}, bf16[2,192,1792]{2,1,0:T(8,128)(2,1)}, bf16[2,192,1408]{2,1,0:T(8,128)(2,1)S(1)}, bf16[2,192,1408]{2,1,0:T(8,128)(2,1)S(1)}) custom-call(s32[1]{0:T(128)} %bitcast.2.core_ref, bf16[4,197,768]{2,1,0:T(8,128)(2,1)} %copy-done.9, bf16[4,197,768]{2,1,0:T(8,128)(2,1)} %copy-done.1, ...), custom_call_target="tpu_custom_call" | custom-call | flops 40000000000 | bytes 40000000 | tf_op jit(solution)/shard_map/attention_backward/pallas_call | solution.py:1213
  334.8 4.2 %collective-permute-done.12 = bf16[2,192,1408]{2,1,0:T(8,128)(2,1)S(1)} collective-permute-done((bf16[2,192,1408]{2,1,0:T(8,128)(2,1)S(1)}, bf16[2,192,1408]{2,1,0:T(8,128)(2,1)S(1)}, u32[]{:S(2)}, u32[]{:S(2)}) %collective-permute-start.12) | collective-permute-done | bytes 1081376 | tf_op jit(solution)/shard_map/ppermute | solution.py:1319
  353.0 4.4 %expert_gradients.3 = (f32[2,768,768]{2,1,0:T(8,128)}, f32[2,192,3072]{2,1,0:T(8,128)}, f32[2,16,768]{2,1,0:T(8,128)S(1)}) custom-call(bf16[1552,768]{1,0:T(8,128)(2,1)S(1)} %get-tuple-element.200.refs_0_.refs_1_.refs_2_, ...), custom_call_target="tpu_custom_call", output_to_operand_aliasing={{0}: (6, {}), {1}: (7, {}), {2}: (8, {})} | custom-call | tf_op jit(solution)/shard_map/expert_gradients/pallas_call | solution.py:857
  358.0 7.2 %collective-permute-done.14 = bf16[192,1408]{1,0:T(8,128)(2,1)} collective-permute-done((bf16[192,1408]{1,0:T(8,128)(2,1)}, bf16[192,1408]{1,0:T(8,128)(2,1)}, u32[]{:S(2)}, u32[]{:S(2)}) %collective-permute-start.14) | collective-permute-done | bytes 540704 | tf_op jit(solution)/shard_map/ppermute | solution.py:1319
  374.7 8.3 %combine_outputs.1 = bf16[4,197,768]{2,1,0:T(8,128)(2,1)S(1)} custom-call(f32[4,197,768]{2,1,0:T(8,128)S(1)} %copy-done.4, s32[4,197,8]{2,1,0:T(8,128)S(1)} %copy-done.17, f32[4,197,16]{2,1,0:T(8,128)S(1)} %copy-done.19, bf16[8,256,768]{2,1,0:T(8,128)(2,1)} %all-to-all-done.6.slots_ref), custom_call_target="tpu_custom_call" | custom-call | tf_op jit(solution)/shard_map/combine_outputs/pallas_call | solution.py:1295
  386.2 5.6 %collective-permute-done.19.refs_5_ = bf16[48,1408]{1,0:T(8,128)(2,1)S(1)} collective-permute-done((bf16[48,1408]{1,0:T(8,128)(2,1)S(1)}, bf16[48,1408]{1,0:T(8,128)(2,1)S(1)}, u32[]{:S(2)}, u32[]{:S(2)}) %collective-permute-start.19) | collective-permute-done | bytes 135200 | tf_op jit(solution)/shard_map/ppermute | solution.py:1319
  (180 shorter events, 105.4 us)
Async XLA Ops:
  8.9 9.2 %collective-permute-start = (bf16[24,1536]{1,0:T(8,128)(2,1)}, bf16[24,1536]{1,0:T(8,128)(2,1)S(1)}, u32[]{:S(2)}, u32[]{:S(2)}) collective-permute-start(bf16[24,1536]{1,0:T(8,128)(2,1)} %get-tuple-element.141), channel_id=1, source_target_pairs={{0,4},{1,5},{2,6},{3,7},{4,0},{5,1},{6,2},{7,3},{8,12},{9,13},{10,... | collective-permute-start | bytes 221192 | tf_op jit(solution)/shard_map/ppermute | solution.py:1319
  30.7 10.2 %collective-permute-start.4 = (bf16[2,2,24,1536]{3,2,0,1:T(8,128)(2,1)S(1)}, bf16[2,2,24,1536]{3,2,0,1:T(8,128)(2,1)S(1)}, u32[]{:S(2)}, u32[]{:S(2)}) collective-permute-start(bf16[2,2,24,1536]{3,2,0,1:T(8,128)(2,1)S(1)} %pad_maximum_fusion.7), channel_id=1, source_target_pairs={{0,1},{1,0},{2,3},{3,2},{4,5},{5,4},{6,7},{7,6},{8,9},{9,8},{10,11... | collective-permute-start | bytes 884744 | tf_op jit(solution)/shard_map/ppermute | solution.py:1319
  32.5 41.2 %all-to-all-start = ((bf16[8,128,768]{2,1,0:T(8,128)(2,1)}), bf16[8,128,768]{2,1,0:T(8,128)(2,1)}, u32[]{:S(2)}, u32[]{:S(2)}) async-start(bf16[8,128,768]{2,1,0:T(8,128)(2,1)} %fill_slots.4), calls=%async_computation | async-start | bytes 3145728 | tf_op jit(solution)/shard_map/all_to_all | solution.py:1398
  37.4 125.6 %all-gather.5.cloned.1.call-start = ((), (), s32[]{:S(2)}) async-start(), calls=%async_computation.9 | async-start | bytes 11919360 | tf_op jit(solution)/shard_map/all_gather | solution.py:1437
  37.5 8.1 %collective-permute-start.5 = (bf16[2,2,24,1664]{3,2,0,1:T(8,128)(2,1)S(1)}, bf16[2,2,24,1664]{3,2,0,1:T(8,128)(2,1)S(1)}, u32[]{:S(2)}, u32[]{:S(2)}) collective-permute-start(bf16[2,2,24,1664]{3,2,0,1:T(8,128)(2,1)S(1)} %pad_maximum_fusion.6), channel_id=1, source_target_pairs={{0,16},{8,24},{16,0},{24,8},{1,17},{9,25},{17,1},{25,9},{2,18},{10... | collective-permute-start | bytes 958472 | tf_op jit(solution)/shard_map/ppermute | solution.py:1319
  52.7 13.1 %collective-permute-start.6 = (bf16[2,2,2,24,1536]{4,3,0,1,2:T(8,128)(2,1)S(1)}, bf16[2,2,2,24,1536]{4,3,0,1,2:T(8,128)(2,1)S(1)}, u32[]{:S(2)}, u32[]{:S(2)}) collective-permute-start(bf16[2,2,2,24,1536]{4,3,0,1,2:T(8,128)(2,1)S(1)} %pad_maximum_fusion.5), channel_id=1, source_target_pairs={{0,16},{8,24},{16,0},{24,8},{1,17},{9,25},{17,1},{25,9},{2,18},{10... | collective-permute-start | bytes 1769480 | tf_op jit(solution)/shard_map/ppermute | solution.py:1319
  54.2 19.2 %collective-permute-start.7 = (bf16[2,2,2,24,1664]{4,3,1,2,0:T(8,128)(2,1)S(1)}, bf16[2,2,2,24,1664]{4,3,1,2,0:T(8,128)(2,1)S(1)}, u32[]{:S(2)}, u32[]{:S(2)}) collective-permute-start(bf16[2,2,2,24,1664]{4,3,1,2,0:T(8,128)(2,1)S(1)} %pad_maximum_fusion.4), channel_id=1, source_target_pairs={{0,1},{1,0},{2,3},{3,2},{4,5},{5,4},{6,7},{7,6},{8,9},{9,8},{10,11... | collective-permute-start | bytes 1916936 | tf_op jit(solution)/shard_map/ppermute | solution.py:1319
  73.8 135.5 %all-gather.7.cloned.1.call-start = ((), (), s32[]{:S(2)}) async-start(), calls=%async_computation.10 | async-start | bytes 11919360 | tf_op jit(solution)/shard_map/all_gather | solution.py:1437
  74.5 8.7 %collective-permute-start.9 = (bf16[2,192,1664]{2,1,0:T(8,128)(2,1)S(1)}, bf16[2,192,1664]{2,1,0:T(8,128)(2,1)}, u32[]{:S(2)}, u32[]{:S(2)}) collective-permute-start(bf16[2,192,1664]{2,1,0:T(8,128)(2,1)S(1)} %bitcast.88), channel_id=1, source_target_pairs={{0,8},{8,0},{16,24},{24,16},{1,9},{9,1},{17,25},{25,17},{2,10},{10... | collective-permute-start | bytes 3833864 | tf_op jit(solution)/shard_map/ppermute | solution.py:1319
  74.6 43.2 %all-to-all-start.1 = ((bf16[8,128,768]{2,1,0:T(8,128)(2,1)}), bf16[8,128,768]{2,1,0:T(8,128)(2,1)}, u32[]{:S(2)}, u32[]{:S(2)}) async-start(bf16[8,128,768]{2,1,0:T(8,128)(2,1)} %fill_slots.5), calls=%async_computation.1 | async-start | bytes 3145728 | tf_op jit(solution)/shard_map/all_to_all | solution.py:1398
  117.9 41.2 %all-to-all-start.2 = ((bf16[8,128,768]{2,1,0:T(8,128)(2,1)}), bf16[8,128,768]{2,1,0:T(8,128)(2,1)}, u32[]{:S(2)}, u32[]{:S(2)}) async-start(bf16[8,128,768]{2,1,0:T(8,128)(2,1)} %fill_slots.6), calls=%async_computation.2 | async-start | bytes 3145728 | tf_op jit(solution)/shard_map/all_to_all | solution.py:1398
  159.0 43.0 %all-to-all-start.3 = ((bf16[8,128,768]{2,1,0:T(8,128)(2,1)}), bf16[8,128,768]{2,1,0:T(8,128)(2,1)S(1)}, u32[]{:S(2)}, u32[]{:S(2)}) async-start(bf16[8,128,768]{2,1,0:T(8,128)(2,1)} %fill_slots.7), calls=%async_computation.3 | async-start | bytes 3145728 | tf_op jit(solution)/shard_map/all_to_all | solution.py:1398
  162.6 186.2 %reduce-scatter.2.cloned.1.call-start = ((), (), s32[]{:S(2)}) async-start(), calls=%async_computation.8 | async-start | bytes 11919360 | tf_op jit(solution)/shard_map/reduce_scatter | solution.py:1459
  203.1 45.1 %all-to-all-start.4 = ((bf16[8,128,768]{2,1,0:T(8,128)(2,1)}), bf16[8,128,768]{2,1,0:T(8,128)(2,1)S(1)}, u32[]{:S(2)}, u32[]{:S(2)}) async-start(bf16[8,128,768]{2,1,0:T(8,128)(2,1)} %get-tuple-element.178), calls=%async_computation.4 | async-start | bytes 3145728 | tf_op jit(solution)/shard_map/all_to_all | solution.py:1398
  248.2 15.6 %collective-permute-start.10 = (bf16[2,1552,768]{2,1,0:T(8,128)(2,1)}, bf16[2,1552,768]{2,1,0:T(8,128)(2,1)}, u32[]{:S(2)}, u32[]{:S(2)}) collective-permute-start(bf16[2,1552,768]{2,1,0:T(8,128)(2,1)} %get-tuple-element.188), channel_id=1, source_target_pairs={{0,8},{8,0},{16,24},{24,16},{1,9},{9,1},{17,25},{25,17},{2,10},{10... | collective-permute-start | bytes 14303240 | tf_op jit(solution)/shard_map/ppermute | solution.py:1319
  248.3 43.8 %all-to-all-start.5 = ((bf16[8,128,768]{2,1,0:T(8,128)(2,1)}), bf16[8,128,768]{2,1,0:T(8,128)(2,1)}, u32[]{:S(2)}, u32[]{:S(2)}) async-start(bf16[8,128,768]{2,1,0:T(8,128)(2,1)} %get-tuple-element.189), calls=%async_computation.5 | async-start | bytes 3145728 | tf_op jit(solution)/shard_map/all_to_all | solution.py:1398
  292.1 60.9 %collective-permute-start.15 = (bf16[1552,768]{1,0:T(8,128)(2,1)}, bf16[1552,768]{1,0:T(8,128)(2,1)}, u32[]{:S(2)}, u32[]{:S(2)}) collective-permute-start(bf16[1552,768]{1,0:T(8,128)(2,1)} %get-tuple-element.201), channel_id=1, source_target_pairs={{0,16},{8,24},{16,0},{24,8},{1,17},{9,25},{17,1},{25,9},{2,18},{10... | collective-permute-start | bytes 7151624 | tf_op jit(solution)/shard_map/ppermute | solution.py:1319
  293.0 79.7 %all-to-all-start.6 = ((bf16[8,256,768]{2,1,0:T(8,128)(2,1)}), bf16[8,256,768]{2,1,0:T(8,128)(2,1)}, u32[]{:S(2)}, u32[]{:S(2)}) async-start(bf16[8,256,768]{2,1,0:T(8,128)(2,1)} %get-tuple-element.214), calls=%async_computation.7 | async-start | bytes 6291456 | tf_op jit(solution)/shard_map/all_to_all | solution.py:1398
  343.4 21.8 %collective-permute-start.13 = (bf16[192,1792]{1,0:T(8,128)(2,1)}, bf16[192,1792]{1,0:T(8,128)(2,1)}, u32[]{:S(2)}, u32[]{:S(2)}) collective-permute-start(bf16[192,1792]{1,0:T(8,128)(2,1)} %get-tuple-element.197), channel_id=1, source_target_pairs={{0,16},{8,24},{16,0},{24,8},{1,17},{9,25},{17,1},{25,9},{2,18},{10... | collective-permute-start | bytes 2064392 | tf_op jit(solution)/shard_map/ppermute | solution.py:1319
  344.5 20.8 %collective-permute-start.14 = (bf16[192,1408]{1,0:T(8,128)(2,1)}, bf16[192,1408]{1,0:T(8,128)(2,1)}, u32[]{:S(2)}, u32[]{:S(2)}) collective-permute-start(bf16[192,1408]{1,0:T(8,128)(2,1)} %get-tuple-element.198), channel_id=1, source_target_pairs={{0,1},{1,0},{2,3},{3,2},{4,5},{5,4},{6,7},{7,6},{8,9},{9,8},{10,11... | collective-permute-start | bytes 1622024 | tf_op jit(solution)/shard_map/ppermute | solution.py:1319
  369.2 13.7 %collective-permute-start.16 = (bf16[96,1792]{1,0:T(8,128)(2,1)}, bf16[96,1792]{1,0:T(8,128)(2,1)S(1)}, u32[]{:S(2)}, u32[]{:S(2)}) collective-permute-start(bf16[96,1792]{1,0:T(8,128)(2,1)} %get-tuple-element.212), channel_id=1, source_target_pairs={{0,1},{1,0},{2,3},{3,2},{4,5},{5,4},{6,7},{7,6},{8,9},{9,8},{10,11... | collective-permute-start | bytes 1032200 | tf_op jit(solution)/shard_map/ppermute | solution.py:1319
  371.7 11.2 %collective-permute-start.17 = (bf16[96,1408]{1,0:T(8,128)(2,1)}, bf16[96,1408]{1,0:T(8,128)(2,1)}, u32[]{:S(2)}, u32[]{:S(2)}) collective-permute-start(bf16[96,1408]{1,0:T(8,128)(2,1)} %get-tuple-element.213), channel_id=1, source_target_pairs={{0,16},{8,24},{16,0},{24,8},{1,17},{9,25},{17,1},{25,9},{2,18},{10... | collective-permute-start | bytes 811016 | tf_op jit(solution)/shard_map/ppermute | solution.py:1319
  384.1 7.7 %collective-permute-start.18 = (bf16[48,1792]{1,0:T(8,128)(2,1)S(1)}, bf16[48,1792]{1,0:T(8,128)(2,1)S(1)}, u32[]{:S(2)}, u32[]{:S(2)}) collective-permute-start(bf16[48,1792]{1,0:T(8,128)(2,1)S(1)} %get-tuple-element.222), channel_id=1, source_target_pairs={{0,2},{1,3},{2,0},{3,1},{4,6},{5,7},{6,4},{7,5},{8,10},{9,11},{10,... | collective-permute-start | bytes 516104 | tf_op jit(solution)/shard_map/ppermute | solution.py:1319
  391.9 8.9 %collective-permute-start.20 = (bf16[24,1792]{1,0:T(8,128)(2,1)S(1)}, bf16[24,1792]{1,0:T(8,128)(2,1)S(1)}, u32[]{:S(2)}, u32[]{:S(2)}) collective-permute-start(bf16[24,1792]{1,0:T(8,128)(2,1)S(1)} %get-tuple-element.226), channel_id=1, source_target_pairs={{0,4},{1,5},{2,6},{3,7},{4,0},{5,1},{6,2},{7,3},{8,12},{9,13},{10,... | collective-permute-start | bytes 258056 | tf_op jit(solution)/shard_map/ppermute | solution.py:1319
  (46 other events, 730.7 us)
Sparse Core Ops, SparseCore 0:
  73.9 64.9 all-gather.4
  141.0 64.7 all-gather.6
  208.5 79.0 reduce-scatter.1
